TPU v7x, 512 devices: a whole 4x4x16 slice. The times are simulated.
512 devices in a mesh: img: 32 (over z, core), bal: 16 (over y, x).
Axes of the slice: x: 4, y: 4, z: 16, core: 2. Of those that a mesh axis runs over, the one named last changes fastest.
Arguments:
- latent: bfloat16 [384, 192, 512], P('img', 'bal'), may hold values from -6 to 6
- gn_mean: float32 [32], replicated, may hold values from -1.5 to 1.5
- gn_rstd: float32 [32], replicated, may hold values from 0.5 to 2
- gn_gain: float32 [512], replicated, may hold values from 0.5 to 1.5
- gn_shift: float32 [512], replicated, may hold values from -3 to 3
- conv1_kernel: bfloat16 [3, 3, 512, 512], replicated, may hold values from -0.09375 to 0.09375
- conv1_bias: float32 [512], replicated, may hold values from -3 to 3
- conv2_kernel: bfloat16 [3, 3, 512, 512], replicated, may hold values from -0.09375 to 0.09375
- conv2_bias: float32 [512], replicated, may hold values from -3 to 3
- tile_dest: int32 [128, 64], P('img', 'bal'), may hold values from -1 to 127, as said below
Outputs:
- decoded: bfloat16 [768, 384, 512], P('img', 'bal')
Inputs may be any that keep to these rules, and one draw needn't show every extreme that they name: `tile_dest`: tile (i, j) belongs to the device at img index i // 4 and bal index j // 4. A value d * 8 + s names the bal index d, within the same img index, that computes the tile, and its slot s there. Among the tiles of one img index every pair (d, s) is named by exactly one tile, so every device computes exactly 8 tiles. No device names one bal index d for more than 1 of its tiles; in every band one device has all its tiles active and names every bal index for exactly 1 of them.
All inputs are finite; a program needn't handle non-finite values.
Results may differ from a plain program's by a relative error of at most 0.0055.
Values may be sent and summed in bfloat16 or wider, within the bound.
No kernel may reach another device: no remote copies, remote signals or barrier semaphores. Data moves between devices by JAX's collectives and lax.ppermute only.
A program may use at most 64 MiB of HBM per device.

v0:
```python
import jax
import jax.numpy as jnp
from jax import lax
from jax.sharding import PartitionSpec as P

TS = 3
TR = 4
TC = 4
SLOTS = 8


def extended(cells, sides, width):
    for axis, dim in sides:
        count = lax.axis_size(axis)
        ends = count - 1
        head = lax.slice_in_dim(cells, 0, width, axis=dim)
        tail = lax.slice_in_dim(cells, cells.shape[dim] - width, cells.shape[dim], axis=dim)
        cells = jnp.concatenate(
            [
                lax.ppermute(tail, axis, [(i, (i + 1) % count) for i in range(ends)]),
                cells,
                lax.ppermute(head, axis, [((i + 1) % count, i) for i in range(ends)]),
            ],
            axis=dim,
        )
    return cells


def norm_act(latent, gn_mean, gn_rstd, gn_gain, gn_shift):
    per_group = latent.shape[-1] // gn_mean.shape[0]
    mean_full = jnp.repeat(gn_mean, per_group)
    rstd_full = jnp.repeat(gn_rstd, per_group)
    normed = (latent.astype(jnp.float32) - mean_full) * rstd_full * gn_gain + gn_shift
    return jax.nn.silu(normed).astype(jnp.bfloat16)


def conv_three(region, kernel, bias_vec):
    batch_count = region.shape[0]
    tile_side = region.shape[1] - 2
    running = jnp.zeros((batch_count * tile_side * tile_side, kernel.shape[3]), jnp.float32)
    for step_y in range(3):
        for step_x in range(3):
            window = region[:, step_y : step_y + tile_side, step_x : step_x + tile_side, :]
            window = window.reshape(batch_count * tile_side * tile_side, region.shape[3])
            running = running + jnp.dot(
                window, kernel[step_y, step_x], preferred_element_type=jnp.float32
            )
    return (running + bias_vec).reshape(batch_count, tile_side, tile_side, kernel.shape[3])


def inside_cells(row_start, col_start, full_height, full_width, tile_side):
    row_ids = row_start[:, None] - 1 + jnp.arange(tile_side + 2, dtype=jnp.int32)[None, :]
    col_ids = col_start[:, None] - 1 + jnp.arange(tile_side + 2, dtype=jnp.int32)[None, :]
    row_ok = (row_ids >= 0) & (row_ids < full_height)
    col_ok = (col_ids >= 0) & (col_ids < full_width)
    return row_ok[:, :, None] & col_ok[:, None, :]


def first_conv(region, inside, kernel, bias_vec):
    hidden = conv_three(region, kernel, bias_vec)
    return jnp.where(inside[..., None], hidden, jnp.zeros((), hidden.dtype)).astype(jnp.bfloat16)


def second_conv(hidden, kernel, bias_vec):
    upsampled = jnp.repeat(jnp.repeat(hidden, 2, axis=1), 2, axis=2)
    cropped = upsampled[:, 1:-1, 1:-1, :]
    return conv_three(cropped, kernel, bias_vec).astype(jnp.bfloat16)


def shards(
    latent,
    gn_mean,
    gn_rstd,
    gn_gain,
    gn_shift,
    conv1_kernel,
    conv1_bias,
    conv2_kernel,
    conv2_bias,
    tile_dest,
):
    band_h = latent.shape[0]
    band_w = latent.shape[1]
    bal_size = lax.axis_size("bal")
    img_id = lax.axis_index("img")
    full_height = band_h * lax.axis_size("img")
    full_width = band_w * bal_size
    tile_count = TR * TC
    peer_slots = tile_count // bal_size
    activated = norm_act(latent, gn_mean, gn_rstd, gn_gain, gn_shift)
    padded = extended(activated, (("img", 0), ("bal", 1)), 2)
    regions = jnp.stack(
        [
            padded[row_n * TS : row_n * TS + TS + 4, col_n * TS : col_n * TS + TS + 4, :]
            for row_n in range(TR)
            for col_n in range(TC)
        ]
    )
    tile_codes = tile_dest.reshape(tile_count)
    local_ids = jnp.arange(tile_count, dtype=jnp.int32)
    row_base = img_id * band_h
    active = tile_codes >= 0
    safe_codes = jnp.maximum(tile_codes, 0)
    dest = safe_codes // SLOTS
    slot_of = safe_codes % SLOTS
    earlier = (
        (dest[:, None] == dest[None, :])
        & active[None, :]
        & (local_ids[None, :] < local_ids[:, None])
    )
    rank_in = jnp.sum(earlier.astype(jnp.int32), axis=1)
    send_pos = dest * peer_slots + rank_in
    send_match = active[:, None] & (send_pos[:, None] == local_ids[None, :])
    send_onehot = send_match.astype(jnp.bfloat16)
    send_regions = jnp.einsum(
        "tr,tyxc->ryxc", send_onehot, regions, preferred_element_type=jnp.float32
    ).astype(jnp.bfloat16)
    send_regions = send_regions.reshape((bal_size, peer_slots) + regions.shape[1:])
    tag_value = slot_of * tile_count + local_ids + 1
    send_tags = jnp.sum(jnp.where(send_match, tag_value[:, None], 0), axis=0)
    send_tags = send_tags.reshape(bal_size, peer_slots)
    got_regions, got_tags = (
        lax.all_to_all(send_regions, "bal", split_axis=0, concat_axis=0, tiled=True),
        lax.all_to_all(send_tags, "bal", split_axis=0, concat_axis=0, tiled=True),
    )
    got_regions = got_regions.reshape((tile_count,) + regions.shape[1:])
    got_tags = got_tags.reshape(tile_count)
    live = got_tags > 0
    work_slot = jnp.maximum(got_tags - 1, 0) // tile_count
    work_local = jnp.maximum(got_tags - 1, 0) % tile_count
    recv_match = live[:, None] & (work_slot[:, None] == jnp.arange(SLOTS, dtype=jnp.int32)[None, :])
    recv_onehot = recv_match.astype(jnp.bfloat16)
    work_tiles = jnp.einsum(
        "rs,ryxc->syxc", recv_onehot, got_regions, preferred_element_type=jnp.float32
    ).astype(jnp.bfloat16)
    source = jnp.sum(jnp.where(recv_match, (local_ids // peer_slots)[:, None], 0), axis=0)
    local_tile = jnp.sum(jnp.where(recv_match, work_local[:, None], 0), axis=0).astype(jnp.int32)
    inside = inside_cells(
        row_base + local_tile // TC * TS,
        source * band_w + local_tile % TC * TS,
        full_height,
        full_width,
        TS,
    )
    hidden = first_conv(work_tiles, inside, conv1_kernel, conv1_bias)
    finished = second_conv(hidden, conv2_kernel, conv2_bias)
    return_tiles = jnp.einsum(
        "rs,syxc->ryxc", recv_onehot, finished, preferred_element_type=jnp.float32
    ).astype(jnp.bfloat16)
    return_tiles = return_tiles.reshape((bal_size, peer_slots) + finished.shape[1:])
    arrived = lax.all_to_all(return_tiles, "bal", split_axis=0, concat_axis=0, tiled=True)
    arrived = arrived.reshape((tile_count,) + finished.shape[1:])
    result = jnp.einsum(
        "tr,ryxc->tyxc", send_onehot, arrived, preferred_element_type=jnp.float32
    ).astype(jnp.bfloat16)
    result = result.reshape(TR, TC, 2 * TS, 2 * TS, result.shape[-1]).transpose(0, 2, 1, 3, 4)
    return result.reshape(2 * band_h, 2 * band_w, result.shape[-1])


def solution(mesh):
    placed = (P("img", "bal", None), P(), P(), P(), P(), P(), P(), P(), P(), P("img", "bal"))
    return jax.shard_map(
        shards, mesh=mesh, in_specs=placed, out_specs=P("img", "bal", None), check_vma=False
    )
```

profile of v0, /device:TPU:1, one launch (start us, length us, event | category | flops | bytes accessed | tf_op | source)
XLA Modules:
  0.0 111.5 jit_solution(10027084771771273209)
XLA Ops:
  2.7 7.6 %all-to-all-start = ((s32[16,1,1]{2,1,0:T(1,128)}), s32[16,1,1]{2,1,0:T(1,128)S(1)}, u32[]{:S(2)}, u32[]{:S(2)}) async-start(s32[16,1,1]{2,1,0:T(1,128)} %copy.751), calls=%async_computation | async-start | bytes 16384 | tf_op jit(solution)/shard_map/all_to_all | solution.py:124
  11.1 0.7 broadcast_in_dim.86
  11.9 1.1 multiply_convert_fusion
  13.0 4.4 %collective-permute-start = (bf16[2,12,512]{2,1,0:T(8,128)(2,1)S(1)}, bf16[2,12,512]{2,1,0:T(8,128)(2,1)S(1)}, u32[]{:S(2)}, u32[]{:S(2)}) collective-permute-start(bf16[2,12,512]{2,1,0:T(8,128)(2,1)S(1)} %get-tuple-element.47), channel_id=1, source_target_pairs={{0,16},{16,32},{32,48},{48,64},{64,80},{80,96},{96,112},{112,128},... | collective-permute-start | bytes 73736 | tf_op jit(solution)/shard_map/ppermute | solution.py:20
  17.4 1.9 %collective-permute-start.1 = (bf16[2,12,512]{2,1,0:T(8,128)(2,1)S(1)}, bf16[2,12,512]{2,1,0:T(8,128)(2,1)S(1)}, u32[]{:S(2)}, u32[]{:S(2)}) collective-permute-start(bf16[2,12,512]{2,1,0:T(8,128)(2,1)S(1)} %get-tuple-element.48), channel_id=1, source_target_pairs={{16,0},{32,16},{48,32},{64,48},{80,64},{96,80},{112,96},{128,112},... | collective-permute-start | bytes 73736 | tf_op jit(solution)/shard_map/ppermute | solution.py:22
  20.7 1.9 %collective-permute-done.1 = bf16[2,12,512]{2,1,0:T(8,128)(2,1)S(1)} collective-permute-done((bf16[2,12,512]{2,1,0:T(8,128)(2,1)S(1)}, bf16[2,12,512]{2,1,0:T(8,128)(2,1)S(1)}, u32[]{:S(2)}, u32[]{:S(2)}) %collective-permute-start.1) | collective-permute-done | bytes 24608 | tf_op jit(solution)/shard_map/ppermute | solution.py:22
  22.7 1.3 %collective-permute-start.3 = (bf16[16,2,512]{2,1,0:T(2,128)(2,1)S(1)}, bf16[16,2,512]{2,1,0:T(2,128)(2,1)S(1)}, u32[]{:S(2)}, u32[]{:S(2)}) collective-permute-start(bf16[16,2,512]{2,1,0:T(2,128)(2,1)S(1)} %get-tuple-element.37), channel_id=1, source_target_pairs={{1,0},{2,1},{3,2},{4,3},{5,4},{6,5},{7,6},{8,7},{9,8},{10,9},{11,1... | collective-permute-start | bytes 98312 | tf_op jit(solution)/shard_map/ppermute | solution.py:22
  24.0 4.2 %collective-permute-start.2 = (bf16[16,2,512]{2,1,0:T(2,128)(2,1)S(1)}, bf16[16,2,512]{2,1,0:T(2,128)(2,1)S(1)}, u32[]{:S(2)}, u32[]{:S(2)}) collective-permute-start(bf16[16,2,512]{2,1,0:T(2,128)(2,1)S(1)} %get-tuple-element.38), channel_id=1, source_target_pairs={{0,1},{1,2},{2,3},{3,4},{4,5},{5,6},{6,7},{7,8},{8,9},{9,10},{10,1... | collective-permute-start | bytes 98312 | tf_op jit(solution)/shard_map/ppermute | solution.py:20
  30.4 3.6 %stack.67 = bf16[16,7,7,512]{3,0,2,1:T(8,128)(2,1)S(1)} concatenate(bf16[1,7,7,512]{3,0,2,1:T(2,128)(2,1)S(1)} %copy.752, bf16[1,7,7,512]{3,0,2,1:T(2,128)(2,1)S(1)} %copy.753, bf16[1,7,7,512]{3,0,2,1:T(2,128)(2,1)S(1)} %copy.754, bf16[1,7,7,512]{3,0,2,1:T(2,128)(2,1)S(1)} %copy.755, bf16[1,7,7,512]{3,0,2,1:T(2,128)(2,1)S(1)} %copy.756, bf16[1,7,7,512]{3,0,2,1:T(2,128)(2,1)S(1)} %copy.757, ...), dimensions={0} | concatenate | bytes 1605632 | tf_op jit(solution)/shard_map/stack | solution.py:92
  34.6 1.4 %copy.769 = bf16[16,1,7,7,512]{4,3,2,1,0:T(8,128)(2,1)} copy(bf16[16,1,7,7,512]{4,0,3,2,1:T(8,128)(2,1)S(1)} %fusion) | data formatting | bytes 1605632 | tf_op jit(solution)/shard_map/reshape | solution.py:118
  35.9 9.1 %all-to-all-start.1 = ((bf16[16,1,7,7,512]{4,3,2,1,0:T(8,128)(2,1)}), bf16[16,1,7,7,512]{4,3,2,1,0:T(8,128)(2,1)S(1)}, u32[]{:S(2)}, u32[]{:S(2)}) async-start(bf16[16,1,7,7,512]{4,3,2,1,0:T(8,128)(2,1)} %copy.769), calls=%async_computation.1 | async-start | bytes 1835008 | tf_op jit(solution)/shard_map/all_to_all | solution.py:123
  45.3 18.1 %all-to-all-done.1 = bf16[16,1,7,7,512]{4,3,2,1,0:T(8,128)(2,1)S(1)} async-done(((bf16[16,1,7,7,512]{4,3,2,1,0:T(8,128)(2,1)}), bf16[16,1,7,7,512]{4,3,2,1,0:T(8,128)(2,1)S(1)}, u32[]{:S(2)}, u32[]{:S(2)}) %all-to-all-start.1) | async-done | bytes 802848 | tf_op jit(solution)/shard_map/all_to_all | solution.py:123
  65.6 1.3 %fusion.27 = f32[200,512]{1,0:T(8,128)S(1)} fusion(bf16[200,512]{1,0:T(8,128)(2,1)S(1)} %reshape.289, bf16[3,3,512,512]{3,2,1,0:T(8,128)(2,1)} %param.15), kind=kOutput, calls=%fused_computation.48 | convolution fusion | flops 104857600 | bytes 1138688 | tf_op jit(solution)/shard_map/dot_general | solution.py:45
  66.9 1.3 %convolution_add_fusion.15 = f32[200,512]{1,0:T(8,128)S(1)} fusion(f32[200,512]{1,0:T(8,128)S(1)} %fusion.27, bf16[200,512]{1,0:T(8,128)(2,1)S(1)} %reshape.290, bf16[3,3,512,512]{3,2,1,0:T(8,128)(2,1)} %param.15), kind=kOutput, calls=%fused_computation.23 | convolution fusion | flops 104960000 | bytes 1548288 | tf_op jit(solution)/shard_map/dot_general | solution.py:45
  68.2 1.3 %convolution_add_fusion.14 = f32[200,512]{1,0:T(8,128)S(1)} fusion(f32[200,512]{1,0:T(8,128)S(1)} %convolution_add_fusion.15, bf16[200,512]{1,0:T(8,128)(2,1)S(1)} %reshape.291, bf16[3,3,512,512]{3,2,1,0:T(8,128)(2,1)} %param.15), kind=kOutput, calls=%fused_computation.22 | convolution fusion | flops 104960000 | bytes 1548288 | tf_op jit(solution)/shard_map/dot_general | solution.py:45
  69.5 1.3 %convolution_add_fusion.13 = f32[200,512]{1,0:T(8,128)S(1)} fusion(f32[200,512]{1,0:T(8,128)S(1)} %convolution_add_fusion.14, bf16[200,512]{1,0:T(8,128)(2,1)S(1)} %reshape.292, bf16[3,3,512,512]{3,2,1,0:T(8,128)(2,1)} %param.15), kind=kOutput, calls=%fused_computation.21 | convolution fusion | flops 104960000 | bytes 1548288 | tf_op jit(solution)/shard_map/dot_general | solution.py:45
  70.9 1.3 %convolution_add_fusion.12 = f32[200,512]{1,0:T(8,128)S(1)} fusion(f32[200,512]{1,0:T(8,128)S(1)} %convolution_add_fusion.13, bf16[200,512]{1,0:T(8,128)(2,1)S(1)} %reshape.293, bf16[3,3,512,512]{3,2,1,0:T(8,128)(2,1)} %param.15), kind=kOutput, calls=%fused_computation.20 | convolution fusion | flops 104960000 | bytes 1548288 | tf_op jit(solution)/shard_map/dot_general | solution.py:45
  72.2 1.3 %convolution_add_fusion.11 = f32[200,512]{1,0:T(8,128)S(1)} fusion(f32[200,512]{1,0:T(8,128)S(1)} %convolution_add_fusion.12, bf16[200,512]{1,0:T(8,128)(2,1)S(1)} %reshape.294, bf16[3,3,512,512]{3,2,1,0:T(8,128)(2,1)} %param.15), kind=kOutput, calls=%fused_computation.19 | convolution fusion | flops 104960000 | bytes 1548288 | tf_op jit(solution)/shard_map/dot_general | solution.py:45
  73.5 1.3 %convolution_add_fusion.10 = f32[200,512]{1,0:T(8,128)S(1)} fusion(f32[200,512]{1,0:T(8,128)S(1)} %convolution_add_fusion.11, bf16[200,512]{1,0:T(8,128)(2,1)S(1)} %reshape.295, bf16[3,3,512,512]{3,2,1,0:T(8,128)(2,1)} %param.15), kind=kOutput, calls=%fused_computation.18 | convolution fusion | flops 104960000 | bytes 1548288 | tf_op jit(solution)/shard_map/dot_general | solution.py:45
  74.8 1.3 %convolution_add_fusion.9 = f32[200,512]{1,0:T(8,128)S(1)} fusion(f32[200,512]{1,0:T(8,128)S(1)} %convolution_add_fusion.10, bf16[200,512]{1,0:T(8,128)(2,1)S(1)} %reshape.296, bf16[3,3,512,512]{3,2,1,0:T(8,128)(2,1)} %param.15), kind=kOutput, calls=%fused_computation.17 | convolution fusion | flops 104960000 | bytes 1548288 | tf_op jit(solution)/shard_map/dot_general | solution.py:45
  76.1 1.3 %fusion.4 = bf16[200,512]{1,0:T(8,128)(2,1)S(1)} fusion(f32[200,512]{1,0:T(8,128)S(1)} %convolution_add_fusion.9, bf16[200,512]{1,0:T(8,128)(2,1)S(1)} %reshape.297, bf16[3,3,512,512]{3,2,1,0:T(8,128)(2,1)} %param.15, f32[512]{0:T(512)S(1)} %copy-done), kind=kOutput, calls=%fused_computation.24 | convolution fusion | flops 105164800 | bytes 1345536 | tf_op jit(solution)/shard_map/dot_general | solution.py:45
  79.9 1.4 %fusion.17 = f32[288,512]{1,0:T(8,128)S(1)} fusion(bf16[288,512]{1,0:T(8,128)(2,1)S(1)} %reshape.301, bf16[3,3,512,512]{3,2,1,0:T(8,128)(2,1)} %param.17), kind=kOutput, calls=%fused_computation.38 | convolution fusion | flops 150994944 | bytes 1409024 | tf_op jit(solution)/shard_map/dot_general | solution.py:45
  81.3 1.4 %convolution_add_fusion.7 = f32[288,512]{1,0:T(8,128)S(1)} fusion(f32[288,512]{1,0:T(8,128)S(1)} %fusion.17, bf16[288,512]{1,0:T(8,128)(2,1)S(1)} %reshape.302, bf16[3,3,512,512]{3,2,1,0:T(8,128)(2,1)} %param.17), kind=kOutput, calls=%fused_computation.14 | convolution fusion | flops 151142400 | bytes 1998848 | tf_op jit(solution)/shard_map/dot_general | solution.py:45
  82.6 1.4 %convolution_add_fusion.6 = f32[288,512]{1,0:T(8,128)S(1)} fusion(f32[288,512]{1,0:T(8,128)S(1)} %convolution_add_fusion.7, bf16[288,512]{1,0:T(8,128)(2,1)S(1)} %reshape.303, bf16[3,3,512,512]{3,2,1,0:T(8,128)(2,1)} %param.17), kind=kOutput, calls=%fused_computation.13 | convolution fusion | flops 151142400 | bytes 1998848 | tf_op jit(solution)/shard_map/dot_general | solution.py:45
  84.0 1.4 %convolution_add_fusion.5 = f32[288,512]{1,0:T(8,128)S(1)} fusion(f32[288,512]{1,0:T(8,128)S(1)} %convolution_add_fusion.6, bf16[288,512]{1,0:T(8,128)(2,1)S(1)} %reshape.304, bf16[3,3,512,512]{3,2,1,0:T(8,128)(2,1)} %param.17), kind=kOutput, calls=%fused_computation.12 | convolution fusion | flops 151142400 | bytes 1998848 | tf_op jit(solution)/shard_map/dot_general | solution.py:45
  85.4 1.4 %convolution_add_fusion.4 = f32[288,512]{1,0:T(8,128)S(1)} fusion(f32[288,512]{1,0:T(8,128)S(1)} %convolution_add_fusion.5, bf16[288,512]{1,0:T(8,128)(2,1)S(1)} %reshape.305, bf16[3,3,512,512]{3,2,1,0:T(8,128)(2,1)} %param.17), kind=kOutput, calls=%fused_computation.11 | convolution fusion | flops 151142400 | bytes 1998848 | tf_op jit(solution)/shard_map/dot_general | solution.py:45
  86.7 1.4 %convolution_add_fusion.3 = f32[288,512]{1,0:T(8,128)S(1)} fusion(f32[288,512]{1,0:T(8,128)S(1)} %convolution_add_fusion.4, bf16[288,512]{1,0:T(8,128)(2,1)S(1)} %reshape.306, bf16[3,3,512,512]{3,2,1,0:T(8,128)(2,1)} %param.17), kind=kOutput, calls=%fused_computation.10 | convolution fusion | flops 151142400 | bytes 1998848 | tf_op jit(solution)/shard_map/dot_general | solution.py:45
  88.1 1.4 %convolution_add_fusion.2 = f32[288,512]{1,0:T(8,128)S(1)} fusion(f32[288,512]{1,0:T(8,128)S(1)} %convolution_add_fusion.3, bf16[288,512]{1,0:T(8,128)(2,1)S(1)} %reshape.307, bf16[3,3,512,512]{3,2,1,0:T(8,128)(2,1)} %param.17), kind=kOutput, calls=%fused_computation.9 | convolution fusion | flops 151142400 | bytes 1998848 | tf_op jit(solution)/shard_map/dot_general | solution.py:45
  89.5 1.4 %convolution_add_fusion.1 = f32[288,512]{1,0:T(8,128)S(1)} fusion(f32[288,512]{1,0:T(8,128)S(1)} %convolution_add_fusion.2, bf16[288,512]{1,0:T(8,128)(2,1)S(1)} %reshape.308, bf16[3,3,512,512]{3,2,1,0:T(8,128)(2,1)} %param.17), kind=kOutput, calls=%fused_computation.8 | convolution fusion | flops 151142400 | bytes 1998848 | tf_op jit(solution)/shard_map/dot_general | solution.py:45
  90.8 1.4 %fusion.3 = bf16[288,512]{1,0:T(8,128)(2,1)S(1)} fusion(f32[288,512]{1,0:T(8,128)S(1)} %convolution_add_fusion.1, bf16[288,512]{1,0:T(8,128)(2,1)S(1)} %reshape.309, bf16[3,3,512,512]{3,2,1,0:T(8,128)(2,1)} %param.17, f32[512]{0:T(512)S(1)} %copy-done.1), kind=kOutput, calls=%fused_computation.15 | convolution fusion | flops 151437312 | bytes 1705984 | tf_op jit(solution)/shard_map/dot_general | solution.py:45
  93.0 16.5 %all_to_all.19 = bf16[16,1,6,6,512]{4,3,2,1,0:T(8,128)(2,1)S(1)} all-to-all(bf16[16,1,6,6,512]{4,3,2,1,0:T(8,128)(2,1)S(1)} %copy.791), channel_id=1, replica_groups=mesh['img'=32,'bal'=16] {'bal'}, dimensions={0} | all-to-all | bytes 1179648 | tf_op jit(solution)/shard_map/all_to_all | solution.py:151
  110.5 1.0 reshape.313
  (100 shorter events, 13.8 us)
Async XLA Ops:
  2.7 16.7 %all-to-all-start = ((s32[16,1,1]{2,1,0:T(1,128)}), s32[16,1,1]{2,1,0:T(1,128)S(1)}, u32[]{:S(2)}, u32[]{:S(2)}) async-start(s32[16,1,1]{2,1,0:T(1,128)} %copy.751), calls=%async_computation | async-start | bytes 16384 | tf_op jit(solution)/shard_map/all_to_all | solution.py:124
  13.0 7.7 %collective-permute-start = (bf16[2,12,512]{2,1,0:T(8,128)(2,1)S(1)}, bf16[2,12,512]{2,1,0:T(8,128)(2,1)S(1)}, u32[]{:S(2)}, u32[]{:S(2)}) collective-permute-start(bf16[2,12,512]{2,1,0:T(8,128)(2,1)S(1)} %get-tuple-element.47), channel_id=1, source_target_pairs={{0,16},{16,32},{32,48},{48,64},{64,80},{80,96},{96,112},{112,128},... | collective-permute-start | bytes 73736 | tf_op jit(solution)/shard_map/ppermute | solution.py:20
  17.4 5.2 %collective-permute-start.1 = (bf16[2,12,512]{2,1,0:T(8,128)(2,1)S(1)}, bf16[2,12,512]{2,1,0:T(8,128)(2,1)S(1)}, u32[]{:S(2)}, u32[]{:S(2)}) collective-permute-start(bf16[2,12,512]{2,1,0:T(8,128)(2,1)S(1)} %get-tuple-element.48), channel_id=1, source_target_pairs={{16,0},{32,16},{48,32},{64,48},{80,64},{96,80},{112,96},{128,112},... | collective-permute-start | bytes 73736 | tf_op jit(solution)/shard_map/ppermute | solution.py:22
  22.7 7.0 %collective-permute-start.3 = (bf16[16,2,512]{2,1,0:T(2,128)(2,1)S(1)}, bf16[16,2,512]{2,1,0:T(2,128)(2,1)S(1)}, u32[]{:S(2)}, u32[]{:S(2)}) collective-permute-start(bf16[16,2,512]{2,1,0:T(2,128)(2,1)S(1)} %get-tuple-element.37), channel_id=1, source_target_pairs={{1,0},{2,1},{3,2},{4,3},{5,4},{6,5},{7,6},{8,7},{9,8},{10,9},{11,1... | collective-permute-start | bytes 98312 | tf_op jit(solution)/shard_map/ppermute | solution.py:22
  24.0 5.2 %collective-permute-start.2 = (bf16[16,2,512]{2,1,0:T(2,128)(2,1)S(1)}, bf16[16,2,512]{2,1,0:T(2,128)(2,1)S(1)}, u32[]{:S(2)}, u32[]{:S(2)}) collective-permute-start(bf16[16,2,512]{2,1,0:T(2,128)(2,1)S(1)} %get-tuple-element.38), channel_id=1, source_target_pairs={{0,1},{1,2},{2,3},{3,4},{4,5},{5,6},{6,7},{7,8},{8,9},{9,10},{10,1... | collective-permute-start | bytes 98312 | tf_op jit(solution)/shard_map/ppermute | solution.py:20
  35.9 27.5 %all-to-all-start.1 = ((bf16[16,1,7,7,512]{4,3,2,1,0:T(8,128)(2,1)}), bf16[16,1,7,7,512]{4,3,2,1,0:T(8,128)(2,1)S(1)}, u32[]{:S(2)}, u32[]{:S(2)}) async-start(bf16[16,1,7,7,512]{4,3,2,1,0:T(8,128)(2,1)} %copy.769), calls=%async_computation.1 | async-start | bytes 1835008 | tf_op jit(solution)/shard_map/all_to_all | solution.py:123
  68.2 7.9 %copy-start = (f32[512]{0:T(512)S(1)}, f32[512]{0:T(512)}, u32[]{:S(2)}) copy-start(f32[512]{0:T(512)} %param.16) | copy-start | bytes 6148
  84.0 6.8 %copy-start.1 = (f32[512]{0:T(512)S(1)}, f32[512]{0:T(512)}, u32[]{:S(2)}) copy-start(f32[512]{0:T(512)} %param.18) | copy-start | bytes 6148
where the time goes:
time: 113 us; the launch traced here: 111 us
  starting transfers between devices  28.5 us (25%)
  matrix products  25.7 us (23%)
  waiting for transfers between devices  20.5 us (18%)
  blocking collectives  16.5 us (15%)
  local copies, waits for them, and re-layouts  14.8 us (13%)
  other arithmetic  4.72 us (4%)
    dot_general x18, matrix products, conv_three(): jnp.dot(window, kernel[step_y, step_x], preferred_element_type=jnp.float32)  24 us
    all_to_all x1, waiting for transfers between devices, shards(): lax.all_to_all(send_regions, 'bal', split_axis=0, concat_axis=0, tiled=True)  18.1 us
    all_to_all x1, blocking collectives, shards(): lax.all_to_all(return_tiles, 'bal', split_axis=0, concat_axis=0, tiled=True)  16.5 us
    all_to_all x1, starting transfers between devices, shards(): lax.all_to_all(send_regions, 'bal', split_axis=0, concat_axis=0, tiled=True)  9.13 us
    ppermute x2, starting transfers between devices, extended(): lax.ppermute(tail, axis, [(i, (i + 1) % count) for i in range(ends)])  8.56 us
    all_to_all x1, starting transfers between devices, shards(): lax.all_to_all(send_tags, 'bal', split_axis=0, concat_axis=0, tiled=True)  7.58 us
    another operation x17, local copies, waits for them, and re-layouts, shards(): jnp.stack([padded[row_n * TS:row_n * TS + TS + 4, col_n * TS:col_n * TS +...  4.96 us
    ppermute x2, starting transfers between devices, extended(): lax.ppermute(head, axis, [((i + 1) % count, i) for i in range(ends)])  3.21 us
  transfers between devices with their start and end apart: 6, of which 3 were waited for; matrix products, arithmetic and copies ran while one was open for 5% of the time, Pallas kernels for 0%

commit v1 on v0

v1 whole, which is shorter than its diff:
```python
import functools

import jax
import jax.numpy as jnp
from jax import lax
from jax.experimental import pallas as pl
from jax.experimental.pallas import tpu as pltpu
from jax.sharding import PartitionSpec as P

TS = 3
TR = 4
TC = 4
ROWS = TR * TS
COLS = TC * TS
LANES = 128
PITCH = 16
F32 = jnp.float32
BF16 = jnp.bfloat16


def swaps(count, first):
    pairs = []
    for i in range(first, count - 1, 2):
        pairs += [(i, i + 1), (i + 1, i)]
    return pairs


def exchange(cells, axis, dim):
    count = lax.axis_size(axis)
    even = lax.axis_index(axis) % 2 == 0
    length = cells.shape[dim]
    head = lax.slice_in_dim(cells, 0, 2, axis=dim)
    tail = lax.slice_in_dim(cells, length - 2, length, axis=dim)
    from_even = lax.ppermute(jnp.where(even, tail, head), axis, swaps(count, 0))
    from_odd = lax.ppermute(jnp.where(even, head, tail), axis, swaps(count, 1))
    return from_even, from_odd


def sum_taps_kernel(w_ref, o_ref):
    chan = w_ref.shape[2]
    step, lanes = 16, 256

    def body(i, carry):
        rows = pl.ds(pl.multiple_of(i * step, step), step)
        for lane in range(0, w_ref.shape[3], lanes):
            cols = slice(lane, lane + lanes)
            k = [[w_ref[y, x, rows, cols].astype(F32) for x in range(3)] for y in range(3)]
            by_row = [
                [k[0][x] for x in range(3)],
                [k[1][x] + k[2][x] for x in range(3)],
                [k[0][x] + k[1][x] for x in range(3)],
                [k[2][x] for x in range(3)],
            ]
            for p in range(2):
                for a in range(2):
                    u = by_row[2 * p + a]
                    full = [u[0], u[1] + u[2], u[0] + u[1], u[2]]
                    for q in range(2):
                        for b in range(2):
                            at = pl.ds(pl.multiple_of((a * 2 + b) * chan + i * step, step), step)
                            o_ref[p, q, at, cols] = full[2 * q + b].astype(BF16)
        return carry

    lax.fori_loop(0, chan // step, body, 0)


def sum_taps(kernel):
    chan, outs = kernel.shape[2:]
    return pl.pallas_call(
        sum_taps_kernel,
        out_shape=jax.ShapeDtypeStruct((2, 2, 4 * chan, outs), BF16),
        in_specs=[pl.BlockSpec(memory_space=pltpu.VMEM)],
        out_specs=pl.BlockSpec(memory_space=pltpu.VMEM),
        compiler_params=pltpu.CompilerParams(vmem_limit_bytes=24 * 2**20),
        cost_estimate=pl.CostEstimate(flops=10_000_000, bytes_accessed=13_000_000, transcendentals=0),
        name="sum_taps",
    )(kernel)


def block_kernel(
    full_rows,
    full_cols,
    x_ref,
    row_even,
    row_odd,
    col_even,
    col_odd,
    mean_ref,
    rstd_ref,
    gain_ref,
    shift_ref,
    w1_ref,
    b1_ref,
    w2_ref,
    b2_ref,
    dest_ref,
    o_ref,
    act,
    taps,
    hid,
    packed,
    near,
    wide,
):
    chan = x_ref.shape[2]
    img = lax.axis_index("img")
    bal = lax.axis_index("bal")
    img_even = img % 2 == 0
    bal_even = bal % 2 == 0

    groups = mean_ref.shape[1]
    group_of = lax.broadcasted_iota(jnp.int32, (groups, chan), 1) // (chan // groups)
    spread = (lax.broadcasted_iota(jnp.int32, (groups, chan), 0) == group_of).astype(F32)
    exact = functools.partial(
        jnp.dot, precision=lax.Precision.HIGHEST, preferred_element_type=F32
    )
    mean = exact(jnp.broadcast_to(mean_ref[...], (8, groups)), spread)[0:1]
    rstd = exact(jnp.broadcast_to(rstd_ref[...], (8, groups)), spread)[0:1]
    gain = gain_ref[...]
    shift = shift_ref[...]

    def activate(cells):
        v = (cells.astype(F32) - mean) * rstd * gain + shift
        return v / (1.0 + jnp.exp(-v))

    def pick(even, even_ref, odd_ref, row):
        a, b = even_ref[row], odd_ref[row]
        return jnp.where(even, a, b), jnp.where(even, b, a)

    side = ROWS + 4
    for r in range(side):
        left, right = pick(bal_even, col_odd, col_even, r)
        if r < 2:
            mid = jnp.where(img_even, row_odd[r], row_even[r])
        elif r < ROWS + 2:
            mid = x_ref[r - 2]
        else:
            mid = jnp.where(img_even, row_even[r - 2 - ROWS], row_odd[r - 2 - ROWS])
        act[r * PITCH : r * PITCH + 2] = left.astype(F32)
        act[r * PITCH + 2 : r * PITCH + 2 + COLS] = mid.astype(F32)
        act[r * PITCH + 2 + COLS : (r + 1) * PITCH] = right.astype(F32)
    cell = lax.broadcasted_iota(jnp.int32, (PITCH, 1), 0)
    col = bal * COLS - 2 + cell
    col_ok = (col >= 0) & (col < full_cols)
    for r in range(side):
        row = img * ROWS - 2 + r
        ok = col_ok & ((row >= 0) & (row < full_rows))
        at = slice(r * PITCH, (r + 1) * PITCH)
        act[at] = jnp.where(ok, activate(act[at]), 0.0)
    total = side * PITCH
    act[total:] = jnp.zeros((act.shape[0] - total, chan), F32)
    for d in range(3):
        taps[:, d * chan : (d + 1) * chan] = act[d : d + total].astype(BF16)

    inner = (ROWS + 2) * PITCH
    h = b1_ref[...]
    for d in range(3):
        h = h + jnp.dot(
            taps[d * PITCH : d * PITCH + inner], w1_ref[d], preferred_element_type=F32
        )
    cell = lax.broadcasted_iota(jnp.int32, (inner, 1), 0)
    row = img * ROWS - 1 + cell // PITCH
    col = bal * COLS - 1 + cell % PITCH
    ok = (row >= 0) & (row < full_rows) & (col >= 0) & (col < full_cols)
    hid[0:inner] = jnp.where(ok, h, 0.0)

    for d in range(3):
        for r in range(ROWS + 2):
            packed[d, r * COLS : (r + 1) * COLS] = hid[r * PITCH + d : r * PITCH + d + COLS]
    count = ROWS * COLS
    for dy in range(3):
        for dx in range(3):
            at = (dy * 3 + dx) * chan
            near[:, at : at + chan] = packed[dx, dy * COLS : dy * COLS + count].astype(BF16)
    bias = b2_ref[...]
    for p in range(2):
        for q in range(2):
            z = bias
            for a in range(2):
                at = ((p + a) * 3 + q) * chan
                z = z + jnp.dot(
                    near[:, at : at + 2 * chan],
                    w2_ref[p, q, a * 2 * chan : (a + 1) * 2 * chan],
                    preferred_element_type=F32,
                )
            for r in range(ROWS):
                for k in range(wide.shape[0]):
                    lane = slice(k * LANES, (k + 1) * LANES)
                    wide[k, 2 * r + p, pl.ds(q, COLS, stride=2)] = z[r * COLS : (r + 1) * COLS, lane]
    cell = lax.broadcasted_iota(jnp.int32, (2 * COLS, 1), 0)
    for i in range(TR):
        live = jnp.zeros((2 * COLS, 1), jnp.int32)
        for j in range(TC):
            live = jnp.where(cell // (2 * TS) == j, (dest_ref[i, j] >= 0).astype(jnp.int32), live)
        for r in range(i * 2 * TS, (i + 1) * 2 * TS):
            for k in range(wide.shape[0]):
                lane = slice(k * LANES, (k + 1) * LANES)
                o_ref[r, :, lane] = jnp.where(live > 0, wide[k, r], 0.0).astype(BF16)


def run_block(full_rows, full_cols, *args):
    chan = args[0].shape[2]
    vmem = pl.BlockSpec(memory_space=pltpu.VMEM)
    smem = pl.BlockSpec(memory_space=pltpu.SMEM)
    side = ROWS + 4
    inner = (ROWS + 2) * PITCH
    count = ROWS * COLS
    return pl.pallas_call(
        functools.partial(block_kernel, full_rows, full_cols),
        out_shape=jax.ShapeDtypeStruct((2 * ROWS, 2 * COLS, chan), BF16),
        in_specs=[vmem] * 13 + [smem],
        out_specs=vmem,
        scratch_shapes=[
            pltpu.VMEM((side * PITCH + 8, chan), F32),
            pltpu.VMEM((side * PITCH, 3 * chan), BF16),
            pltpu.VMEM((inner + 8, chan), F32),
            pltpu.VMEM((3, (ROWS + 2) * COLS, chan), F32),
            pltpu.VMEM((count, 9 * chan), BF16),
            pltpu.VMEM((chan // LANES, 2 * ROWS, 2 * COLS, LANES), F32),
        ],
        compiler_params=pltpu.CompilerParams(vmem_limit_bytes=36 * 2**20),
        cost_estimate=pl.CostEstimate(
            flops=2_300_000_000, bytes_accessed=14_000_000, transcendentals=131_072
        ),
        name="decode_block",
    )(*args)


def shards(
    latent,
    gn_mean,
    gn_rstd,
    gn_gain,
    gn_shift,
    conv1_kernel,
    conv1_bias,
    conv2_kernel,
    conv2_bias,
    tile_dest,
):
    chan = latent.shape[2]
    full_rows = latent.shape[0] * lax.axis_size("img")
    full_cols = latent.shape[1] * lax.axis_size("bal")
    row_even, row_odd = exchange(latent, "img", 0)
    img_even = lax.axis_index("img") % 2 == 0
    above = jnp.where(img_even, row_odd, row_even)
    below = jnp.where(img_even, row_even, row_odd)
    tall = jnp.concatenate([above, latent, below], axis=0)
    col_even, col_odd = exchange(tall, "bal", 1)
    summed = sum_taps(conv2_kernel)
    return run_block(
        full_rows,
        full_cols,
        latent,
        row_even,
        row_odd,
        col_even,
        col_odd,
        gn_mean.reshape(1, -1),
        gn_rstd.reshape(1, -1),
        gn_gain.reshape(1, chan),
        gn_shift.reshape(1, chan),
        conv1_kernel.reshape(3, 3 * chan, -1),
        conv1_bias.reshape(1, -1),
        summed,
        conv2_bias.reshape(1, -1),
        tile_dest,
    )


def solution(mesh):
    placed = (P("img", "bal", None), P(), P(), P(), P(), P(), P(), P(), P(), P("img", "bal"))
    return jax.shard_map(
        shards, mesh=mesh, in_specs=placed, out_specs=P("img", "bal", None), check_vma=False
    )
```

time: 113 us -> 26.9 us (0.24)
  the two profiles are of different devices: /device:TPU:1 before, /device:TPU:248 now
where the time goes in v1:
time: 26.9 us; the launch traced here: 26.6 us
  starting transfers between devices  14.6 us (54%)
  Pallas kernels  5.77 us (21%)
  local copies, waits for them, and re-layouts  3.33 us (12%)
  other arithmetic  1.83 us (7%)
  waiting for transfers between devices  0.9 us (3%)
    ppermute x2, starting transfers between devices, exchange(): from_even = lax.ppermute(jnp.where(even, tail, head), axis, swaps(count, 0))  8.54 us
    ppermute x2, starting transfers between devices, exchange(): from_odd = lax.ppermute(jnp.where(even, head, tail), axis, swaps(count, 1))  6.1 us
    pallas_call x1, Pallas kernels, run_block(): pl.pallas_call(functools.partial(block_kernel, full_rows, full_cols), out...  4.55 us
    unnamed x20, local copies, waits for them, and re-layouts  3.33 us
    select_n x2, other arithmetic, exchange(): from_odd = lax.ppermute(jnp.where(even, head, tail), axis, swaps(count, 1))  1.81 us
    pallas_call x1, Pallas kernels, sum_taps(): pl.pallas_call(sum_taps_kernel, out_shape=jax.ShapeDtypeStruct((2, 2, 4 *...  1.21 us
    ppermute x2, waiting for transfers between devices, exchange(): from_even = lax.ppermute(jnp.where(even, tail, head), axis, swaps(count, 0))  0.82 us
  transfers between devices with their start and end apart: 4, of which 2 were waited for; matrix products, arithmetic and copies ran while one was open for 0% of the time, Pallas kernels for 5%

profile of v1, /device:TPU:248, one launch (start us, length us, event | category | flops | bytes accessed | tf_op | source)
XLA Modules:
  0.0 26.6 jit_solution(5423862010146812641)
XLA Ops:
  0.0 0.8 %broadcast_select_fusion.4 = (bf16[2,12,512]{2,1,0:T(8,128)(2,1)S(1)}, bf16[2,12,512]{2,1,0:T(8,128)(2,1)S(1)}) fusion(pred[]{:T(512)S(6)} %eq.11, bf16[12,12,512]{2,1,0:T(8,128)(2,1)} %x_ref.1), kind=kLoop, calls=%fused_computation.7 | loop fusion | flops 24576 | bytes 98305 | tf_op jit(solution)/shard_map/jit(_where)/select_n | solution.py:35
  0.8 1.9 %collective-permute-start.1 = (bf16[2,12,512]{2,1,0:T(8,128)(2,1)S(1)}, bf16[2,12,512]{2,1,0:T(8,128)(2,1)S(1)}, u32[]{:S(2)}, u32[]{:S(2)}) collective-permute-start(bf16[2,12,512]{2,1,0:T(8,128)(2,1)S(1)} %get-tuple-element.8), channel_id=1, source_target_pairs={{16,32},{32,16},{48,64},{64,48},{80,96},{96,80},{112,128},{128,112... | collective-permute-start | bytes 73736 | tf_op jit(solution)/shard_map/ppermute | solution.py:35
  2.7 5.1 %collective-permute-start = (bf16[2,12,512]{2,1,0:T(8,128)(2,1)S(1)}, bf16[2,12,512]{2,1,0:T(8,128)(2,1)S(1)}, u32[]{:S(2)}, u32[]{:S(2)}) collective-permute-start(bf16[2,12,512]{2,1,0:T(8,128)(2,1)S(1)} %get-tuple-element.9), channel_id=1, source_target_pairs={{0,16},{16,0},{32,48},{48,32},{64,80},{80,64},{96,112},{112,96},{1... | collective-permute-start | bytes 73736 | tf_op jit(solution)/shard_map/ppermute | solution.py:34
  7.9 0.0 collective-permute-done.1.row_odd
  7.9 0.8 %collective-permute-done.row_even = bf16[2,12,512]{2,1,0:T(8,128)(2,1)S(1)} collective-permute-done((bf16[2,12,512]{2,1,0:T(8,128)(2,1)S(1)}, bf16[2,12,512]{2,1,0:T(8,128)(2,1)S(1)}, u32[]{:S(2)}, u32[]{:S(2)}) %collective-permute-start) | collective-permute-done | bytes 24608 | tf_op jit(solution)/shard_map/ppermute | solution.py:34
  8.7 1.0 %broadcast_select_fusion = (bf16[16,2,512]{2,1,0:T(2,128)(2,1)S(1)}, bf16[16,2,512]{2,1,0:T(2,128)(2,1)S(1)}, bf16[16,2,512]{2,1,0:T(2,128)(2,1)S(1)}) fusion(pred[]{:T(512)S(6)} %eq.12, bf16[2,12,512]{2,1,0:T(8,128)(2,1)S(1)} %get-tuple-element.11, bf16[12,12,512]{2,1,0:T(8,128)(2,1)} %x_ref.1, bf16[2,12,512]{2,1,0:T(8,128)(2,1)S(1)} %get-tuple-element.10), kind=kLoop, calls=%fused_computation | loop fusion | flops 212992 | bytes 294913 | tf_op jit(solution)/shard_map/jit(_where)/select_n | solution.py:35
  9.7 3.4 %collective-permute-start.2 = (bf16[16,2,512]{2,1,0:T(2,128)(2,1)S(1)}, bf16[16,2,512]{2,1,0:T(2,128)(2,1)S(1)}, u32[]{:S(2)}, u32[]{:S(2)}) collective-permute-start(bf16[16,2,512]{2,1,0:T(2,128)(2,1)S(1)} %bitcast.19), channel_id=1, source_target_pairs={{0,1},{1,0},{2,3},{3,2},{4,5},{5,4},{6,7},{7,6},{8,9},{9,8},{10,11... | collective-permute-start | bytes 98312 | tf_op jit(solution)/shard_map/ppermute | solution.py:34
  13.2 4.2 %collective-permute-start.3 = (bf16[16,2,512]{2,1,0:T(2,128)(2,1)S(1)}, bf16[16,2,512]{2,1,0:T(2,128)(2,1)S(1)}, u32[]{:S(2)}, u32[]{:S(2)}) collective-permute-start(bf16[16,2,512]{2,1,0:T(2,128)(2,1)S(1)} %get-tuple-element.5), channel_id=1, source_target_pairs={{1,2},{2,1},{3,4},{4,3},{5,6},{6,5},{7,8},{8,7},{9,10},{10,9},{11,... | collective-permute-start | bytes 98312 | tf_op jit(solution)/shard_map/ppermute | solution.py:35
  17.3 0.0 copy-start
  17.4 2.3 %copy-done = bf16[3,3,512,512]{3,2,1,0:T(8,128)(2,1)S(1)} copy-done((bf16[3,3,512,512]{3,2,1,0:T(8,128)(2,1)S(1)}, bf16[3,3,512,512]{3,2,1,0:T(8,128)(2,1)}, u32[]{:S(2)}) %copy-start) | copy-done | bytes 4718616
  19.7 0.0 copy-start.1
  19.7 0.0 copy-start.2
  19.7 0.0 copy-start.3
  19.7 0.0 copy-start.4
  19.7 0.0 copy-start.5
  19.7 0.0 copy-start.6
  19.7 0.0 copy-start.7
  19.7 0.0 copy-start.8
  19.7 0.0 copy-start.9
  19.8 1.2 %sum_taps.1.w2_ref = bf16[2,2,2048,512]{3,2,1,0:T(8,128)(2,1)S(1)} custom-call(bf16[3,3,512,512]{3,2,1,0:T(8,128)(2,1)S(1)} %copy-done), custom_call_target="tpu_custom_call" | custom-call | flops 10000000 | bytes 13000000 | tf_op jit(solution)/shard_map/sum_taps/pallas_call | solution.py:69
  21.0 0.0 collective-permute-done.2.col_even
  21.0 0.1 collective-permute-done.3.col_odd
  21.1 1.0 %copy-done.1 = bf16[3,3,512,512]{3,2,1,0:T(8,128)(2,1)S(1)} copy-done((bf16[3,3,512,512]{3,2,1,0:T(8,128)(2,1)S(1)}, bf16[3,3,512,512]{3,2,1,0:T(8,128)(2,1)}, u32[]{:S(2)}) %copy-start.1) | copy-done | bytes 4718616
  22.0 0.0 copy-done.2
  22.0 0.0 copy-done.3
  22.0 0.0 copy-done.4
  22.0 0.0 copy-done.5
  22.0 0.0 copy-done.6
  22.0 0.0 copy-done.7
  22.1 0.0 copy-done.8
  22.1 0.0 copy-done.9
  22.1 4.6 %decode_block.1 = bf16[24,24,512]{2,1,0:T(8,128)(2,1)} custom-call(bf16[12,12,512]{2,1,0:T(8,128)(2,1)S(1)} %copy-done.2, bf16[2,12,512]{2,1,0:T(8,128)(2,1)S(1)} %collective-permute-done.row_even, bf16[2,12,512]{2,1,0:T(8,128)(2,1)S(1)} %collective-permute-done.1.row_odd, bf16[16,2,512]{2,1,0:T(2,128)(2,1)S(1)} %collective-permute-done.2.col_even, ...), custom_call_target="tpu_custom_call" | custom-call | flops 2300000000 | bytes 14000000 | tf_op jit(solution)/shard_map/decode_block/pallas_call | solution.py:208
  (2 shorter events, 0.0 us)
Async XLA Ops:
  0.8 7.1 %collective-permute-start.1 = (bf16[2,12,512]{2,1,0:T(8,128)(2,1)S(1)}, bf16[2,12,512]{2,1,0:T(8,128)(2,1)S(1)}, u32[]{:S(2)}, u32[]{:S(2)}) collective-permute-start(bf16[2,12,512]{2,1,0:T(8,128)(2,1)S(1)} %get-tuple-element.8), channel_id=1, source_target_pairs={{16,32},{32,16},{48,64},{64,48},{80,96},{96,80},{112,128},{128,112... | collective-permute-start | bytes 73736 | tf_op jit(solution)/shard_map/ppermute | solution.py:35
  2.7 6.0 %collective-permute-start = (bf16[2,12,512]{2,1,0:T(8,128)(2,1)S(1)}, bf16[2,12,512]{2,1,0:T(8,128)(2,1)S(1)}, u32[]{:S(2)}, u32[]{:S(2)}) collective-permute-start(bf16[2,12,512]{2,1,0:T(8,128)(2,1)S(1)} %get-tuple-element.9), channel_id=1, source_target_pairs={{0,16},{16,0},{32,48},{48,32},{64,80},{80,64},{96,112},{112,96},{1... | collective-permute-start | bytes 73736 | tf_op jit(solution)/shard_map/ppermute | solution.py:34
  9.7 11.2 %collective-permute-start.2 = (bf16[16,2,512]{2,1,0:T(2,128)(2,1)S(1)}, bf16[16,2,512]{2,1,0:T(2,128)(2,1)S(1)}, u32[]{:S(2)}, u32[]{:S(2)}) collective-permute-start(bf16[16,2,512]{2,1,0:T(2,128)(2,1)S(1)} %bitcast.19), channel_id=1, source_target_pairs={{0,1},{1,0},{2,3},{3,2},{4,5},{5,4},{6,7},{7,6},{8,9},{9,8},{10,11... | collective-permute-start | bytes 98312 | tf_op jit(solution)/shard_map/ppermute | solution.py:34
  13.2 7.9 %collective-permute-start.3 = (bf16[16,2,512]{2,1,0:T(2,128)(2,1)S(1)}, bf16[16,2,512]{2,1,0:T(2,128)(2,1)S(1)}, u32[]{:S(2)}, u32[]{:S(2)}) collective-permute-start(bf16[16,2,512]{2,1,0:T(2,128)(2,1)S(1)} %get-tuple-element.5), channel_id=1, source_target_pairs={{1,2},{2,1},{3,4},{4,3},{5,6},{6,5},{7,8},{8,7},{9,10},{10,9},{11,... | collective-permute-start | bytes 98312 | tf_op jit(solution)/shard_map/ppermute | solution.py:35
  17.3 2.3 %copy-start = (bf16[3,3,512,512]{3,2,1,0:T(8,128)(2,1)S(1)}, bf16[3,3,512,512]{3,2,1,0:T(8,128)(2,1)}, u32[]{:S(2)}) copy-start(bf16[3,3,512,512]{3,2,1,0:T(8,128)(2,1)} %w_ref.1) | copy-start | bytes 14155780
  19.7 2.3 %copy-start.1 = (bf16[3,3,512,512]{3,2,1,0:T(8,128)(2,1)S(1)}, bf16[3,3,512,512]{3,2,1,0:T(8,128)(2,1)}, u32[]{:S(2)}) copy-start(bf16[3,3,512,512]{3,2,1,0:T(8,128)(2,1)} %param.15) | copy-start | bytes 14155780
  19.7 2.3 %copy-start.2 = (bf16[12,12,512]{2,1,0:T(8,128)(2,1)S(1)}, bf16[12,12,512]{2,1,0:T(8,128)(2,1)}, u32[]{:S(2)}) copy-start(bf16[12,12,512]{2,1,0:T(8,128)(2,1)} %x_ref.1) | copy-start | bytes 442372
  19.7 2.3 %copy-start.3 = (f32[512]{0:T(512)S(1)}, f32[512]{0:T(512)}, u32[]{:S(2)}) copy-start(f32[512]{0:T(512)} %param.13) | copy-start | bytes 6148
  19.7 2.3 %copy-start.4 = (f32[512]{0:T(512)S(1)}, f32[512]{0:T(512)}, u32[]{:S(2)}) copy-start(f32[512]{0:T(512)} %param.14) | copy-start | bytes 6148
  19.7 2.3 %copy-start.5 = (f32[512]{0:T(512)S(1)}, f32[512]{0:T(512)}, u32[]{:S(2)}) copy-start(f32[512]{0:T(512)} %param.16) | copy-start | bytes 6148
  19.7 2.3 %copy-start.6 = (f32[512]{0:T(512)S(1)}, f32[512]{0:T(512)}, u32[]{:S(2)}) copy-start(f32[512]{0:T(512)} %param.18) | copy-start | bytes 6148
  19.7 2.3 %copy-start.7 = (s32[4,4]{1,0:T(4,128)S(1)}, s32[4,4]{1,0:T(4,128)}, u32[]{:S(2)}) copy-start(s32[4,4]{1,0:T(4,128)} %dest_ref.1) | copy-start | bytes 196
  19.7 2.3 %copy-start.8 = (f32[32]{0:T(128)S(1)}, f32[32]{0:T(128)}, u32[]{:S(2)}) copy-start(f32[32]{0:T(128)} %param.11) | copy-start | bytes 388
  19.7 2.3 %copy-start.9 = (f32[32]{0:T(128)S(1)}, f32[32]{0:T(128)}, u32[]{:S(2)}) copy-start(f32[32]{0:T(128)} %param.12) | copy-start | bytes 388

commit v2 on v1

--- a/solution.py
+++ b/solution.py
@@ -25,20 +25,32 @@
     return pairs
 
 
-def exchange(cells, axis, dim):
-    count = lax.axis_size(axis)
+def edges(cells, axis, dim):
     even = lax.axis_index(axis) % 2 == 0
     length = cells.shape[dim]
     head = lax.slice_in_dim(cells, 0, 2, axis=dim)
     tail = lax.slice_in_dim(cells, length - 2, length, axis=dim)
-    from_even = lax.ppermute(jnp.where(even, tail, head), axis, swaps(count, 0))
-    from_odd = lax.ppermute(jnp.where(even, head, tail), axis, swaps(count, 1))
-    return from_even, from_odd
-
-
-def sum_taps_kernel(w_ref, o_ref):
+    return jnp.where(even, head, tail), jnp.where(even, tail, head)
+
+
+def swap(edge_odd, edge_even, axis):
+    count = lax.axis_size(axis)
+    from_odd = lax.ppermute(edge_odd, axis, swaps(count, 1))
+    from_even = lax.ppermute(edge_even, axis, swaps(count, 0))
+    return from_odd, from_even
+
+
+def sum_taps_kernel(w_hbm, o_ref, w_ref, sems):
     chan = w_ref.shape[2]
     step, lanes = 16, 256
+    parts = sems.shape[0]
+    depth = chan // parts
+    copies = []
+    for part in range(parts):
+        at = pl.ds(part * depth, depth)
+        copy = pltpu.make_async_copy(w_hbm.at[:, :, at], w_ref.at[:, :, at], sems.at[part])
+        copy.start()
+        copies.append(copy)
 
     def body(i, carry):
         rows = pl.ds(pl.multiple_of(i * step, step), step)
@@ -61,7 +73,9 @@
                             o_ref[p, q, at, cols] = full[2 * q + b].astype(BF16)
         return carry
 
-    lax.fori_loop(0, chan // step, body, 0)
+    for part in range(parts):
+        copies[part].wait()
+        lax.fori_loop(part * depth // step, (part + 1) * depth // step, body, 0)
 
 
 def sum_taps(kernel):
@@ -69,12 +83,13 @@
     return pl.pallas_call(
         sum_taps_kernel,
         out_shape=jax.ShapeDtypeStruct((2, 2, 4 * chan, outs), BF16),
-        in_specs=[pl.BlockSpec(memory_space=pltpu.VMEM)],
+        in_specs=[pl.BlockSpec(memory_space=pltpu.HBM)],
         out_specs=pl.BlockSpec(memory_space=pltpu.VMEM),
-        compiler_params=pltpu.CompilerParams(vmem_limit_bytes=24 * 2**20),
+        scratch_shapes=[pltpu.VMEM(kernel.shape, BF16), pltpu.SemaphoreType.DMA((4,))],
+        compiler_params=pltpu.CompilerParams(vmem_limit_bytes=20 * 2**20),
         cost_estimate=pl.CostEstimate(flops=10_000_000, bytes_accessed=13_000_000, transcendentals=0),
         name="sum_taps",
-    )(kernel)
+    )(pltpu.with_memory_space_constraint(kernel, pltpu.HBM))
 
 
 def block_kernel(
@@ -83,8 +98,8 @@
     x_ref,
     row_even,
     row_odd,
+    col_odd,
     col_even,
-    col_odd,
     mean_ref,
     rstd_ref,
     gain_ref,
@@ -119,9 +134,12 @@
     gain = gain_ref[...]
     shift = shift_ref[...]
 
+    scale = 0.5 * rstd * gain
+    offset = 0.5 * shift - mean * scale
+
     def activate(cells):
-        v = (cells.astype(F32) - mean) * rstd * gain + shift
-        return v / (1.0 + jnp.exp(-v))
+        v = cells * scale + offset
+        return v * jnp.tanh(v) + v
 
     def pick(even, even_ref, odd_ref, row):
         a, b = even_ref[row], odd_ref[row]
@@ -187,28 +205,26 @@
                 for k in range(wide.shape[0]):
                     lane = slice(k * LANES, (k + 1) * LANES)
                     wide[k, 2 * r + p, pl.ds(q, COLS, stride=2)] = z[r * COLS : (r + 1) * COLS, lane]
-    cell = lax.broadcasted_iota(jnp.int32, (2 * COLS, 1), 0)
+    cell = lax.broadcasted_iota(jnp.int32, (2 * COLS, TC), 0)
+    own = cell // (2 * TS) == lax.broadcasted_iota(jnp.int32, (2 * COLS, TC), 1)
     for i in range(TR):
-        live = jnp.zeros((2 * COLS, 1), jnp.int32)
-        for j in range(TC):
-            live = jnp.where(cell // (2 * TS) == j, (dest_ref[i, j] >= 0).astype(jnp.int32), live)
+        live = jnp.max(jnp.where(own, dest_ref[i : i + 1], -1), axis=1, keepdims=True)
         for r in range(i * 2 * TS, (i + 1) * 2 * TS):
             for k in range(wide.shape[0]):
                 lane = slice(k * LANES, (k + 1) * LANES)
-                o_ref[r, :, lane] = jnp.where(live > 0, wide[k, r], 0.0).astype(BF16)
+                o_ref[r, :, lane] = jnp.where(live >= 0, wide[k, r], 0.0).astype(BF16)
 
 
 def run_block(full_rows, full_cols, *args):
     chan = args[0].shape[2]
     vmem = pl.BlockSpec(memory_space=pltpu.VMEM)
-    smem = pl.BlockSpec(memory_space=pltpu.SMEM)
     side = ROWS + 4
     inner = (ROWS + 2) * PITCH
     count = ROWS * COLS
     return pl.pallas_call(
         functools.partial(block_kernel, full_rows, full_cols),
         out_shape=jax.ShapeDtypeStruct((2 * ROWS, 2 * COLS, chan), BF16),
-        in_specs=[vmem] * 13 + [smem],
+        in_specs=[vmem] * 14,
         out_specs=vmem,
         scratch_shapes=[
             pltpu.VMEM((side * PITCH + 8, chan), F32),
@@ -241,12 +257,14 @@
     chan = latent.shape[2]
     full_rows = latent.shape[0] * lax.axis_size("img")
     full_cols = latent.shape[1] * lax.axis_size("bal")
-    row_even, row_odd = exchange(latent, "img", 0)
+    row_odd, row_even = swap(*edges(latent, "img", 0), "img")
+    col_own = lax.optimization_barrier(edges(latent, "bal", 1))
     img_even = lax.axis_index("img") % 2 == 0
-    above = jnp.where(img_even, row_odd, row_even)
-    below = jnp.where(img_even, row_even, row_odd)
-    tall = jnp.concatenate([above, latent, below], axis=0)
-    col_even, col_odd = exchange(tall, "bal", 1)
+    above = edges(jnp.where(img_even, row_odd, row_even), "bal", 1)
+    below = edges(jnp.where(img_even, row_even, row_odd), "bal", 1)
+    col_odd, col_even = swap(
+        *(jnp.concatenate(part, axis=0) for part in zip(above, col_own, below)), "bal"
+    )
     summed = sum_taps(conv2_kernel)
     return run_block(
         full_rows,
@@ -254,8 +272,8 @@
         latent,
         row_even,
         row_odd,
+        col_odd,
         col_even,
-        col_odd,
         gn_mean.reshape(1, -1),
         gn_rstd.reshape(1, -1),
         gn_gain.reshape(1, chan),

time: 26.9 us -> 24.4 us (0.907)
  local copies, waits for them, and re-layouts: 3.33 us -> 0.07 us
  Pallas kernels: 5.77 us -> 6.58 us
  starting transfers between devices: 14.6 us -> 14.1 us
  waiting for transfers between devices: 0.9 us -> 1.17 us
    unnamed x20, local copies, waits for them, and re-layouts: 3.33 us -> 0.07 us
    pallas_call x1, Pallas kernels: 1.21 us -> 2.67 us  [sum_taps(): pl.pallas_call(sum_taps_kernel, out_shape=jax.ShapeDtypeStruct((2, 2, 4 *...]
    pallas_call x1, Pallas kernels: 4.55 us -> 3.91 us  [run_block(): pl.pallas_call(functools.partial(block_kernel, full_rows, full_cols), out...]
    ppermute x4, starting transfers between devices: 14.6 us -> 14.1 us  [the longest x2 7.36 us: swap(): from_even = lax.ppermute(edge_even, axis, swaps(count, 0))]
  transfers between devices with their start and end apart: 4 -> 4, of which waited for: 2 -> 1; matrix products, arithmetic and copies ran while one was open for 0% -> 4% of each run, Pallas kernels for 5% -> 11%
where the time goes in v2:
time: 24.4 us; the launch traced here: 24.1 us
  starting transfers between devices  14.1 us (58%)
  Pallas kernels  6.58 us (27%)
  other arithmetic  1.93 us (8%)
  waiting for transfers between devices  1.17 us (5%)
  between operations  0.26 us (1%)
    ppermute x2, starting transfers between devices, swap(): from_even = lax.ppermute(edge_even, axis, swaps(count, 0))  7.36 us
    ppermute x2, starting transfers between devices, swap(): from_odd = lax.ppermute(edge_odd, axis, swaps(count, 1))  6.76 us
    pallas_call x1, Pallas kernels, run_block(): pl.pallas_call(functools.partial(block_kernel, full_rows, full_cols), out...  3.91 us
    pallas_call x1, Pallas kernels, sum_taps(): pl.pallas_call(sum_taps_kernel, out_shape=jax.ShapeDtypeStruct((2, 2, 4 *...  2.67 us
    select_n x3, other arithmetic, edges(): return (jnp.where(even, head, tail), jnp.where(even, tail, head))  1.81 us
    ppermute x2, waiting for transfers between devices, swap(): from_even = lax.ppermute(edge_even, axis, swaps(count, 0))  1.16 us
  transfers between devices with their start and end apart: 4, of which 1 were waited for; matrix products, arithmetic and copies ran while one was open for 4% of the time, Pallas kernels for 11%

profile of v2, /device:TPU:248, one launch (start us, length us, event | category | flops | bytes accessed | tf_op | source)
XLA Modules:
  0.0 24.1 jit_solution(8927547038940997552)
XLA Ops:
  0.0 0.8 %broadcast_select_fusion.4 = (bf16[2,12,512]{2,1,0:T(8,128)(2,1)S(1)}, bf16[2,12,512]{2,1,0:T(8,128)(2,1)S(1)}) fusion(pred[]{:T(512)S(6)} %eq.15, bf16[12,12,512]{2,1,0:T(8,128)(2,1)} %x_ref.1), kind=kLoop, calls=%fused_computation.6 | loop fusion | flops 24576 | bytes 98305 | tf_op jit(solution)/shard_map/jit(_where)/select_n | solution.py:33
  0.8 1.9 %collective-permute-start.1 = (bf16[2,12,512]{2,1,0:T(8,128)(2,1)S(1)}, bf16[2,12,512]{2,1,0:T(8,128)(2,1)S(1)}, u32[]{:S(2)}, u32[]{:S(2)}) collective-permute-start(bf16[2,12,512]{2,1,0:T(8,128)(2,1)S(1)} %get-tuple-element.11), channel_id=1, source_target_pairs={{16,32},{32,16},{48,64},{64,48},{80,96},{96,80},{112,128},{128,112... | collective-permute-start | bytes 73736 | tf_op jit(solution)/shard_map/ppermute | solution.py:38
  2.7 5.1 %collective-permute-start = (bf16[2,12,512]{2,1,0:T(8,128)(2,1)S(1)}, bf16[2,12,512]{2,1,0:T(8,128)(2,1)S(1)}, u32[]{:S(2)}, u32[]{:S(2)}) collective-permute-start(bf16[2,12,512]{2,1,0:T(8,128)(2,1)S(1)} %get-tuple-element.12), channel_id=1, source_target_pairs={{0,16},{16,0},{32,48},{48,32},{64,80},{80,64},{96,112},{112,96},{1... | collective-permute-start | bytes 73736 | tf_op jit(solution)/shard_map/ppermute | solution.py:39
  7.9 1.0 %broadcast_select_fusion = (bf16[12,2,512]{2,1,0:T(2,128)(2,1)S(1)}, bf16[12,2,512]{2,1,0:T(2,128)(2,1)S(1)}) fusion(pred[]{:T(512)S(6)} %eq.16, bf16[12,12,512]{2,1,0:T(8,128)(2,1)} %x_ref.1), kind=kLoop, calls=%fused_computation | loop fusion | flops 24576 | bytes 98305 | tf_op jit(solution)/shard_map/jit(_where)/select_n | solution.py:33
  8.9 0.0 collective-permute-done.1.row_odd
  8.9 0.0 collective-permute-done.row_even
  8.9 0.1 pad_maximum_fusion
  9.0 4.8 %collective-permute-start.2 = (bf16[16,2,512]{2,1,0:T(2,128)(2,1)S(1)}, bf16[16,2,512]{2,1,0:T(2,128)(2,1)S(1)}, u32[]{:S(2)}, u32[]{:S(2)}) collective-permute-start(bf16[16,2,512]{2,1,0:T(2,128)(2,1)S(1)} %pad_maximum_fusion), channel_id=1, source_target_pairs={{1,2},{2,1},{3,4},{4,3},{5,6},{6,5},{7,8},{8,7},{9,10},{10,9},{11,... | collective-permute-start | bytes 98312 | tf_op jit(solution)/shard_map/ppermute | solution.py:38
  13.9 0.0 slice-start
  13.9 0.1 pad_maximum_fusion.1
  13.9 0.0 slice-start.1
  13.9 0.0 copy-start
  14.0 0.0 copy-start.1
  14.0 0.0 copy-start.2
  14.0 0.0 copy-start.3
  14.0 0.0 copy-start.4
  14.0 0.0 copy-start.5
  14.0 0.0 copy-start.6
  14.0 0.0 copy-start.7
  14.0 2.2 %collective-permute-start.3 = (bf16[16,2,512]{2,1,0:T(2,128)(2,1)S(1)}, bf16[16,2,512]{2,1,0:T(2,128)(2,1)S(1)}, u32[]{:S(2)}, u32[]{:S(2)}) collective-permute-start(bf16[16,2,512]{2,1,0:T(2,128)(2,1)S(1)} %pad_maximum_fusion.1), channel_id=1, source_target_pairs={{0,1},{1,0},{2,3},{3,2},{4,5},{5,4},{6,7},{7,6},{8,9},{9,8},{10,11... | collective-permute-start | bytes 98312 | tf_op jit(solution)/shard_map/ppermute | solution.py:39
  16.3 2.7 %sum_taps.1.w2_ref = bf16[2,2,2048,512]{3,2,1,0:T(8,128)(2,1)S(1)} custom-call(bf16[3,3,512,512]{3,2,1,0:T(8,128)(2,1)} %w_hbm.1), custom_call_target="tpu_custom_call" | custom-call | flops 10000000 | bytes 13000000 | tf_op jit(solution)/shard_map/sum_taps/pallas_call | solution.py:83
  18.9 0.0 collective-permute-done.2.col_odd
  19.0 1.2 %collective-permute-done.3.col_even = bf16[16,2,512]{2,1,0:T(2,128)(2,1)S(1)} collective-permute-done((bf16[16,2,512]{2,1,0:T(2,128)(2,1)S(1)}, bf16[16,2,512]{2,1,0:T(2,128)(2,1)S(1)}, u32[]{:S(2)}, u32[]{:S(2)}) %collective-permute-start.3) | collective-permute-done | bytes 32800 | tf_op jit(solution)/shard_map/ppermute | solution.py:39
  20.1 0.0 slice-done
  20.1 0.0 slice-done.1
  20.1 0.0 copy-done
  20.1 0.0 copy-done.1
  20.1 0.0 copy-done.2
  20.1 0.0 copy-done.3
  20.2 0.0 copy-done.4
  20.2 0.0 copy-done.5
  20.2 3.9 %decode_block.1 = bf16[24,24,512]{2,1,0:T(8,128)(2,1)} custom-call(bf16[12,12,512]{2,1,0:T(8,128)(2,1)S(1)} %copy-done, bf16[2,12,512]{2,1,0:T(8,128)(2,1)S(1)} %collective-permute-done.row_even, bf16[2,12,512]{2,1,0:T(8,128)(2,1)S(1)} %collective-permute-done.1.row_odd, bf16[16,2,512]{2,1,0:T(2,128)(2,1)S(1)} %collective-permute-done.2.col_odd, ...), custom_call_target="tpu_custom_call" | custom-call | flops 2300000000 | bytes 14000000 | tf_op jit(solution)/shard_map/decode_block/pallas_call | solution.py:224
  (5 shorter events, 0.0 us)
Async XLA Ops:
  0.8 8.1 %collective-permute-start.1 = (bf16[2,12,512]{2,1,0:T(8,128)(2,1)S(1)}, bf16[2,12,512]{2,1,0:T(8,128)(2,1)S(1)}, u32[]{:S(2)}, u32[]{:S(2)}) collective-permute-start(bf16[2,12,512]{2,1,0:T(8,128)(2,1)S(1)} %get-tuple-element.11), channel_id=1, source_target_pairs={{16,32},{32,16},{48,64},{64,48},{80,96},{96,80},{112,128},{128,112... | collective-permute-start | bytes 73736 | tf_op jit(solution)/shard_map/ppermute | solution.py:38
  2.7 6.2 %collective-permute-start = (bf16[2,12,512]{2,1,0:T(8,128)(2,1)S(1)}, bf16[2,12,512]{2,1,0:T(8,128)(2,1)S(1)}, u32[]{:S(2)}, u32[]{:S(2)}) collective-permute-start(bf16[2,12,512]{2,1,0:T(8,128)(2,1)S(1)} %get-tuple-element.12), channel_id=1, source_target_pairs={{0,16},{16,0},{32,48},{48,32},{64,80},{80,64},{96,112},{112,96},{1... | collective-permute-start | bytes 73736 | tf_op jit(solution)/shard_map/ppermute | solution.py:39
  9.0 9.9 %collective-permute-start.2 = (bf16[16,2,512]{2,1,0:T(2,128)(2,1)S(1)}, bf16[16,2,512]{2,1,0:T(2,128)(2,1)S(1)}, u32[]{:S(2)}, u32[]{:S(2)}) collective-permute-start(bf16[16,2,512]{2,1,0:T(2,128)(2,1)S(1)} %pad_maximum_fusion), channel_id=1, source_target_pairs={{1,2},{2,1},{3,4},{4,3},{5,6},{6,5},{7,8},{8,7},{9,10},{10,9},{11,... | collective-permute-start | bytes 98312 | tf_op jit(solution)/shard_map/ppermute | solution.py:38
  13.9 6.3 %slice-start = ((s8[4718592]{0:T(1024)(128)(4,1)}), s8[4194304]{0:T(1024)(128)(4,1)S(1)}, s32[]{:S(2)}) async-start(s8[4718592]{0:T(1024)(128)(4,1)} %bitcast.7), calls=%async_computation | async-start | bytes 8388608
  13.9 6.2 %slice-start.1 = ((s8[4718592]{0:T(1024)(128)(4,1)}), s8[524288]{0:T(1024)(128)(4,1)S(1)}, s32[]{:S(2)}) async-start(s8[4718592]{0:T(1024)(128)(4,1)} %bitcast.7), calls=%async_computation.1 | async-start | bytes 1048576
  13.9 6.2 %copy-start = (bf16[12,12,512]{2,1,0:T(8,128)(2,1)S(1)}, bf16[12,12,512]{2,1,0:T(8,128)(2,1)}, u32[]{:S(2)}) copy-start(bf16[12,12,512]{2,1,0:T(8,128)(2,1)} %x_ref.1) | copy-start | bytes 442372
  14.0 6.2 %copy-start.1 = (f32[512]{0:T(512)S(1)}, f32[512]{0:T(512)}, u32[]{:S(2)}) copy-start(f32[512]{0:T(512)} %param.13) | copy-start | bytes 6148
  14.0 6.2 %copy-start.2 = (f32[512]{0:T(512)S(1)}, f32[512]{0:T(512)}, u32[]{:S(2)}) copy-start(f32[512]{0:T(512)} %param.14) | copy-start | bytes 6148
  14.0 6.2 %copy-start.3 = (f32[512]{0:T(512)S(1)}, f32[512]{0:T(512)}, u32[]{:S(2)}) copy-start(f32[512]{0:T(512)} %param.16) | copy-start | bytes 6148
  14.0 6.2 %copy-start.4 = (f32[512]{0:T(512)S(1)}, f32[512]{0:T(512)}, u32[]{:S(2)}) copy-start(f32[512]{0:T(512)} %param.18) | copy-start | bytes 6148
  14.0 6.2 %copy-start.5 = (s32[4,4]{1,0:T(4,128)S(1)}, s32[4,4]{1,0:T(4,128)}, u32[]{:S(2)}) copy-start(s32[4,4]{1,0:T(4,128)} %dest_ref.1) | copy-start | bytes 196
  14.0 6.2 %copy-start.6 = (f32[32]{0:T(128)S(1)}, f32[32]{0:T(128)}, u32[]{:S(2)}) copy-start(f32[32]{0:T(128)} %param.11) | copy-start | bytes 388
  14.0 6.2 %copy-start.7 = (f32[32]{0:T(128)S(1)}, f32[32]{0:T(128)}, u32[]{:S(2)}) copy-start(f32[32]{0:T(128)} %param.12) | copy-start | bytes 388
  14.0 6.1 %collective-permute-start.3 = (bf16[16,2,512]{2,1,0:T(2,128)(2,1)S(1)}, bf16[16,2,512]{2,1,0:T(2,128)(2,1)S(1)}, u32[]{:S(2)}, u32[]{:S(2)}) collective-permute-start(bf16[16,2,512]{2,1,0:T(2,128)(2,1)S(1)} %pad_maximum_fusion.1), channel_id=1, source_target_pairs={{0,1},{1,0},{2,3},{3,2},{4,5},{5,4},{6,7},{7,6},{8,9},{9,8},{10,11... | collective-permute-start | bytes 98312 | tf_op jit(solution)/shard_map/ppermute | solution.py:39

commit v3 on v2

--- a/solution.py
+++ b/solution.py
@@ -13,6 +13,7 @@
 ROWS = TR * TS
 COLS = TC * TS
 LANES = 128
+SPLIT = 256
 PITCH = 16
 F32 = jnp.float32
 BF16 = jnp.bfloat16
@@ -57,20 +58,9 @@
         for lane in range(0, w_ref.shape[3], lanes):
             cols = slice(lane, lane + lanes)
             k = [[w_ref[y, x, rows, cols].astype(F32) for x in range(3)] for y in range(3)]
-            by_row = [
-                [k[0][x] for x in range(3)],
-                [k[1][x] + k[2][x] for x in range(3)],
-                [k[0][x] + k[1][x] for x in range(3)],
-                [k[2][x] for x in range(3)],
-            ]
-            for p in range(2):
-                for a in range(2):
-                    u = by_row[2 * p + a]
-                    full = [u[0], u[1] + u[2], u[0] + u[1], u[2]]
-                    for q in range(2):
-                        for b in range(2):
-                            at = pl.ds(pl.multiple_of((a * 2 + b) * chan + i * step, step), step)
-                            o_ref[p, q, at, cols] = full[2 * q + b].astype(BF16)
+            for y, row in enumerate((k[0], [u + v + w for u, v, w in zip(*k)], k[2])):
+                for x, tap in enumerate((row[0], row[0] + row[1] + row[2], row[2])):
+                    o_ref[y, x, rows, cols] = tap.astype(BF16)
         return carry
 
     for part in range(parts):
@@ -79,10 +69,9 @@
 
 
 def sum_taps(kernel):
-    chan, outs = kernel.shape[2:]
     return pl.pallas_call(
         sum_taps_kernel,
-        out_shape=jax.ShapeDtypeStruct((2, 2, 4 * chan, outs), BF16),
+        out_shape=jax.ShapeDtypeStruct(kernel.shape, BF16),
         in_specs=[pl.BlockSpec(memory_space=pltpu.HBM)],
         out_specs=pl.BlockSpec(memory_space=pltpu.VMEM),
         scratch_shapes=[pltpu.VMEM(kernel.shape, BF16), pltpu.SemaphoreType.DMA((4,))],
@@ -116,6 +105,8 @@
     packed,
     near,
     wide,
+    done,
+    sems,
 ):
     chan = x_ref.shape[2]
     img = lax.axis_index("img")
@@ -171,48 +162,73 @@
         taps[:, d * chan : (d + 1) * chan] = act[d : d + total].astype(BF16)
 
     inner = (ROWS + 2) * PITCH
-    h = b1_ref[...]
-    for d in range(3):
-        h = h + jnp.dot(
-            taps[d * PITCH : d * PITCH + inner], w1_ref[d], preferred_element_type=F32
-        )
     cell = lax.broadcasted_iota(jnp.int32, (inner, 1), 0)
     row = img * ROWS - 1 + cell // PITCH
     col = bal * COLS - 1 + cell % PITCH
     ok = (row >= 0) & (row < full_rows) & (col >= 0) & (col < full_cols)
-    hid[0:inner] = jnp.where(ok, h, 0.0)
-
-    for d in range(3):
-        for r in range(ROWS + 2):
-            packed[d, r * COLS : (r + 1) * COLS] = hid[r * PITCH + d : r * PITCH + d + COLS]
     count = ROWS * COLS
-    for dy in range(3):
+    parts = [slice(n, n + SPLIT) for n in range(0, chan, SPLIT)]
+
+    for part in parts:
+        h = b1_ref[:, part]
+        for d in range(3):
+            h = h + jnp.dot(
+                taps[d * PITCH : d * PITCH + inner], w1_ref[d, :, part], preferred_element_type=F32
+            )
+        hid[0:inner, part] = jnp.where(ok, h, 0.0).astype(BF16).astype(F32)
+        for d in range(3):
+            for r in range(ROWS + 2):
+                at = r * PITCH + d
+                packed[d, r * COLS : (r + 1) * COLS, part] = hid[at : at + COLS, part]
+        packed[0, :, part] = packed[0, :, part] - packed[1, :, part]
+        packed[2, :, part] = packed[2, :, part] - packed[1, :, part]
         for dx in range(3):
-            at = (dy * 3 + dx) * chan
-            near[:, at : at + chan] = packed[dx, dy * COLS : dy * COLS + count].astype(BF16)
-    bias = b2_ref[...]
-    for p in range(2):
-        for q in range(2):
-            z = bias
-            for a in range(2):
-                at = ((p + a) * 3 + q) * chan
-                z = z + jnp.dot(
-                    near[:, at : at + 2 * chan],
-                    w2_ref[p, q, a * 2 * chan : (a + 1) * 2 * chan],
-                    preferred_element_type=F32,
-                )
-            for r in range(ROWS):
-                for k in range(wide.shape[0]):
-                    lane = slice(k * LANES, (k + 1) * LANES)
-                    wide[k, 2 * r + p, pl.ds(q, COLS, stride=2)] = z[r * COLS : (r + 1) * COLS, lane]
+            here = packed[dx, COLS : COLS + count, part]
+            for dy in range(3):
+                at = (dy * 3 + dx) * chan + part.start
+                cells = here
+                if dy != 1:
+                    cells = packed[dx, dy * COLS : dy * COLS + count, part] - here
+                near[:, at : at + SPLIT] = cells.astype(BF16)
+
     cell = lax.broadcasted_iota(jnp.int32, (2 * COLS, TC), 0)
     own = cell // (2 * TS) == lax.broadcasted_iota(jnp.int32, (2 * COLS, TC), 1)
-    for i in range(TR):
-        live = jnp.max(jnp.where(own, dest_ref[i : i + 1], -1), axis=1, keepdims=True)
-        for r in range(i * 2 * TS, (i + 1) * 2 * TS):
-            for k in range(wide.shape[0]):
+    live = [
+        jnp.max(jnp.where(own, dest_ref[i : i + 1], -1), axis=1, keepdims=True) >= 0
+        for i in range(TR)
+    ]
+    copies = []
+    for n, part in enumerate(parts):
+
+        def term(dy, dx):
+            at = (dy * 3 + dx) * chan
+            return jnp.dot(
+                near[:, at : at + chan], w2_ref[dy, dx, :, part], preferred_element_type=F32
+            )
+
+        base = term(1, 1) + b2_ref[:, part]
+        by_row = [base + term(0, 1), base + term(2, 1)]
+        lanes = range(part.start // LANES, part.stop // LANES)
+        for q in range(2):
+            by_col = term(1, 2 * q)
+            for p in range(2):
+                z = by_row[p] + by_col + term(2 * p, 2 * q)
+                for r in range(ROWS):
+                    for k in lanes:
+                        at = k * LANES - part.start
+                        wide[k, 2 * r + p, pl.ds(q, COLS, stride=2)] = z[
+                            r * COLS : (r + 1) * COLS, at : at + LANES
+                        ]
+        for r in range(2 * ROWS):
+            for k in lanes:
                 lane = slice(k * LANES, (k + 1) * LANES)
-                o_ref[r, :, lane] = jnp.where(live >= 0, wide[k, r], 0.0).astype(BF16)
+                kept = jnp.where(live[r // (2 * TS)], wide[k, r], 0.0)
+                done[r, :, lane] = kept.astype(BF16)
+        copy = pltpu.make_async_copy(done.at[:, :, part], o_ref.at[:, :, part], sems.at[n])
+        copy.start()
+        copies.append(copy)
+    for copy in copies:
+        copy.wait()
 
 
 def run_block(full_rows, full_cols, *args):
@@ -225,7 +241,7 @@
         functools.partial(block_kernel, full_rows, full_cols),
         out_shape=jax.ShapeDtypeStruct((2 * ROWS, 2 * COLS, chan), BF16),
         in_specs=[vmem] * 14,
-        out_specs=vmem,
+        out_specs=pl.BlockSpec(memory_space=pltpu.HBM),
         scratch_shapes=[
             pltpu.VMEM((side * PITCH + 8, chan), F32),
             pltpu.VMEM((side * PITCH, 3 * chan), BF16),
@@ -233,6 +249,8 @@
             pltpu.VMEM((3, (ROWS + 2) * COLS, chan), F32),
             pltpu.VMEM((count, 9 * chan), BF16),
             pltpu.VMEM((chan // LANES, 2 * ROWS, 2 * COLS, LANES), F32),
+            pltpu.VMEM((2 * ROWS, 2 * COLS, chan), BF16),
+            pltpu.SemaphoreType.DMA((chan // SPLIT,)),
         ],
         compiler_params=pltpu.CompilerParams(vmem_limit_bytes=36 * 2**20),
         cost_estimate=pl.CostEstimate(

time: 24.4 us -> 23.9 us (0.980)
  Pallas kernels: 6.58 us -> 6 us
    pallas_call x1, Pallas kernels: 3.91 us -> 3.4 us  [run_block(): pl.pallas_call(functools.partial(block_kernel, full_rows, full_cols), out...]
where the time goes in v3:
time: 23.9 us; the launch traced here: 23.6 us
  starting transfers between devices  14.1 us (59%)
  Pallas kernels  6 us (25%)
  other arithmetic  1.93 us (8%)
  waiting for transfers between devices  1.23 us (5%)
  between operations  0.26 us (1%)
    ppermute x2, starting transfers between devices, swap(): from_even = lax.ppermute(edge_even, axis, swaps(count, 0))  7.36 us
    ppermute x2, starting transfers between devices, swap(): from_odd = lax.ppermute(edge_odd, axis, swaps(count, 1))  6.76 us
    pallas_call x1, Pallas kernels, run_block(): pl.pallas_call(functools.partial(block_kernel, full_rows, full_cols), out...  3.4 us
    pallas_call x1, Pallas kernels, sum_taps(): pl.pallas_call(sum_taps_kernel, out_shape=jax.ShapeDtypeStruct(kernel.sha...  2.6 us
    select_n x3, other arithmetic, edges(): return (jnp.where(even, head, tail), jnp.where(even, tail, head))  1.81 us
    ppermute x2, waiting for transfers between devices, swap(): from_even = lax.ppermute(edge_even, axis, swaps(count, 0))  1.23 us
  transfers between devices with their start and end apart: 4, of which 1 were waited for; matrix products, arithmetic and copies ran while one was open for 4% of the time, Pallas kernels for 11%

profile of v3, /device:TPU:248, one launch (start us, length us, event | category | flops | bytes accessed | tf_op | source)
XLA Modules:
  0.0 23.6 jit_solution(13762211506870020048)
XLA Ops:
  0.0 0.8 %broadcast_select_fusion.4 = (bf16[2,12,512]{2,1,0:T(8,128)(2,1)S(1)}, bf16[2,12,512]{2,1,0:T(8,128)(2,1)S(1)}) fusion(pred[]{:T(512)S(6)} %eq.15, bf16[12,12,512]{2,1,0:T(8,128)(2,1)} %x_ref.1), kind=kLoop, calls=%fused_computation.6 | loop fusion | flops 24576 | bytes 98305 | tf_op jit(solution)/shard_map/jit(_where)/select_n | solution.py:34
  0.8 1.9 %collective-permute-start.1 = (bf16[2,12,512]{2,1,0:T(8,128)(2,1)S(1)}, bf16[2,12,512]{2,1,0:T(8,128)(2,1)S(1)}, u32[]{:S(2)}, u32[]{:S(2)}) collective-permute-start(bf16[2,12,512]{2,1,0:T(8,128)(2,1)S(1)} %get-tuple-element.11), channel_id=1, source_target_pairs={{16,32},{32,16},{48,64},{64,48},{80,96},{96,80},{112,128},{128,112... | collective-permute-start | bytes 73736 | tf_op jit(solution)/shard_map/ppermute | solution.py:39
  2.7 5.1 %collective-permute-start = (bf16[2,12,512]{2,1,0:T(8,128)(2,1)S(1)}, bf16[2,12,512]{2,1,0:T(8,128)(2,1)S(1)}, u32[]{:S(2)}, u32[]{:S(2)}) collective-permute-start(bf16[2,12,512]{2,1,0:T(8,128)(2,1)S(1)} %get-tuple-element.12), channel_id=1, source_target_pairs={{0,16},{16,0},{32,48},{48,32},{64,80},{80,64},{96,112},{112,96},{1... | collective-permute-start | bytes 73736 | tf_op jit(solution)/shard_map/ppermute | solution.py:40
  7.9 1.0 %broadcast_select_fusion = (bf16[12,2,512]{2,1,0:T(2,128)(2,1)S(1)}, bf16[12,2,512]{2,1,0:T(2,128)(2,1)S(1)}) fusion(pred[]{:T(512)S(6)} %eq.16, bf16[12,12,512]{2,1,0:T(8,128)(2,1)} %x_ref.1), kind=kLoop, calls=%fused_computation | loop fusion | flops 24576 | bytes 98305 | tf_op jit(solution)/shard_map/jit(_where)/select_n | solution.py:34
  8.9 0.0 collective-permute-done.1.row_odd
  8.9 0.0 collective-permute-done.row_even
  8.9 0.1 pad_maximum_fusion
  9.0 4.8 %collective-permute-start.2 = (bf16[16,2,512]{2,1,0:T(2,128)(2,1)S(1)}, bf16[16,2,512]{2,1,0:T(2,128)(2,1)S(1)}, u32[]{:S(2)}, u32[]{:S(2)}) collective-permute-start(bf16[16,2,512]{2,1,0:T(2,128)(2,1)S(1)} %pad_maximum_fusion), channel_id=1, source_target_pairs={{1,2},{2,1},{3,4},{4,3},{5,6},{6,5},{7,8},{8,7},{9,10},{10,9},{11,... | collective-permute-start | bytes 98312 | tf_op jit(solution)/shard_map/ppermute | solution.py:39
  13.9 0.0 slice-start
  13.9 0.1 pad_maximum_fusion.1
  13.9 0.0 slice-start.1
  13.9 0.0 copy-start
  14.0 0.0 copy-start.1
  14.0 0.0 copy-start.2
  14.0 0.0 copy-start.3
  14.0 0.0 copy-start.4
  14.0 0.0 copy-start.5
  14.0 0.0 copy-start.6
  14.0 0.0 copy-start.7
  14.0 2.2 %collective-permute-start.3 = (bf16[16,2,512]{2,1,0:T(2,128)(2,1)S(1)}, bf16[16,2,512]{2,1,0:T(2,128)(2,1)S(1)}, u32[]{:S(2)}, u32[]{:S(2)}) collective-permute-start(bf16[16,2,512]{2,1,0:T(2,128)(2,1)S(1)} %pad_maximum_fusion.1), channel_id=1, source_target_pairs={{0,1},{1,0},{2,3},{3,2},{4,5},{5,4},{6,7},{7,6},{8,9},{9,8},{10,11... | collective-permute-start | bytes 98312 | tf_op jit(solution)/shard_map/ppermute | solution.py:40
  16.3 2.6 %sum_taps.1.w2_ref = bf16[3,3,512,512]{3,2,1,0:T(8,128)(2,1)S(1)} custom-call(bf16[3,3,512,512]{3,2,1,0:T(8,128)(2,1)} %w_hbm.1), custom_call_target="tpu_custom_call" | custom-call | flops 10000000 | bytes 13000000 | tf_op jit(solution)/shard_map/sum_taps/pallas_call | solution.py:72
  18.9 0.0 collective-permute-done.2.col_odd
  18.9 1.2 %collective-permute-done.3.col_even = bf16[16,2,512]{2,1,0:T(2,128)(2,1)S(1)} collective-permute-done((bf16[16,2,512]{2,1,0:T(2,128)(2,1)S(1)}, bf16[16,2,512]{2,1,0:T(2,128)(2,1)S(1)}, u32[]{:S(2)}, u32[]{:S(2)}) %collective-permute-start.3) | collective-permute-done | bytes 32800 | tf_op jit(solution)/shard_map/ppermute | solution.py:40
  20.1 0.0 slice-done
  20.1 0.0 slice-done.1
  20.1 0.0 copy-done
  20.1 0.0 copy-done.1
  20.1 0.0 copy-done.2
  20.1 0.0 copy-done.3
  20.2 0.0 copy-done.4
  20.2 0.0 copy-done.5
  20.2 3.4 %decode_block.1 = bf16[24,24,512]{2,1,0:T(8,128)(2,1)} custom-call(bf16[12,12,512]{2,1,0:T(8,128)(2,1)S(1)} %copy-done, bf16[2,12,512]{2,1,0:T(8,128)(2,1)S(1)} %collective-permute-done.row_even, bf16[2,12,512]{2,1,0:T(8,128)(2,1)S(1)} %collective-permute-done.1.row_odd, bf16[16,2,512]{2,1,0:T(2,128)(2,1)S(1)} %collective-permute-done.2.col_odd, ...), custom_call_target="tpu_custom_call" | custom-call | flops 2300000000 | bytes 14000000 | tf_op jit(solution)/shard_map/decode_block/pallas_call | solution.py:240
  (5 shorter events, 0.0 us)
Async XLA Ops:
  0.8 8.1 %collective-permute-start.1 = (bf16[2,12,512]{2,1,0:T(8,128)(2,1)S(1)}, bf16[2,12,512]{2,1,0:T(8,128)(2,1)S(1)}, u32[]{:S(2)}, u32[]{:S(2)}) collective-permute-start(bf16[2,12,512]{2,1,0:T(8,128)(2,1)S(1)} %get-tuple-element.11), channel_id=1, source_target_pairs={{16,32},{32,16},{48,64},{64,48},{80,96},{96,80},{112,128},{128,112... | collective-permute-start | bytes 73736 | tf_op jit(solution)/shard_map/ppermute | solution.py:39
  2.7 6.2 %collective-permute-start = (bf16[2,12,512]{2,1,0:T(8,128)(2,1)S(1)}, bf16[2,12,512]{2,1,0:T(8,128)(2,1)S(1)}, u32[]{:S(2)}, u32[]{:S(2)}) collective-permute-start(bf16[2,12,512]{2,1,0:T(8,128)(2,1)S(1)} %get-tuple-element.12), channel_id=1, source_target_pairs={{0,16},{16,0},{32,48},{48,32},{64,80},{80,64},{96,112},{112,96},{1... | collective-permute-start | bytes 73736 | tf_op jit(solution)/shard_map/ppermute | solution.py:40
  9.0 9.9 %collective-permute-start.2 = (bf16[16,2,512]{2,1,0:T(2,128)(2,1)S(1)}, bf16[16,2,512]{2,1,0:T(2,128)(2,1)S(1)}, u32[]{:S(2)}, u32[]{:S(2)}) collective-permute-start(bf16[16,2,512]{2,1,0:T(2,128)(2,1)S(1)} %pad_maximum_fusion), channel_id=1, source_target_pairs={{1,2},{2,1},{3,4},{4,3},{5,6},{6,5},{7,8},{8,7},{9,10},{10,9},{11,... | collective-permute-start | bytes 98312 | tf_op jit(solution)/shard_map/ppermute | solution.py:39
  13.9 6.3 %slice-start = ((s8[4718592]{0:T(1024)(128)(4,1)}), s8[4194304]{0:T(1024)(128)(4,1)S(1)}, s32[]{:S(2)}) async-start(s8[4718592]{0:T(1024)(128)(4,1)} %bitcast.7), calls=%async_computation | async-start | bytes 8388608
  13.9 6.2 %slice-start.1 = ((s8[4718592]{0:T(1024)(128)(4,1)}), s8[524288]{0:T(1024)(128)(4,1)S(1)}, s32[]{:S(2)}) async-start(s8[4718592]{0:T(1024)(128)(4,1)} %bitcast.7), calls=%async_computation.1 | async-start | bytes 1048576
  13.9 6.2 %copy-start = (bf16[12,12,512]{2,1,0:T(8,128)(2,1)S(1)}, bf16[12,12,512]{2,1,0:T(8,128)(2,1)}, u32[]{:S(2)}) copy-start(bf16[12,12,512]{2,1,0:T(8,128)(2,1)} %x_ref.1) | copy-start | bytes 442372
  14.0 6.2 %copy-start.1 = (f32[512]{0:T(512)S(1)}, f32[512]{0:T(512)}, u32[]{:S(2)}) copy-start(f32[512]{0:T(512)} %param.13) | copy-start | bytes 6148
  14.0 6.2 %copy-start.2 = (f32[512]{0:T(512)S(1)}, f32[512]{0:T(512)}, u32[]{:S(2)}) copy-start(f32[512]{0:T(512)} %param.14) | copy-start | bytes 6148
  14.0 6.2 %copy-start.3 = (f32[512]{0:T(512)S(1)}, f32[512]{0:T(512)}, u32[]{:S(2)}) copy-start(f32[512]{0:T(512)} %param.16) | copy-start | bytes 6148
  14.0 6.2 %copy-start.4 = (f32[512]{0:T(512)S(1)}, f32[512]{0:T(512)}, u32[]{:S(2)}) copy-start(f32[512]{0:T(512)} %param.18) | copy-start | bytes 6148
  14.0 6.2 %copy-start.5 = (s32[4,4]{1,0:T(4,128)S(1)}, s32[4,4]{1,0:T(4,128)}, u32[]{:S(2)}) copy-start(s32[4,4]{1,0:T(4,128)} %dest_ref.1) | copy-start | bytes 196
  14.0 6.2 %copy-start.6 = (f32[32]{0:T(128)S(1)}, f32[32]{0:T(128)}, u32[]{:S(2)}) copy-start(f32[32]{0:T(128)} %param.11) | copy-start | bytes 388
  14.0 6.2 %copy-start.7 = (f32[32]{0:T(128)S(1)}, f32[32]{0:T(128)}, u32[]{:S(2)}) copy-start(f32[32]{0:T(128)} %param.12) | copy-start | bytes 388
  14.0 6.1 %collective-permute-start.3 = (bf16[16,2,512]{2,1,0:T(2,128)(2,1)S(1)}, bf16[16,2,512]{2,1,0:T(2,128)(2,1)S(1)}, u32[]{:S(2)}, u32[]{:S(2)}) collective-permute-start(bf16[16,2,512]{2,1,0:T(2,128)(2,1)S(1)} %pad_maximum_fusion.1), channel_id=1, source_target_pairs={{0,1},{1,0},{2,3},{3,2},{4,5},{5,4},{6,7},{7,6},{8,9},{9,8},{10,11... | collective-permute-start | bytes 98312 | tf_op jit(solution)/shard_map/ppermute | solution.py:40

commit v4 on v3

--- a/solution.py
+++ b/solution.py
@@ -13,6 +13,7 @@
 ROWS = TR * TS
 COLS = TC * TS
 LANES = 128
+STEP = 16
 SPLIT = 256
 PITCH = 16
 F32 = jnp.float32
@@ -26,67 +27,78 @@
     return pairs
 
 
-def edges(cells, axis, dim):
-    even = lax.axis_index(axis) % 2 == 0
-    length = cells.shape[dim]
-    head = lax.slice_in_dim(cells, 0, 2, axis=dim)
-    tail = lax.slice_in_dim(cells, length - 2, length, axis=dim)
-    return jnp.where(even, head, tail), jnp.where(even, tail, head)
-
-
-def swap(edge_odd, edge_even, axis):
-    count = lax.axis_size(axis)
-    from_odd = lax.ppermute(edge_odd, axis, swaps(count, 1))
-    from_even = lax.ppermute(edge_even, axis, swaps(count, 0))
-    return from_odd, from_even
-
-
-def sum_taps_kernel(w_hbm, o_ref, w_ref, sems):
-    chan = w_ref.shape[2]
-    step, lanes = 16, 256
-    parts = sems.shape[0]
-    depth = chan // parts
-    copies = []
-    for part in range(parts):
-        at = pl.ds(part * depth, depth)
-        copy = pltpu.make_async_copy(w_hbm.at[:, :, at], w_ref.at[:, :, at], sems.at[part])
+def pair_groups(rows, cols):
+    img = [[i * cols + j, (i + 1) * cols + j] for i in range(0, rows, 2) for j in range(cols)]
+    bal = [[i * cols + j, i * cols + j + 1] for i in range(rows) for j in range(0, cols, 2)]
+    return img, bal
+
+
+def rows_kernel(x_hbm, w1_hbm, w2_hbm, core_ref, z_ref, sems):
+    img_even = lax.axis_index("img") % 2 == 0
+    last = x_hbm.shape[0] - 2
+    core_at = jnp.where(img_even, last, 0)
+    copies = [
+        pltpu.make_async_copy(x_hbm.at[pl.ds(at, 2)], ref, sems.at[n])
+        for n, (at, ref) in enumerate(((last - core_at, z_ref), (core_at, core_ref)))
+    ]
+    for copy in copies:
         copy.start()
-        copies.append(copy)
-
-    def body(i, carry):
-        rows = pl.ds(pl.multiple_of(i * step, step), step)
-        for lane in range(0, w_ref.shape[3], lanes):
-            cols = slice(lane, lane + lanes)
-            k = [[w_ref[y, x, rows, cols].astype(F32) for x in range(3)] for y in range(3)]
-            for y, row in enumerate((k[0], [u + v + w for u, v, w in zip(*k)], k[2])):
-                for x, tap in enumerate((row[0], row[0] + row[1] + row[2], row[2])):
-                    o_ref[y, x, rows, cols] = tap.astype(BF16)
-        return carry
-
-    for part in range(parts):
-        copies[part].wait()
-        lax.fori_loop(part * depth // step, (part + 1) * depth // step, body, 0)
-
-
-def sum_taps(kernel):
+    for copy in copies:
+        copy.wait()
+
+
+def row_edges(x, w1, w2):
+    vmem = pl.BlockSpec(memory_space=pltpu.VMEM)
+    edge = jax.ShapeDtypeStruct((2,) + x.shape[1:], BF16)
     return pl.pallas_call(
-        sum_taps_kernel,
-        out_shape=jax.ShapeDtypeStruct(kernel.shape, BF16),
-        in_specs=[pl.BlockSpec(memory_space=pltpu.HBM)],
-        out_specs=pl.BlockSpec(memory_space=pltpu.VMEM),
-        scratch_shapes=[pltpu.VMEM(kernel.shape, BF16), pltpu.SemaphoreType.DMA((4,))],
-        compiler_params=pltpu.CompilerParams(vmem_limit_bytes=20 * 2**20),
-        cost_estimate=pl.CostEstimate(flops=10_000_000, bytes_accessed=13_000_000, transcendentals=0),
-        name="sum_taps",
-    )(pltpu.with_memory_space_constraint(kernel, pltpu.HBM))
+        rows_kernel,
+        out_shape=(edge, edge),
+        in_specs=[pl.BlockSpec(memory_space=pltpu.HBM)] * 3,
+        out_specs=(vmem, vmem),
+        scratch_shapes=[pltpu.SemaphoreType.DMA((2,))],
+        compiler_params=pltpu.CompilerParams(vmem_limit_bytes=4 * 2**20),
+        cost_estimate=pl.CostEstimate(flops=0, bytes_accessed=30_000_000, transcendentals=0),
+        name="row_edges",
+    )(*(pltpu.with_memory_space_constraint(a, pltpu.HBM) for a in (x, w1, w2)))
+
+
+def columns_kernel(x_ref, row_z, row_core, w1_hbm, w2_hbm, odd_ref, even_ref):
+    img_even = lax.axis_index("img") % 2 == 0
+    bal_even = lax.axis_index("bal") % 2 == 0
+    last = x_ref.shape[1]
+
+    def put(row, cells):
+        head, tail = cells[0:2], cells[last - 2 : last]
+        odd_ref[row] = jnp.where(bal_even, head, tail)
+        even_ref[row] = jnp.where(bal_even, tail, head)
+
+    for r in range(2):
+        put(r, jnp.where(img_even, row_z[r], row_core[0, r]))
+        put(r + 2 + ROWS, jnp.where(img_even, row_core[1, r], row_z[r]))
+    for r in range(ROWS):
+        put(r + 2, x_ref[r])
+
+
+def column_edges(x, row_z, row_core, w1, w2):
+    vmem = pl.BlockSpec(memory_space=pltpu.VMEM)
+    edge = jax.ShapeDtypeStruct((ROWS + 4, 2, x.shape[2]), BF16)
+    return pl.pallas_call(
+        columns_kernel,
+        out_shape=(edge, edge),
+        in_specs=[vmem] * 3 + [pl.BlockSpec(memory_space=pltpu.HBM)] * 2,
+        out_specs=(vmem, vmem),
+        compiler_params=pltpu.CompilerParams(vmem_limit_bytes=4 * 2**20),
+        cost_estimate=pl.CostEstimate(flops=0, bytes_accessed=30_000_000, transcendentals=0),
+        name="column_edges",
+    )(x, row_z, row_core, *(pltpu.with_memory_space_constraint(a, pltpu.HBM) for a in (w1, w2)))
 
 
 def block_kernel(
     full_rows,
     full_cols,
     x_ref,
-    row_even,
-    row_odd,
+    row_z,
+    row_core,
     col_odd,
     col_even,
     mean_ref,
@@ -106,6 +118,7 @@
     near,
     wide,
     done,
+    sums,
     sems,
 ):
     chan = x_ref.shape[2]
@@ -132,22 +145,17 @@
         v = cells * scale + offset
         return v * jnp.tanh(v) + v
 
-    def pick(even, even_ref, odd_ref, row):
-        a, b = even_ref[row], odd_ref[row]
-        return jnp.where(even, a, b), jnp.where(even, b, a)
-
     side = ROWS + 4
-    for r in range(side):
-        left, right = pick(bal_even, col_odd, col_even, r)
-        if r < 2:
-            mid = jnp.where(img_even, row_odd[r], row_even[r])
-        elif r < ROWS + 2:
-            mid = x_ref[r - 2]
-        else:
-            mid = jnp.where(img_even, row_even[r - 2 - ROWS], row_odd[r - 2 - ROWS])
-        act[r * PITCH : r * PITCH + 2] = left.astype(F32)
-        act[r * PITCH + 2 : r * PITCH + 2 + COLS] = mid.astype(F32)
-        act[r * PITCH + 2 + COLS : (r + 1) * PITCH] = right.astype(F32)
+    lines = [x_ref[r] for r in range(ROWS)]
+    lines = [jnp.where(img_even, row_z[r], row_core[0, r]) for r in range(2)] + lines
+    lines += [jnp.where(img_even, row_core[1, r], row_z[r]) for r in range(2)]
+    for r, line in enumerate(lines):
+        left = jnp.where(bal_even, col_odd[r], col_even[0, r])
+        right = jnp.where(bal_even, col_even[1, r], col_odd[r])
+        at = r * PITCH
+        act[at : at + 2] = left.astype(F32)
+        act[at + 2 : at + 2 + COLS] = line.astype(F32)
+        act[at + 2 + COLS : at + PITCH] = right.astype(F32)
     cell = lax.broadcasted_iota(jnp.int32, (PITCH, 1), 0)
     col = bal * COLS - 2 + cell
     col_ok = (col >= 0) & (col < full_cols)
@@ -169,12 +177,28 @@
     count = ROWS * COLS
     parts = [slice(n, n + SPLIT) for n in range(0, chan, SPLIT)]
 
-    for part in parts:
+    summed = [(0, 1), (1, 0), (1, 1), (1, 2), (2, 1)]
+
+    def sum_taps(first, stop):
+        for at in range(first, stop, STEP):
+            rows = slice(at, at + STEP)
+            for lane in range(0, chan, SPLIT):
+                cols = slice(lane, lane + SPLIT)
+                k = [[w2_ref[y, x, rows, cols].astype(F32) for x in range(3)] for y in range(3)]
+                down = [u + v + w for u, v, w in zip(*k)]
+                full = (sum(k[0]), down[0], sum(down), down[2], sum(k[2]))
+                for n, tap in enumerate(full):
+                    sums[n, rows, cols] = tap.astype(BF16)
+
+    turns = 3 * len(parts)
+    marks = [chan // STEP * turn // turns * STEP for turn in range(turns + 1)]
+    for n, part in enumerate(parts):
         h = b1_ref[:, part]
         for d in range(3):
             h = h + jnp.dot(
                 taps[d * PITCH : d * PITCH + inner], w1_ref[d, :, part], preferred_element_type=F32
             )
+            sum_taps(marks[3 * n + d], marks[3 * n + d + 1])
         hid[0:inner, part] = jnp.where(ok, h, 0.0).astype(BF16).astype(F32)
         for d in range(3):
             for r in range(ROWS + 2):
@@ -202,9 +226,11 @@
 
         def term(dy, dx):
             at = (dy * 3 + dx) * chan
-            return jnp.dot(
-                near[:, at : at + chan], w2_ref[dy, dx, :, part], preferred_element_type=F32
-            )
+            if (dy, dx) in summed:
+                w = sums[summed.index((dy, dx)), :, part]
+            else:
+                w = w2_ref[dy, dx, :, part]
+            return jnp.dot(near[:, at : at + chan], w, preferred_element_type=F32)
 
         base = term(1, 1) + b2_ref[:, part]
         by_row = [base + term(0, 1), base + term(2, 1)]
@@ -250,6 +276,7 @@
             pltpu.VMEM((count, 9 * chan), BF16),
             pltpu.VMEM((chan // LANES, 2 * ROWS, 2 * COLS, LANES), F32),
             pltpu.VMEM((2 * ROWS, 2 * COLS, chan), BF16),
+            pltpu.VMEM((5, chan, chan), BF16),
             pltpu.SemaphoreType.DMA((chan // SPLIT,)),
         ],
         compiler_params=pltpu.CompilerParams(vmem_limit_bytes=36 * 2**20),
@@ -275,21 +302,20 @@
     chan = latent.shape[2]
     full_rows = latent.shape[0] * lax.axis_size("img")
     full_cols = latent.shape[1] * lax.axis_size("bal")
-    row_odd, row_even = swap(*edges(latent, "img", 0), "img")
-    col_own = lax.optimization_barrier(edges(latent, "bal", 1))
-    img_even = lax.axis_index("img") % 2 == 0
-    above = edges(jnp.where(img_even, row_odd, row_even), "bal", 1)
-    below = edges(jnp.where(img_even, row_even, row_odd), "bal", 1)
-    col_odd, col_even = swap(
-        *(jnp.concatenate(part, axis=0) for part in zip(above, col_own, below)), "bal"
-    )
-    summed = sum_taps(conv2_kernel)
+    mesh_axes = ("img", "bal")
+    core_pairs, even_pairs = pair_groups(lax.axis_size("img"), lax.axis_size("bal"))
+    edge_core, edge_z = row_edges(latent, conv1_kernel, conv2_kernel)
+    row_z = lax.ppermute(edge_z, "img", swaps(lax.axis_size("img"), 1))
+    row_core = lax.all_gather(edge_core, mesh_axes, axis_index_groups=core_pairs)
+    edge_odd, edge_even = column_edges(latent, row_z, row_core, conv1_kernel, conv2_kernel)
+    col_odd = lax.ppermute(edge_odd, "bal", swaps(lax.axis_size("bal"), 1))
+    col_even = lax.all_gather(edge_even, mesh_axes, axis_index_groups=even_pairs)
     return run_block(
         full_rows,
         full_cols,
         latent,
-        row_even,
-        row_odd,
+        row_z,
+        row_core,
         col_odd,
         col_even,
         gn_mean.reshape(1, -1),
@@ -298,7 +324,7 @@
         gn_shift.reshape(1, chan),
         conv1_kernel.reshape(3, 3 * chan, -1),
         conv1_bias.reshape(1, -1),
-        summed,
+        conv2_kernel,
         conv2_bias.reshape(1, -1),
         tile_dest,
     )

time: 23.9 us -> 22.1 us (0.925)
  the two profiles are of different devices: /device:TPU:248 before, /device:TPU:120 now
where the time goes in v4:
time: 22.1 us; the launch traced here: 22 us
  blocking collectives  9.2 us (42%)
  starting transfers between devices  7.29 us (33%)
  Pallas kernels  5.22 us (24%)
    ppermute x1, starting transfers between devices, shards(): col_odd = lax.ppermute(edge_odd, 'bal', swaps(lax.axis_size('bal'), 1))  4.98 us
    all_gather x1, blocking collectives, shards(): lax.all_gather(edge_core, mesh_axes, axis_index_groups=core_pairs)  4.61 us
    all_gather x1, blocking collectives, shards(): lax.all_gather(edge_even, mesh_axes, axis_index_groups=even_pairs)  4.59 us
    pallas_call x1, Pallas kernels, run_block(): pl.pallas_call(functools.partial(block_kernel, full_rows, full_cols), out...  4.21 us
    ppermute x1, starting transfers between devices, shards(): row_z = lax.ppermute(edge_z, 'img', swaps(lax.axis_size('img'), 1))  2.32 us
    pallas_call x1, Pallas kernels, row_edges(): pl.pallas_call(rows_kernel, out_shape=(edge, edge), in_specs=[pl.BlockSpe...  0.96 us
  transfers between devices with their start and end apart: 2, of which 0 were waited for; matrix products, arithmetic and copies ran while one was open for 0% of the time, Pallas kernels for 0%

profile of v4, /device:TPU:120, one launch (start us, length us, event | category | flops | bytes accessed | tf_op | source)
XLA Modules:
  0.0 22.0 jit_solution(11635970127078460408)
XLA Ops:
  0.0 0.0 copy-start
  0.0 0.0 slice-start
  0.0 0.0 slice-start.2
  0.0 1.0 %row_edges.1 = (bf16[2,12,512]{2,1,0:T(8,128)(2,1)S(1)}, bf16[2,12,512]{2,1,0:T(8,128)(2,1)S(1)}) custom-call(bf16[12,12,512]{2,1,0:T(8,128)(2,1)} %x_ref.3, bf16[3,3,512,512]{3,2,1,0:T(8,128)(2,1)} %w1_hbm.3, bf16[3,3,512,512]{3,2,1,0:T(8,128)(2,1)} %w2_ref.1), custom_call_target="tpu_custom_call" | custom-call | bytes 30000000 | tf_op jit(solution)/shard_map/row_edges/pallas_call | solution.py:53
  1.0 2.3 %collective-permute-start = (bf16[2,12,512]{2,1,0:T(8,128)(2,1)S(1)}, bf16[2,12,512]{2,1,0:T(8,128)(2,1)S(1)}, u32[]{:S(2)}, u32[]{:S(2)}) collective-permute-start(bf16[2,12,512]{2,1,0:T(8,128)(2,1)S(1)} %get-tuple-element.9), channel_id=1, source_target_pairs={{16,32},{32,16},{48,64},{64,48},{80,96},{96,80},{112,128},{128,112... | collective-permute-start | bytes 73736 | tf_op jit(solution)/shard_map/ppermute | solution.py:308
  3.3 4.6 %all-gather = bf16[4,12,512]{2,1,0:T(8,128)(2,1)S(1)} all-gather(bf16[2,12,512]{2,1,0:T(8,128)(2,1)S(1)} %get-tuple-element.10), channel_id=2, replica_groups={{0,16},{1,17},{2,18},{3,19},{4,20},{5,21},{6,22},{7,23},{8,24},{9,25},{..., dimensions={0}, use_global_device_ids=true | all-gather | bytes 73728 | tf_op jit(solution)/shard_map/all_gather | solution.py:309
  7.9 0.0 collective-permute-done.row_z
  7.9 0.0 copy-done
  7.9 0.0 slice-start.1
  7.9 0.0 copy-start.1
  7.9 0.0 copy-start.2
  7.9 0.0 copy-start.3
  8.0 0.0 copy-start.4
  8.0 0.0 copy-start.5
  8.0 0.0 copy-start.6
  8.0 0.0 copy-start.7
  8.0 0.1 column_edges.1
  8.1 5.0 %collective-permute-start.1 = (bf16[16,2,512]{2,1,0:T(2,128)(2,1)S(1)}, bf16[16,2,512]{2,1,0:T(2,128)(2,1)S(1)}, u32[]{:S(2)}, u32[]{:S(2)}) collective-permute-start(bf16[16,2,512]{2,1,0:T(2,128)(2,1)S(1)} %get-tuple-element.11), channel_id=1, source_target_pairs={{1,2},{2,1},{3,4},{4,3},{5,6},{6,5},{7,8},{8,7},{9,10},{10,9},{11,... | collective-permute-start | bytes 98312 | tf_op jit(solution)/shard_map/ppermute | solution.py:311
  13.1 4.6 %all-gather.1 = bf16[32,2,512]{2,1,0:T(2,128)(2,1)S(1)} all-gather(bf16[16,2,512]{2,1,0:T(2,128)(2,1)S(1)} %get-tuple-element.12), channel_id=3, replica_groups={{0,1},{2,3},{4,5},{6,7},{8,9},{10,11},{12,13},{14,15},{16,17},{18,19},{..., dimensions={0}, use_global_device_ids=true | all-gather | bytes 98304 | tf_op jit(solution)/shard_map/all_gather | solution.py:312
  17.6 0.0 collective-permute-done.1.col_odd
  17.6 0.0 slice-done
  17.7 0.0 slice-done.2
  17.7 0.0 slice-done.1
  17.7 0.0 slice-done.3
  17.7 0.0 copy-done.1
  17.7 0.0 copy-done.2
  17.7 0.0 copy-done.3
  17.7 0.0 copy-done.4
  17.7 0.0 copy-done.5
  17.7 0.0 copy-done.6
  17.7 0.0 copy-done.7
  17.8 4.2 %decode_block.1 = bf16[24,24,512]{2,1,0:T(8,128)(2,1)} custom-call(bf16[12,12,512]{2,1,0:T(8,128)(2,1)S(1)} %copy-done, bf16[2,12,512]{2,1,0:T(8,128)(2,1)S(1)} %collective-permute-done.row_z, bf16[2,2,12,512]{3,2,1,0:T(8,128)(2,1)S(1)} %bitcast.15, bf16[16,2,512]{2,1,0:T(2,128)(2,1)S(1)} %collective-permute-done.1.col_odd, ...), custom_call_target="tpu_custom_call" | custom-call | flops 2300000000 | bytes 14000000 | tf_op jit(solution)/shard_map/decode_block/pallas_call | solution.py:266
  (3 shorter events, 0.0 us)
Async XLA Ops:
  0.0 7.9 %copy-start = (bf16[12,12,512]{2,1,0:T(8,128)(2,1)S(1)}, bf16[12,12,512]{2,1,0:T(8,128)(2,1)}, u32[]{:S(2)}) copy-start(bf16[12,12,512]{2,1,0:T(8,128)(2,1)} %x_ref.3) | copy-start | bytes 442372
  0.0 17.6 %slice-start = ((s8[4718592]{0:T(1024)(128)(4,1)}), s8[4194304]{0:T(1024)(128)(4,1)S(1)}, s32[]{:S(2)}) async-start(s8[4718592]{0:T(1024)(128)(4,1)} %bitcast.9), calls=%async_computation | async-start | bytes 8388608
  0.0 17.6 %slice-start.2 = ((s8[4718592]{0:T(1024)(128)(4,1)}), s8[4194304]{0:T(1024)(128)(4,1)S(1)}, s32[]{:S(2)}) async-start(s8[4718592]{0:T(1024)(128)(4,1)} %bitcast.12), calls=%async_computation.2 | async-start | bytes 8388608
  1.0 6.9 %collective-permute-start = (bf16[2,12,512]{2,1,0:T(8,128)(2,1)S(1)}, bf16[2,12,512]{2,1,0:T(8,128)(2,1)S(1)}, u32[]{:S(2)}, u32[]{:S(2)}) collective-permute-start(bf16[2,12,512]{2,1,0:T(8,128)(2,1)S(1)} %get-tuple-element.9), channel_id=1, source_target_pairs={{16,32},{32,16},{48,64},{64,48},{80,96},{96,80},{112,128},{128,112... | collective-permute-start | bytes 73736 | tf_op jit(solution)/shard_map/ppermute | solution.py:308
  7.9 9.7 %slice-start.1 = ((s8[4718592]{0:T(1024)(128)(4,1)}), s8[524288]{0:T(1024)(128)(4,1)S(1)}, s32[]{:S(2)}) async-start(s8[4718592]{0:T(1024)(128)(4,1)} %bitcast.9), calls=%async_computation.1 | async-start | bytes 1048576
  7.9 9.8 %slice-start.3 = ((s8[4718592]{0:T(1024)(128)(4,1)}), s8[524288]{0:T(1024)(128)(4,1)S(1)}, s32[]{:S(2)}) async-start(s8[4718592]{0:T(1024)(128)(4,1)} %bitcast.12), calls=%async_computation.3 | async-start | bytes 1048576
  7.9 9.8 %copy-start.1 = (f32[512]{0:T(512)S(1)}, f32[512]{0:T(512)}, u32[]{:S(2)}) copy-start(f32[512]{0:T(512)} %param.13) | copy-start | bytes 6148
  7.9 9.8 %copy-start.2 = (f32[512]{0:T(512)S(1)}, f32[512]{0:T(512)}, u32[]{:S(2)}) copy-start(f32[512]{0:T(512)} %param.14) | copy-start | bytes 6148
  7.9 9.8 %copy-start.3 = (f32[512]{0:T(512)S(1)}, f32[512]{0:T(512)}, u32[]{:S(2)}) copy-start(f32[512]{0:T(512)} %param.16) | copy-start | bytes 6148
  8.0 9.8 %copy-start.4 = (f32[512]{0:T(512)S(1)}, f32[512]{0:T(512)}, u32[]{:S(2)}) copy-start(f32[512]{0:T(512)} %param.18) | copy-start | bytes 6148
  8.0 9.7 %copy-start.5 = (s32[4,4]{1,0:T(4,128)S(1)}, s32[4,4]{1,0:T(4,128)}, u32[]{:S(2)}) copy-start(s32[4,4]{1,0:T(4,128)} %dest_ref.1) | copy-start | bytes 196
  8.0 9.7 %copy-start.6 = (f32[32]{0:T(128)S(1)}, f32[32]{0:T(128)}, u32[]{:S(2)}) copy-start(f32[32]{0:T(128)} %param.11) | copy-start | bytes 388
  8.0 9.7 %copy-start.7 = (f32[32]{0:T(128)S(1)}, f32[32]{0:T(128)}, u32[]{:S(2)}) copy-start(f32[32]{0:T(128)} %param.12) | copy-start | bytes 388
  8.1 9.6 %collective-permute-start.1 = (bf16[16,2,512]{2,1,0:T(2,128)(2,1)S(1)}, bf16[16,2,512]{2,1,0:T(2,128)(2,1)S(1)}, u32[]{:S(2)}, u32[]{:S(2)}) collective-permute-start(bf16[16,2,512]{2,1,0:T(2,128)(2,1)S(1)} %get-tuple-element.11), channel_id=1, source_target_pairs={{1,2},{2,1},{3,4},{4,3},{5,6},{6,5},{7,8},{8,7},{9,10},{10,9},{11,... | collective-permute-start | bytes 98312 | tf_op jit(solution)/shard_map/ppermute | solution.py:311

commit v5 on v4

--- a/solution.py
+++ b/solution.py
@@ -13,7 +13,6 @@
 ROWS = TR * TS
 COLS = TC * TS
 LANES = 128
-STEP = 16
 SPLIT = 256
 PITCH = 16
 F32 = jnp.float32
@@ -114,11 +113,9 @@
     act,
     taps,
     hid,
-    packed,
     near,
     wide,
     done,
-    sums,
     sems,
 ):
     chan = x_ref.shape[2]
@@ -174,46 +171,19 @@
     row = img * ROWS - 1 + cell // PITCH
     col = bal * COLS - 1 + cell % PITCH
     ok = (row >= 0) & (row < full_rows) & (col >= 0) & (col < full_cols)
-    count = ROWS * COLS
     parts = [slice(n, n + SPLIT) for n in range(0, chan, SPLIT)]
 
-    summed = [(0, 1), (1, 0), (1, 1), (1, 2), (2, 1)]
-
-    def sum_taps(first, stop):
-        for at in range(first, stop, STEP):
-            rows = slice(at, at + STEP)
-            for lane in range(0, chan, SPLIT):
-                cols = slice(lane, lane + SPLIT)
-                k = [[w2_ref[y, x, rows, cols].astype(F32) for x in range(3)] for y in range(3)]
-                down = [u + v + w for u, v, w in zip(*k)]
-                full = (sum(k[0]), down[0], sum(down), down[2], sum(k[2]))
-                for n, tap in enumerate(full):
-                    sums[n, rows, cols] = tap.astype(BF16)
-
-    turns = 3 * len(parts)
-    marks = [chan // STEP * turn // turns * STEP for turn in range(turns + 1)]
-    for n, part in enumerate(parts):
+    for part in parts:
         h = b1_ref[:, part]
-        for d in range(3):
-            h = h + jnp.dot(
-                taps[d * PITCH : d * PITCH + inner], w1_ref[d, :, part], preferred_element_type=F32
-            )
-            sum_taps(marks[3 * n + d], marks[3 * n + d + 1])
-        hid[0:inner, part] = jnp.where(ok, h, 0.0).astype(BF16).astype(F32)
-        for d in range(3):
-            for r in range(ROWS + 2):
-                at = r * PITCH + d
-                packed[d, r * COLS : (r + 1) * COLS, part] = hid[at : at + COLS, part]
-        packed[0, :, part] = packed[0, :, part] - packed[1, :, part]
-        packed[2, :, part] = packed[2, :, part] - packed[1, :, part]
-        for dx in range(3):
-            here = packed[dx, COLS : COLS + count, part]
-            for dy in range(3):
-                at = (dy * 3 + dx) * chan + part.start
-                cells = here
-                if dy != 1:
-                    cells = packed[dx, dy * COLS : dy * COLS + count, part] - here
-                near[:, at : at + SPLIT] = cells.astype(BF16)
+        for e in range(3):
+            lane = slice(e * chan, (e + 1) * chan)
+            for d in range(3):
+                h = h + jnp.dot(
+                    taps[d * PITCH : d * PITCH + inner, lane],
+                    w1_ref[d, lane, part],
+                    preferred_element_type=F32,
+                )
+        hid[:, part] = jnp.where(ok, h, 0.0).astype(BF16)
 
     cell = lax.broadcasted_iota(jnp.int32, (2 * COLS, TC), 0)
     own = cell // (2 * TS) == lax.broadcasted_iota(jnp.int32, (2 * COLS, TC), 1)
@@ -224,26 +194,34 @@
     copies = []
     for n, part in enumerate(parts):
 
-        def term(dy, dx):
-            at = (dy * 3 + dx) * chan
-            if (dy, dx) in summed:
-                w = sums[summed.index((dy, dx)), :, part]
-            else:
-                w = w2_ref[dy, dx, :, part]
-            return jnp.dot(near[:, at : at + chan], w, preferred_element_type=F32)
-
-        base = term(1, 1) + b2_ref[:, part]
-        by_row = [base + term(0, 1), base + term(2, 1)]
         lanes = range(part.start // LANES, part.stop // LANES)
-        for q in range(2):
-            by_col = term(1, 2 * q)
-            for p in range(2):
-                z = by_row[p] + by_col + term(2 * p, 2 * q)
-                for r in range(ROWS):
-                    for k in lanes:
-                        at = k * LANES - part.start
+        span = ROWS * PITCH
+        by_row = [[], []]
+        for dx in range(3):
+            first, mid, last = [
+                jnp.dot(hid[...], w2_ref[dy, dx, :, part], preferred_element_type=F32)
+                for dy in range(3)
+            ]
+            here = slice(PITCH, PITCH + span)
+            by_row[0].append(first[:span] + (mid[here] + last[here]))
+            by_row[1].append((first[here] + mid[here]) + last[2 * PITCH :])
+        bias = b2_ref[:, part]
+        for p in range(2):
+            left, mid, right = by_row[p]
+            mid = mid + bias
+            near[0, :span] = mid + right
+            near[1, :span] = mid + left
+            near[2, :span] = right
+            for r in range(ROWS):
+                at = r * PITCH
+                zs = (
+                    left[at : at + COLS] + near[0, at + 1 : at + 1 + COLS],
+                    near[1, at + 1 : at + 1 + COLS] + near[2, at + 2 : at + 2 + COLS],
+                )
+                for q, z in enumerate(zs):
+                    for n_lane, k in enumerate(lanes):
                         wide[k, 2 * r + p, pl.ds(q, COLS, stride=2)] = z[
-                            r * COLS : (r + 1) * COLS, at : at + LANES
+                            :, n_lane * LANES : (n_lane + 1) * LANES
                         ]
         for r in range(2 * ROWS):
             for k in lanes:
@@ -262,7 +240,6 @@
     vmem = pl.BlockSpec(memory_space=pltpu.VMEM)
     side = ROWS + 4
     inner = (ROWS + 2) * PITCH
-    count = ROWS * COLS
     return pl.pallas_call(
         functools.partial(block_kernel, full_rows, full_cols),
         out_shape=jax.ShapeDtypeStruct((2 * ROWS, 2 * COLS, chan), BF16),
@@ -271,12 +248,10 @@
         scratch_shapes=[
             pltpu.VMEM((side * PITCH + 8, chan), F32),
             pltpu.VMEM((side * PITCH, 3 * chan), BF16),
-            pltpu.VMEM((inner + 8, chan), F32),
-            pltpu.VMEM((3, (ROWS + 2) * COLS, chan), F32),
-            pltpu.VMEM((count, 9 * chan), BF16),
+            pltpu.VMEM((inner, chan), BF16),
+            pltpu.VMEM((3, ROWS * PITCH + 8, SPLIT), F32),
             pltpu.VMEM((chan // LANES, 2 * ROWS, 2 * COLS, LANES), F32),
             pltpu.VMEM((2 * ROWS, 2 * COLS, chan), BF16),
-            pltpu.VMEM((5, chan, chan), BF16),
             pltpu.SemaphoreType.DMA((chan // SPLIT,)),
         ],
         compiler_params=pltpu.CompilerParams(vmem_limit_bytes=36 * 2**20),

time: 22.1 us -> 21.7 us (0.982)
  Pallas kernels: 5.22 us -> 4.84 us
    pallas_call x1, Pallas kernels: 4.21 us -> 3.83 us  [run_block(): pl.pallas_call(functools.partial(block_kernel, full_rows, full_cols), out...]
where the time goes in v5:
time: 21.7 us; the launch traced here: 21.6 us
  blocking collectives  9.2 us (42%)
  starting transfers between devices  7.29 us (34%)
  Pallas kernels  4.84 us (22%)
    ppermute x1, starting transfers between devices, shards(): col_odd = lax.ppermute(edge_odd, 'bal', swaps(lax.axis_size('bal'), 1))  4.98 us
    all_gather x1, blocking collectives, shards(): lax.all_gather(edge_core, mesh_axes, axis_index_groups=core_pairs)  4.61 us
    all_gather x1, blocking collectives, shards(): lax.all_gather(edge_even, mesh_axes, axis_index_groups=even_pairs)  4.59 us
    pallas_call x1, Pallas kernels, run_block(): pl.pallas_call(functools.partial(block_kernel, full_rows, full_cols), out...  3.83 us
    ppermute x1, starting transfers between devices, shards(): row_z = lax.ppermute(edge_z, 'img', swaps(lax.axis_size('img'), 1))  2.32 us
    pallas_call x1, Pallas kernels, row_edges(): pl.pallas_call(rows_kernel, out_shape=(edge, edge), in_specs=[pl.BlockSpe...  0.96 us
  transfers between devices with their start and end apart: 2, of which 0 were waited for; matrix products, arithmetic and copies ran while one was open for 0% of the time, Pallas kernels for 0%

profile of v5, /device:TPU:120, one launch (start us, length us, event | category | flops | bytes accessed | tf_op | source)
XLA Modules:
  0.0 21.6 jit_solution(6993621172908962386)
XLA Ops:
  0.0 0.0 copy-start
  0.0 0.0 slice-start
  0.0 0.0 slice-start.2
  0.0 1.0 %row_edges.1 = (bf16[2,12,512]{2,1,0:T(8,128)(2,1)S(1)}, bf16[2,12,512]{2,1,0:T(8,128)(2,1)S(1)}) custom-call(bf16[12,12,512]{2,1,0:T(8,128)(2,1)} %x_ref.3, bf16[3,3,512,512]{3,2,1,0:T(8,128)(2,1)} %w1_hbm.3, bf16[3,3,512,512]{3,2,1,0:T(8,128)(2,1)} %w2_ref.1), custom_call_target="tpu_custom_call" | custom-call | bytes 30000000 | tf_op jit(solution)/shard_map/row_edges/pallas_call | solution.py:52
  1.0 2.3 %collective-permute-start = (bf16[2,12,512]{2,1,0:T(8,128)(2,1)S(1)}, bf16[2,12,512]{2,1,0:T(8,128)(2,1)S(1)}, u32[]{:S(2)}, u32[]{:S(2)}) collective-permute-start(bf16[2,12,512]{2,1,0:T(8,128)(2,1)S(1)} %get-tuple-element.9), channel_id=1, source_target_pairs={{16,32},{32,16},{48,64},{64,48},{80,96},{96,80},{112,128},{128,112... | collective-permute-start | bytes 73736 | tf_op jit(solution)/shard_map/ppermute | solution.py:283
  3.3 4.6 %all-gather = bf16[4,12,512]{2,1,0:T(8,128)(2,1)S(1)} all-gather(bf16[2,12,512]{2,1,0:T(8,128)(2,1)S(1)} %get-tuple-element.10), channel_id=2, replica_groups={{0,16},{1,17},{2,18},{3,19},{4,20},{5,21},{6,22},{7,23},{8,24},{9,25},{..., dimensions={0}, use_global_device_ids=true | all-gather | bytes 73728 | tf_op jit(solution)/shard_map/all_gather | solution.py:284
  7.9 0.0 collective-permute-done.row_z
  7.9 0.0 copy-done
  7.9 0.0 slice-start.1
  7.9 0.0 copy-start.1
  7.9 0.0 copy-start.2
  7.9 0.0 copy-start.3
  8.0 0.0 copy-start.4
  8.0 0.0 copy-start.5
  8.0 0.0 copy-start.6
  8.0 0.0 copy-start.7
  8.0 0.1 column_edges.1
  8.1 5.0 %collective-permute-start.1 = (bf16[16,2,512]{2,1,0:T(2,128)(2,1)S(1)}, bf16[16,2,512]{2,1,0:T(2,128)(2,1)S(1)}, u32[]{:S(2)}, u32[]{:S(2)}) collective-permute-start(bf16[16,2,512]{2,1,0:T(2,128)(2,1)S(1)} %get-tuple-element.11), channel_id=1, source_target_pairs={{1,2},{2,1},{3,4},{4,3},{5,6},{6,5},{7,8},{8,7},{9,10},{10,9},{11,... | collective-permute-start | bytes 98312 | tf_op jit(solution)/shard_map/ppermute | solution.py:286
  13.1 4.6 %all-gather.1 = bf16[32,2,512]{2,1,0:T(2,128)(2,1)S(1)} all-gather(bf16[16,2,512]{2,1,0:T(2,128)(2,1)S(1)} %get-tuple-element.12), channel_id=3, replica_groups={{0,1},{2,3},{4,5},{6,7},{8,9},{10,11},{12,13},{14,15},{16,17},{18,19},{..., dimensions={0}, use_global_device_ids=true | all-gather | bytes 98304 | tf_op jit(solution)/shard_map/all_gather | solution.py:287
  17.6 0.0 collective-permute-done.1.col_odd
  17.6 0.0 slice-done
  17.7 0.0 slice-done.2
  17.7 0.0 slice-done.1
  17.7 0.0 slice-done.3
  17.7 0.0 copy-done.1
  17.7 0.0 copy-done.2
  17.7 0.0 copy-done.3
  17.7 0.0 copy-done.4
  17.7 0.0 copy-done.5
  17.7 0.0 copy-done.6
  17.7 0.0 copy-done.7
  17.8 3.8 %decode_block.1 = bf16[24,24,512]{2,1,0:T(8,128)(2,1)} custom-call(bf16[12,12,512]{2,1,0:T(8,128)(2,1)S(1)} %copy-done, bf16[2,12,512]{2,1,0:T(8,128)(2,1)S(1)} %collective-permute-done.row_z, bf16[2,2,12,512]{3,2,1,0:T(8,128)(2,1)S(1)} %bitcast.15, bf16[16,2,512]{2,1,0:T(2,128)(2,1)S(1)} %collective-permute-done.1.col_odd, ...), custom_call_target="tpu_custom_call" | custom-call | flops 2300000000 | bytes 14000000 | tf_op jit(solution)/shard_map/decode_block/pallas_call | solution.py:243
  (3 shorter events, 0.0 us)
Async XLA Ops:
  0.0 7.9 %copy-start = (bf16[12,12,512]{2,1,0:T(8,128)(2,1)S(1)}, bf16[12,12,512]{2,1,0:T(8,128)(2,1)}, u32[]{:S(2)}) copy-start(bf16[12,12,512]{2,1,0:T(8,128)(2,1)} %x_ref.3) | copy-start | bytes 442372
  0.0 17.6 %slice-start = ((s8[4718592]{0:T(1024)(128)(4,1)}), s8[4194304]{0:T(1024)(128)(4,1)S(1)}, s32[]{:S(2)}) async-start(s8[4718592]{0:T(1024)(128)(4,1)} %bitcast.9), calls=%async_computation | async-start | bytes 8388608
  0.0 17.6 %slice-start.2 = ((s8[4718592]{0:T(1024)(128)(4,1)}), s8[4194304]{0:T(1024)(128)(4,1)S(1)}, s32[]{:S(2)}) async-start(s8[4718592]{0:T(1024)(128)(4,1)} %bitcast.12), calls=%async_computation.2 | async-start | bytes 8388608
  1.0 6.9 %collective-permute-start = (bf16[2,12,512]{2,1,0:T(8,128)(2,1)S(1)}, bf16[2,12,512]{2,1,0:T(8,128)(2,1)S(1)}, u32[]{:S(2)}, u32[]{:S(2)}) collective-permute-start(bf16[2,12,512]{2,1,0:T(8,128)(2,1)S(1)} %get-tuple-element.9), channel_id=1, source_target_pairs={{16,32},{32,16},{48,64},{64,48},{80,96},{96,80},{112,128},{128,112... | collective-permute-start | bytes 73736 | tf_op jit(solution)/shard_map/ppermute | solution.py:283
  7.9 9.7 %slice-start.1 = ((s8[4718592]{0:T(1024)(128)(4,1)}), s8[524288]{0:T(1024)(128)(4,1)S(1)}, s32[]{:S(2)}) async-start(s8[4718592]{0:T(1024)(128)(4,1)} %bitcast.9), calls=%async_computation.1 | async-start | bytes 1048576
  7.9 9.8 %slice-start.3 = ((s8[4718592]{0:T(1024)(128)(4,1)}), s8[524288]{0:T(1024)(128)(4,1)S(1)}, s32[]{:S(2)}) async-start(s8[4718592]{0:T(1024)(128)(4,1)} %bitcast.12), calls=%async_computation.3 | async-start | bytes 1048576
  7.9 9.8 %copy-start.1 = (f32[512]{0:T(512)S(1)}, f32[512]{0:T(512)}, u32[]{:S(2)}) copy-start(f32[512]{0:T(512)} %param.13) | copy-start | bytes 6148
  7.9 9.8 %copy-start.2 = (f32[512]{0:T(512)S(1)}, f32[512]{0:T(512)}, u32[]{:S(2)}) copy-start(f32[512]{0:T(512)} %param.14) | copy-start | bytes 6148
  7.9 9.8 %copy-start.3 = (f32[512]{0:T(512)S(1)}, f32[512]{0:T(512)}, u32[]{:S(2)}) copy-start(f32[512]{0:T(512)} %param.16) | copy-start | bytes 6148
  8.0 9.8 %copy-start.4 = (f32[512]{0:T(512)S(1)}, f32[512]{0:T(512)}, u32[]{:S(2)}) copy-start(f32[512]{0:T(512)} %param.18) | copy-start | bytes 6148
  8.0 9.7 %copy-start.5 = (s32[4,4]{1,0:T(4,128)S(1)}, s32[4,4]{1,0:T(4,128)}, u32[]{:S(2)}) copy-start(s32[4,4]{1,0:T(4,128)} %dest_ref.1) | copy-start | bytes 196
  8.0 9.7 %copy-start.6 = (f32[32]{0:T(128)S(1)}, f32[32]{0:T(128)}, u32[]{:S(2)}) copy-start(f32[32]{0:T(128)} %param.11) | copy-start | bytes 388
  8.0 9.7 %copy-start.7 = (f32[32]{0:T(128)S(1)}, f32[32]{0:T(128)}, u32[]{:S(2)}) copy-start(f32[32]{0:T(128)} %param.12) | copy-start | bytes 388
  8.1 9.6 %collective-permute-start.1 = (bf16[16,2,512]{2,1,0:T(2,128)(2,1)S(1)}, bf16[16,2,512]{2,1,0:T(2,128)(2,1)S(1)}, u32[]{:S(2)}, u32[]{:S(2)}) collective-permute-start(bf16[16,2,512]{2,1,0:T(2,128)(2,1)S(1)} %get-tuple-element.11), channel_id=1, source_target_pairs={{1,2},{2,1},{3,4},{4,3},{5,6},{6,5},{7,8},{8,7},{9,10},{10,9},{11,... | collective-permute-start | bytes 98312 | tf_op jit(solution)/shard_map/ppermute | solution.py:286

commit v6 on v5

--- a/solution.py
+++ b/solution.py
@@ -14,6 +14,7 @@
 COLS = TC * TS
 LANES = 128
 SPLIT = 256
+MARGIN = 8
 PITCH = 16
 F32 = jnp.float32
 BF16 = jnp.bfloat16
@@ -113,7 +114,6 @@
     act,
     taps,
     hid,
-    near,
     wide,
     done,
     sems,
@@ -163,8 +163,11 @@
         act[at] = jnp.where(ok, activate(act[at]), 0.0)
     total = side * PITCH
     act[total:] = jnp.zeros((act.shape[0] - total, chan), F32)
-    for d in range(3):
+
+    def shift(d):
         taps[:, d * chan : (d + 1) * chan] = act[d : d + total].astype(BF16)
+
+    shift(0)
 
     inner = (ROWS + 2) * PITCH
     cell = lax.broadcasted_iota(jnp.int32, (inner, 1), 0)
@@ -183,6 +186,8 @@
                     w1_ref[d, lane, part],
                     preferred_element_type=F32,
                 )
+                if part.start == 0 and d == 0 and e < 2:
+                    shift(e + 1)
         hid[:, part] = jnp.where(ok, h, 0.0).astype(BF16)
 
     cell = lax.broadcasted_iota(jnp.int32, (2 * COLS, TC), 0)
@@ -191,46 +196,55 @@
         jnp.max(jnp.where(own, dest_ref[i : i + 1], -1), axis=1, keepdims=True) >= 0
         for i in range(TR)
     ]
-    copies = []
-    for n, part in enumerate(parts):
-
+    span = ROWS * PITCH
+    met = ((0, PITCH + span), (PITCH, PITCH + span), (PITCH, 2 * PITCH + span))
+
+    def finish(n, part, by_row):
         lanes = range(part.start // LANES, part.stop // LANES)
-        span = ROWS * PITCH
-        by_row = [[], []]
-        for dx in range(3):
-            first, mid, last = [
-                jnp.dot(hid[...], w2_ref[dy, dx, :, part], preferred_element_type=F32)
-                for dy in range(3)
-            ]
-            here = slice(PITCH, PITCH + span)
-            by_row[0].append(first[:span] + (mid[here] + last[here]))
-            by_row[1].append((first[here] + mid[here]) + last[2 * PITCH :])
         bias = b2_ref[:, part]
+
+        def row(p, r, sums):
+            for m, (q, shift) in enumerate(((0, 0), (0, 1), (1, 1), (1, 2))):
+                cells = sums[m][r * PITCH : (r + 1) * PITCH]
+                at = pl.ds(MARGIN - 2 * shift + q, PITCH, stride=2)
+                for lane, k in enumerate(lanes):
+                    wide[m % 2, k, 2 * r + p, at] = cells[:, lane * LANES : (lane + 1) * LANES]
+            for k in lanes:
+                cells = wide[0, k, 2 * r + p, within] + wide[1, k, 2 * r + p, within]
+                lane = slice(k * LANES, (k + 1) * LANES)
+                done[2 * r + p, :, lane] = jnp.where(live[r // TS], cells, 0.0).astype(BF16)
+
+        within = slice(MARGIN, MARGIN + 2 * COLS)
         for p in range(2):
             left, mid, right = by_row[p]
             mid = mid + bias
-            near[0, :span] = mid + right
-            near[1, :span] = mid + left
-            near[2, :span] = right
+            sums = (left, mid + right, mid + left, right)
             for r in range(ROWS):
-                at = r * PITCH
-                zs = (
-                    left[at : at + COLS] + near[0, at + 1 : at + 1 + COLS],
-                    near[1, at + 1 : at + 1 + COLS] + near[2, at + 2 : at + 2 + COLS],
-                )
-                for q, z in enumerate(zs):
-                    for n_lane, k in enumerate(lanes):
-                        wide[k, 2 * r + p, pl.ds(q, COLS, stride=2)] = z[
-                            :, n_lane * LANES : (n_lane + 1) * LANES
-                        ]
-        for r in range(2 * ROWS):
-            for k in lanes:
-                lane = slice(k * LANES, (k + 1) * LANES)
-                kept = jnp.where(live[r // (2 * TS)], wide[k, r], 0.0)
-                done[r, :, lane] = kept.astype(BF16)
+                yield functools.partial(row, p, r, sums)
+
+    copies = []
+
+    def send(n, part):
         copy = pltpu.make_async_copy(done.at[:, :, part], o_ref.at[:, :, part], sems.at[n])
         copy.start()
         copies.append(copy)
+
+    steps = []
+    for n, part in enumerate(parts):
+        terms = {}
+        turns = 9
+        for turn in range(turns):
+            dx, dy = divmod(turn, 3)
+            a, b = met[dy]
+            terms[dy, dx] = jnp.dot(hid[a:b], w2_ref[dy, dx, :, part], preferred_element_type=F32)
+        by_row = [[], []]
+        for dx in range(3):
+            first, mid, last = (terms[dy, dx] for dy in range(3))
+            by_row[0].append(first[:span] + (mid + last[:span]))
+            by_row[1].append((first[PITCH:] + mid) + last[PITCH:])
+        for step in finish(n, part, by_row):
+            step()
+        send(n, part)
     for copy in copies:
         copy.wait()
 
@@ -249,8 +263,7 @@
             pltpu.VMEM((side * PITCH + 8, chan), F32),
             pltpu.VMEM((side * PITCH, 3 * chan), BF16),
             pltpu.VMEM((inner, chan), BF16),
-            pltpu.VMEM((3, ROWS * PITCH + 8, SPLIT), F32),
-            pltpu.VMEM((chan // LANES, 2 * ROWS, 2 * COLS, LANES), F32),
+            pltpu.VMEM((2, chan // LANES, 2 * ROWS, MARGIN + 2 * PITCH, LANES), F32),
             pltpu.VMEM((2 * ROWS, 2 * COLS, chan), BF16),
             pltpu.SemaphoreType.DMA((chan // SPLIT,)),
         ],

time: 21.7 us -> 21.6 us (level)
  the two profiles are of different devices: /device:TPU:120 before, /device:TPU:248 now
where the time goes in v6:
time: 21.6 us; the launch traced here: 21.4 us
  blocking collectives  9.2 us (43%)
  starting transfers between devices  7.29 us (34%)
  Pallas kernels  4.67 us (22%)
    ppermute x1, starting transfers between devices, shards(): col_odd = lax.ppermute(edge_odd, 'bal', swaps(lax.axis_size('bal'), 1))  4.98 us
    all_gather x1, blocking collectives, shards(): lax.all_gather(edge_core, mesh_axes, axis_index_groups=core_pairs)  4.61 us
    all_gather x1, blocking collectives, shards(): lax.all_gather(edge_even, mesh_axes, axis_index_groups=even_pairs)  4.59 us
    pallas_call x1, Pallas kernels, run_block(): pl.pallas_call(functools.partial(block_kernel, full_rows, full_cols), out...  3.66 us
    ppermute x1, starting transfers between devices, shards(): row_z = lax.ppermute(edge_z, 'img', swaps(lax.axis_size('img'), 1))  2.32 us
    pallas_call x1, Pallas kernels, row_edges(): pl.pallas_call(rows_kernel, out_shape=(edge, edge), in_specs=[pl.BlockSpe...  0.96 us
  transfers between devices with their start and end apart: 2, of which 0 were waited for; matrix products, arithmetic and copies ran while one was open for 0% of the time, Pallas kernels for 0%

profile of v6, /device:TPU:248, one launch (start us, length us, event | category | flops | bytes accessed | tf_op | source)
XLA Modules:
  0.0 21.4 jit_solution(8502620613942528938)
XLA Ops:
  0.0 0.0 copy-start
  0.0 0.0 slice-start
  0.0 0.0 slice-start.2
  0.0 1.0 %row_edges.1 = (bf16[2,12,512]{2,1,0:T(8,128)(2,1)S(1)}, bf16[2,12,512]{2,1,0:T(8,128)(2,1)S(1)}) custom-call(bf16[12,12,512]{2,1,0:T(8,128)(2,1)} %x_ref.3, bf16[3,3,512,512]{3,2,1,0:T(8,128)(2,1)} %w1_hbm.3, bf16[3,3,512,512]{3,2,1,0:T(8,128)(2,1)} %w2_ref.1), custom_call_target="tpu_custom_call" | custom-call | bytes 30000000 | tf_op jit(solution)/shard_map/row_edges/pallas_call | solution.py:53
  1.0 2.3 %collective-permute-start = (bf16[2,12,512]{2,1,0:T(8,128)(2,1)S(1)}, bf16[2,12,512]{2,1,0:T(8,128)(2,1)S(1)}, u32[]{:S(2)}, u32[]{:S(2)}) collective-permute-start(bf16[2,12,512]{2,1,0:T(8,128)(2,1)S(1)} %get-tuple-element.9), channel_id=1, source_target_pairs={{16,32},{32,16},{48,64},{64,48},{80,96},{96,80},{112,128},{128,112... | collective-permute-start | bytes 73736 | tf_op jit(solution)/shard_map/ppermute | solution.py:296
  3.3 4.6 %all-gather = bf16[4,12,512]{2,1,0:T(8,128)(2,1)S(1)} all-gather(bf16[2,12,512]{2,1,0:T(8,128)(2,1)S(1)} %get-tuple-element.10), channel_id=2, replica_groups={{0,16},{1,17},{2,18},{3,19},{4,20},{5,21},{6,22},{7,23},{8,24},{9,25},{..., dimensions={0}, use_global_device_ids=true | all-gather | bytes 73728 | tf_op jit(solution)/shard_map/all_gather | solution.py:297
  7.9 0.0 collective-permute-done.row_z
  7.9 0.0 copy-done
  7.9 0.0 slice-start.1
  7.9 0.0 copy-start.1
  7.9 0.0 copy-start.2
  7.9 0.0 copy-start.3
  8.0 0.0 copy-start.4
  8.0 0.0 copy-start.5
  8.0 0.0 copy-start.6
  8.0 0.0 copy-start.7
  8.0 0.1 column_edges.1
  8.1 5.0 %collective-permute-start.1 = (bf16[16,2,512]{2,1,0:T(2,128)(2,1)S(1)}, bf16[16,2,512]{2,1,0:T(2,128)(2,1)S(1)}, u32[]{:S(2)}, u32[]{:S(2)}) collective-permute-start(bf16[16,2,512]{2,1,0:T(2,128)(2,1)S(1)} %get-tuple-element.11), channel_id=1, source_target_pairs={{1,2},{2,1},{3,4},{4,3},{5,6},{6,5},{7,8},{8,7},{9,10},{10,9},{11,... | collective-permute-start | bytes 98312 | tf_op jit(solution)/shard_map/ppermute | solution.py:299
  13.1 4.6 %all-gather.1 = bf16[32,2,512]{2,1,0:T(2,128)(2,1)S(1)} all-gather(bf16[16,2,512]{2,1,0:T(2,128)(2,1)S(1)} %get-tuple-element.12), channel_id=3, replica_groups={{0,1},{2,3},{4,5},{6,7},{8,9},{10,11},{12,13},{14,15},{16,17},{18,19},{..., dimensions={0}, use_global_device_ids=true | all-gather | bytes 98304 | tf_op jit(solution)/shard_map/all_gather | solution.py:300
  17.6 0.0 collective-permute-done.1.col_odd
  17.6 0.0 slice-done
  17.7 0.0 slice-done.2
  17.7 0.0 slice-done.1
  17.7 0.0 slice-done.3
  17.7 0.0 copy-done.1
  17.7 0.0 copy-done.2
  17.7 0.0 copy-done.3
  17.7 0.0 copy-done.4
  17.7 0.0 copy-done.5
  17.7 0.0 copy-done.6
  17.7 0.0 copy-done.7
  17.8 3.7 %decode_block.1 = bf16[24,24,512]{2,1,0:T(8,128)(2,1)} custom-call(bf16[12,12,512]{2,1,0:T(8,128)(2,1)S(1)} %copy-done, bf16[2,12,512]{2,1,0:T(8,128)(2,1)S(1)} %collective-permute-done.row_z, bf16[2,2,12,512]{3,2,1,0:T(8,128)(2,1)S(1)} %bitcast.15, bf16[16,2,512]{2,1,0:T(2,128)(2,1)S(1)} %collective-permute-done.1.col_odd, ...), custom_call_target="tpu_custom_call" | custom-call | flops 2300000000 | bytes 14000000 | tf_op jit(solution)/shard_map/decode_block/pallas_call | solution.py:257
  (3 shorter events, 0.0 us)
Async XLA Ops:
  0.0 7.9 %copy-start = (bf16[12,12,512]{2,1,0:T(8,128)(2,1)S(1)}, bf16[12,12,512]{2,1,0:T(8,128)(2,1)}, u32[]{:S(2)}) copy-start(bf16[12,12,512]{2,1,0:T(8,128)(2,1)} %x_ref.3) | copy-start | bytes 442372
  0.0 17.6 %slice-start = ((s8[4718592]{0:T(1024)(128)(4,1)}), s8[4194304]{0:T(1024)(128)(4,1)S(1)}, s32[]{:S(2)}) async-start(s8[4718592]{0:T(1024)(128)(4,1)} %bitcast.9), calls=%async_computation | async-start | bytes 8388608
  0.0 17.6 %slice-start.2 = ((s8[4718592]{0:T(1024)(128)(4,1)}), s8[4194304]{0:T(1024)(128)(4,1)S(1)}, s32[]{:S(2)}) async-start(s8[4718592]{0:T(1024)(128)(4,1)} %bitcast.12), calls=%async_computation.2 | async-start | bytes 8388608
  1.0 6.9 %collective-permute-start = (bf16[2,12,512]{2,1,0:T(8,128)(2,1)S(1)}, bf16[2,12,512]{2,1,0:T(8,128)(2,1)S(1)}, u32[]{:S(2)}, u32[]{:S(2)}) collective-permute-start(bf16[2,12,512]{2,1,0:T(8,128)(2,1)S(1)} %get-tuple-element.9), channel_id=1, source_target_pairs={{16,32},{32,16},{48,64},{64,48},{80,96},{96,80},{112,128},{128,112... | collective-permute-start | bytes 73736 | tf_op jit(solution)/shard_map/ppermute | solution.py:296
  7.9 9.7 %slice-start.1 = ((s8[4718592]{0:T(1024)(128)(4,1)}), s8[524288]{0:T(1024)(128)(4,1)S(1)}, s32[]{:S(2)}) async-start(s8[4718592]{0:T(1024)(128)(4,1)} %bitcast.9), calls=%async_computation.1 | async-start | bytes 1048576
  7.9 9.8 %slice-start.3 = ((s8[4718592]{0:T(1024)(128)(4,1)}), s8[524288]{0:T(1024)(128)(4,1)S(1)}, s32[]{:S(2)}) async-start(s8[4718592]{0:T(1024)(128)(4,1)} %bitcast.12), calls=%async_computation.3 | async-start | bytes 1048576
  7.9 9.8 %copy-start.1 = (f32[512]{0:T(512)S(1)}, f32[512]{0:T(512)}, u32[]{:S(2)}) copy-start(f32[512]{0:T(512)} %param.13) | copy-start | bytes 6148
  7.9 9.8 %copy-start.2 = (f32[512]{0:T(512)S(1)}, f32[512]{0:T(512)}, u32[]{:S(2)}) copy-start(f32[512]{0:T(512)} %param.14) | copy-start | bytes 6148
  7.9 9.8 %copy-start.3 = (f32[512]{0:T(512)S(1)}, f32[512]{0:T(512)}, u32[]{:S(2)}) copy-start(f32[512]{0:T(512)} %param.16) | copy-start | bytes 6148
  8.0 9.8 %copy-start.4 = (f32[512]{0:T(512)S(1)}, f32[512]{0:T(512)}, u32[]{:S(2)}) copy-start(f32[512]{0:T(512)} %param.18) | copy-start | bytes 6148
  8.0 9.7 %copy-start.5 = (s32[4,4]{1,0:T(4,128)S(1)}, s32[4,4]{1,0:T(4,128)}, u32[]{:S(2)}) copy-start(s32[4,4]{1,0:T(4,128)} %dest_ref.1) | copy-start | bytes 196
  8.0 9.7 %copy-start.6 = (f32[32]{0:T(128)S(1)}, f32[32]{0:T(128)}, u32[]{:S(2)}) copy-start(f32[32]{0:T(128)} %param.11) | copy-start | bytes 388
  8.0 9.7 %copy-start.7 = (f32[32]{0:T(128)S(1)}, f32[32]{0:T(128)}, u32[]{:S(2)}) copy-start(f32[32]{0:T(128)} %param.12) | copy-start | bytes 388
  8.1 9.6 %collective-permute-start.1 = (bf16[16,2,512]{2,1,0:T(2,128)(2,1)S(1)}, bf16[16,2,512]{2,1,0:T(2,128)(2,1)S(1)}, u32[]{:S(2)}, u32[]{:S(2)}) collective-permute-start(bf16[16,2,512]{2,1,0:T(2,128)(2,1)S(1)} %get-tuple-element.11), channel_id=1, source_target_pairs={{1,2},{2,1},{3,4},{4,3},{5,6},{6,5},{7,8},{8,7},{9,10},{10,9},{11,... | collective-permute-start | bytes 98312 | tf_op jit(solution)/shard_map/ppermute | solution.py:299

commit v7 on v6

--- a/solution.py
+++ b/solution.py
@@ -33,13 +33,18 @@
     return img, bal
 
 
-def rows_kernel(x_hbm, w1_hbm, w2_hbm, core_ref, z_ref, sems):
+def rows_kernel(x_hbm, core_ref, z_ref, sems):
     img_even = lax.axis_index("img") % 2 == 0
     last = x_hbm.shape[0] - 2
     core_at = jnp.where(img_even, last, 0)
     copies = [
-        pltpu.make_async_copy(x_hbm.at[pl.ds(at, 2)], ref, sems.at[n])
-        for n, (at, ref) in enumerate(((last - core_at, z_ref), (core_at, core_ref)))
+        pltpu.make_async_copy(source, ref, sems.at[n])
+        for n, (source, ref) in enumerate(
+            (
+                (x_hbm.at[pl.ds(last - core_at, 2)], z_ref),
+                (x_hbm.at[pl.ds(core_at, 2)], core_ref),
+            )
+        )
     ]
     for copy in copies:
         copy.start()
@@ -47,22 +52,38 @@
         copy.wait()
 
 
-def row_edges(x, w1, w2):
+def row_edges(x):
     vmem = pl.BlockSpec(memory_space=pltpu.VMEM)
     edge = jax.ShapeDtypeStruct((2,) + x.shape[1:], BF16)
     return pl.pallas_call(
         rows_kernel,
         out_shape=(edge, edge),
-        in_specs=[pl.BlockSpec(memory_space=pltpu.HBM)] * 3,
+        in_specs=[pl.BlockSpec(memory_space=pltpu.HBM)],
         out_specs=(vmem, vmem),
         scratch_shapes=[pltpu.SemaphoreType.DMA((2,))],
         compiler_params=pltpu.CompilerParams(vmem_limit_bytes=4 * 2**20),
-        cost_estimate=pl.CostEstimate(flops=0, bytes_accessed=30_000_000, transcendentals=0),
+        cost_estimate=pl.CostEstimate(flops=0, bytes_accessed=500_000, transcendentals=0),
         name="row_edges",
-    )(*(pltpu.with_memory_space_constraint(a, pltpu.HBM) for a in (x, w1, w2)))
-
-
-def columns_kernel(x_ref, row_z, row_core, w1_hbm, w2_hbm, odd_ref, even_ref):
+    )(pltpu.with_memory_space_constraint(x, pltpu.HBM))
+
+
+def keep_kernel(edge_ref, *refs):
+    refs[-1][...] = edge_ref[...]
+
+
+def keep(edge, w1, w2):
+    vmem = pl.BlockSpec(memory_space=pltpu.VMEM)
+    return pl.pallas_call(
+        keep_kernel,
+        out_shape=jax.ShapeDtypeStruct(edge.shape, edge.dtype),
+        in_specs=[vmem] + [pl.BlockSpec(memory_space=pltpu.HBM)] * 6,
+        out_specs=vmem,
+        compiler_params=pltpu.CompilerParams(vmem_limit_bytes=4 * 2**20),
+        name="keep",
+    )(edge, *(pltpu.with_memory_space_constraint(a, pltpu.HBM) for a in (w1, w2) * 3))
+
+
+def columns_kernel(x_ref, row_z, row_core, odd_ref, even_ref):
     img_even = lax.axis_index("img") % 2 == 0
     bal_even = lax.axis_index("bal") % 2 == 0
     last = x_ref.shape[1]
@@ -79,18 +100,18 @@
         put(r + 2, x_ref[r])
 
 
-def column_edges(x, row_z, row_core, w1, w2):
+def column_edges(x, row_z, row_core):
     vmem = pl.BlockSpec(memory_space=pltpu.VMEM)
     edge = jax.ShapeDtypeStruct((ROWS + 4, 2, x.shape[2]), BF16)
     return pl.pallas_call(
         columns_kernel,
         out_shape=(edge, edge),
-        in_specs=[vmem] * 3 + [pl.BlockSpec(memory_space=pltpu.HBM)] * 2,
+        in_specs=[vmem] * 3,
         out_specs=(vmem, vmem),
         compiler_params=pltpu.CompilerParams(vmem_limit_bytes=4 * 2**20),
         cost_estimate=pl.CostEstimate(flops=0, bytes_accessed=30_000_000, transcendentals=0),
         name="column_edges",
-    )(x, row_z, row_core, *(pltpu.with_memory_space_constraint(a, pltpu.HBM) for a in (w1, w2)))
+    )(x, row_z, row_core)
 
 
 def block_kernel(
@@ -292,10 +313,11 @@
     full_cols = latent.shape[1] * lax.axis_size("bal")
     mesh_axes = ("img", "bal")
     core_pairs, even_pairs = pair_groups(lax.axis_size("img"), lax.axis_size("bal"))
-    edge_core, edge_z = row_edges(latent, conv1_kernel, conv2_kernel)
+    edge_core, edge_z = row_edges(latent)
     row_z = lax.ppermute(edge_z, "img", swaps(lax.axis_size("img"), 1))
+    edge_core = keep(edge_core, conv1_kernel, conv2_kernel)
     row_core = lax.all_gather(edge_core, mesh_axes, axis_index_groups=core_pairs)
-    edge_odd, edge_even = column_edges(latent, row_z, row_core, conv1_kernel, conv2_kernel)
+    edge_odd, edge_even = column_edges(latent, row_z, row_core)
     col_odd = lax.ppermute(edge_odd, "bal", swaps(lax.axis_size("bal"), 1))
     col_even = lax.all_gather(edge_even, mesh_axes, axis_index_groups=even_pairs)
     return run_block(

time: 21.6 us -> 21.2 us (0.981)
  the two profiles are of different devices: /device:TPU:248 before, /device:TPU:120 now
where the time goes in v7:
time: 21.2 us; the launch traced here: 21 us
  blocking collectives  9.46 us (45%)
  starting transfers between devices  6.77 us (32%)
  Pallas kernels  4.5 us (21%)
    all_gather x1, blocking collectives, shards(): lax.all_gather(edge_core, mesh_axes, axis_index_groups=core_pairs)  4.87 us
    ppermute x1, starting transfers between devices, shards(): col_odd = lax.ppermute(edge_odd, 'bal', swaps(lax.axis_size('bal'), 1))  4.85 us
    all_gather x1, blocking collectives, shards(): lax.all_gather(edge_even, mesh_axes, axis_index_groups=even_pairs)  4.59 us
    pallas_call x1, Pallas kernels, run_block(): pl.pallas_call(functools.partial(block_kernel, full_rows, full_cols), out...  3.66 us
    ppermute x1, starting transfers between devices, shards(): row_z = lax.ppermute(edge_z, 'img', swaps(lax.axis_size('img'), 1))  1.92 us
    pallas_call x1, Pallas kernels, row_edges(): pl.pallas_call(rows_kernel, out_shape=(edge, edge), in_specs=[pl.BlockSpe...  0.79 us
  transfers between devices with their start and end apart: 2, of which 0 were waited for; matrix products, arithmetic and copies ran while one was open for 0% of the time, Pallas kernels for 0%

profile of v7, /device:TPU:120, one launch (start us, length us, event | category | flops | bytes accessed | tf_op | source)
XLA Modules:
  0.0 21.0 jit_solution(739071848374819067)
XLA Ops:
  0.0 0.8 %row_edges.1 = (bf16[2,12,512]{2,1,0:T(8,128)(2,1)S(1)}, bf16[2,12,512]{2,1,0:T(8,128)(2,1)S(1)}) custom-call(bf16[12,12,512]{2,1,0:T(8,128)(2,1)} %x_ref.3), custom_call_target="tpu_custom_call" | custom-call | bytes 500000 | tf_op jit(solution)/shard_map/row_edges/pallas_call | solution.py:58
  0.8 1.9 %collective-permute-start = (bf16[2,12,512]{2,1,0:T(8,128)(2,1)S(1)}, bf16[2,12,512]{2,1,0:T(8,128)(2,1)S(1)}, u32[]{:S(2)}, u32[]{:S(2)}) collective-permute-start(bf16[2,12,512]{2,1,0:T(8,128)(2,1)S(1)} %get-tuple-element.9), channel_id=1, source_target_pairs={{16,32},{32,16},{48,64},{64,48},{80,96},{96,80},{112,128},{128,112... | collective-permute-start | bytes 73736 | tf_op jit(solution)/shard_map/ppermute | solution.py:317
  2.7 0.0 copy-start.2
  2.7 0.0 copy-start
  2.8 0.0 copy-start.1
  2.8 0.0 copy-start.3
  2.8 0.0 copy-start.4
  2.8 0.0 copy-start.5
  2.8 0.0 copy-start.6
  2.8 0.0 copy-start.7
  2.8 0.0 copy-start.8
  2.8 0.0 copy-start.9
  2.9 4.9 %all-gather = bf16[4,12,512]{2,1,0:T(8,128)(2,1)S(1)} all-gather(bf16[2,12,512]{2,1,0:T(8,128)(2,1)S(1)} %keep.1), channel_id=2, replica_groups={{0,16},{1,17},{2,18},{3,19},{4,20},{5,21},{6,22},{7,23},{8,24},{9,25},{..., dimensions={0}, use_global_device_ids=true | all-gather | bytes 73728 | tf_op jit(solution)/shard_map/all_gather | solution.py:319
  7.7 0.0 collective-permute-done.row_z
  7.7 0.0 copy-done.2
  7.7 0.1 column_edges.1
  7.8 4.8 %collective-permute-start.1 = (bf16[16,2,512]{2,1,0:T(2,128)(2,1)S(1)}, bf16[16,2,512]{2,1,0:T(2,128)(2,1)S(1)}, u32[]{:S(2)}, u32[]{:S(2)}) collective-permute-start(bf16[16,2,512]{2,1,0:T(2,128)(2,1)S(1)} %get-tuple-element.11), channel_id=1, source_target_pairs={{1,2},{2,1},{3,4},{4,3},{5,6},{6,5},{7,8},{8,7},{9,10},{10,9},{11,... | collective-permute-start | bytes 98312 | tf_op jit(solution)/shard_map/ppermute | solution.py:321
  12.6 4.6 %all-gather.1 = bf16[32,2,512]{2,1,0:T(2,128)(2,1)S(1)} all-gather(bf16[16,2,512]{2,1,0:T(2,128)(2,1)S(1)} %get-tuple-element.12), channel_id=3, replica_groups={{0,1},{2,3},{4,5},{6,7},{8,9},{10,11},{12,13},{14,15},{16,17},{18,19},{..., dimensions={0}, use_global_device_ids=true | all-gather | bytes 98304 | tf_op jit(solution)/shard_map/all_gather | solution.py:322
  17.2 0.0 collective-permute-done.1.col_odd
  17.2 0.0 copy-done
  17.2 0.0 copy-done.1
  17.2 0.0 copy-done.3
  17.3 0.0 copy-done.4
  17.3 0.0 copy-done.5
  17.3 0.0 copy-done.6
  17.3 0.0 copy-done.7
  17.3 0.0 copy-done.8
  17.3 0.0 copy-done.9
  17.3 3.7 %decode_block.1 = bf16[24,24,512]{2,1,0:T(8,128)(2,1)} custom-call(bf16[12,12,512]{2,1,0:T(8,128)(2,1)S(1)} %copy-done.2, bf16[2,12,512]{2,1,0:T(8,128)(2,1)S(1)} %collective-permute-done.row_z, bf16[2,2,12,512]{3,2,1,0:T(8,128)(2,1)S(1)} %bitcast.11, bf16[16,2,512]{2,1,0:T(2,128)(2,1)S(1)} %collective-permute-done.1.col_odd, ...), custom_call_target="tpu_custom_call" | custom-call | flops 2300000000 | bytes 14000000 | tf_op jit(solution)/shard_map/decode_block/pallas_call | solution.py:278
  (1 shorter events, 0.0 us)
Async XLA Ops:
  0.8 6.9 %collective-permute-start = (bf16[2,12,512]{2,1,0:T(8,128)(2,1)S(1)}, bf16[2,12,512]{2,1,0:T(8,128)(2,1)S(1)}, u32[]{:S(2)}, u32[]{:S(2)}) collective-permute-start(bf16[2,12,512]{2,1,0:T(8,128)(2,1)S(1)} %get-tuple-element.9), channel_id=1, source_target_pairs={{16,32},{32,16},{48,64},{64,48},{80,96},{96,80},{112,128},{128,112... | collective-permute-start | bytes 73736 | tf_op jit(solution)/shard_map/ppermute | solution.py:317
  2.7 5.0 %copy-start.2 = (bf16[12,12,512]{2,1,0:T(8,128)(2,1)S(1)}, bf16[12,12,512]{2,1,0:T(8,128)(2,1)}, u32[]{:S(2)}) copy-start(bf16[12,12,512]{2,1,0:T(8,128)(2,1)} %x_ref.3) | copy-start | bytes 442372
  2.7 14.5 %copy-start = (bf16[3,3,512,512]{3,2,1,0:T(8,128)(2,1)S(1)}, bf16[3,3,512,512]{3,2,1,0:T(8,128)(2,1)}, u32[]{:S(2)}) copy-start(bf16[3,3,512,512]{3,2,1,0:T(8,128)(2,1)} %refs_4_.1) | copy-start | bytes 14155780
  2.8 14.5 %copy-start.1 = (bf16[3,3,512,512]{3,2,1,0:T(8,128)(2,1)S(1)}, bf16[3,3,512,512]{3,2,1,0:T(8,128)(2,1)}, u32[]{:S(2)}) copy-start(bf16[3,3,512,512]{3,2,1,0:T(8,128)(2,1)} %w2_ref.1) | copy-start | bytes 14155780
  2.8 14.5 %copy-start.3 = (f32[512]{0:T(512)S(1)}, f32[512]{0:T(512)}, u32[]{:S(2)}) copy-start(f32[512]{0:T(512)} %param.13) | copy-start | bytes 6148
  2.8 14.5 %copy-start.4 = (f32[512]{0:T(512)S(1)}, f32[512]{0:T(512)}, u32[]{:S(2)}) copy-start(f32[512]{0:T(512)} %param.14) | copy-start | bytes 6148
  2.8 14.5 %copy-start.5 = (f32[512]{0:T(512)S(1)}, f32[512]{0:T(512)}, u32[]{:S(2)}) copy-start(f32[512]{0:T(512)} %param.16) | copy-start | bytes 6148
  2.8 14.5 %copy-start.6 = (f32[512]{0:T(512)S(1)}, f32[512]{0:T(512)}, u32[]{:S(2)}) copy-start(f32[512]{0:T(512)} %param.18) | copy-start | bytes 6148
  2.8 14.5 %copy-start.7 = (s32[4,4]{1,0:T(4,128)S(1)}, s32[4,4]{1,0:T(4,128)}, u32[]{:S(2)}) copy-start(s32[4,4]{1,0:T(4,128)} %dest_ref.1) | copy-start | bytes 196
  2.8 14.5 %copy-start.8 = (f32[32]{0:T(128)S(1)}, f32[32]{0:T(128)}, u32[]{:S(2)}) copy-start(f32[32]{0:T(128)} %param.11) | copy-start | bytes 388
  2.8 14.5 %copy-start.9 = (f32[32]{0:T(128)S(1)}, f32[32]{0:T(128)}, u32[]{:S(2)}) copy-start(f32[32]{0:T(128)} %param.12) | copy-start | bytes 388
  7.8 9.4 %collective-permute-start.1 = (bf16[16,2,512]{2,1,0:T(2,128)(2,1)S(1)}, bf16[16,2,512]{2,1,0:T(2,128)(2,1)S(1)}, u32[]{:S(2)}, u32[]{:S(2)}) collective-permute-start(bf16[16,2,512]{2,1,0:T(2,128)(2,1)S(1)} %get-tuple-element.11), channel_id=1, source_target_pairs={{1,2},{2,1},{3,4},{4,3},{5,6},{6,5},{7,8},{8,7},{9,10},{10,9},{11,... | collective-permute-start | bytes 98312 | tf_op jit(solution)/shard_map/ppermute | solution.py:321

commit v8 on v7

--- a/solution.py
+++ b/solution.py
@@ -185,10 +185,8 @@
     total = side * PITCH
     act[total:] = jnp.zeros((act.shape[0] - total, chan), F32)
 
-    def shift(d):
+    for d in range(3):
         taps[:, d * chan : (d + 1) * chan] = act[d : d + total].astype(BF16)
-
-    shift(0)
 
     inner = (ROWS + 2) * PITCH
     cell = lax.broadcasted_iota(jnp.int32, (inner, 1), 0)
@@ -199,16 +197,10 @@
 
     for part in parts:
         h = b1_ref[:, part]
-        for e in range(3):
-            lane = slice(e * chan, (e + 1) * chan)
-            for d in range(3):
-                h = h + jnp.dot(
-                    taps[d * PITCH : d * PITCH + inner, lane],
-                    w1_ref[d, lane, part],
-                    preferred_element_type=F32,
-                )
-                if part.start == 0 and d == 0 and e < 2:
-                    shift(e + 1)
+        for d in range(3):
+            h = h + jnp.dot(
+                taps[d * PITCH : d * PITCH + inner], w1_ref[d, :, part], preferred_element_type=F32
+            )
         hid[:, part] = jnp.where(ok, h, 0.0).astype(BF16)
 
     cell = lax.broadcasted_iota(jnp.int32, (2 * COLS, TC), 0)
@@ -220,52 +212,44 @@
     span = ROWS * PITCH
     met = ((0, PITCH + span), (PITCH, PITCH + span), (PITCH, 2 * PITCH + span))
 
-    def finish(n, part, by_row):
+    within = slice(MARGIN, MARGIN + 2 * COLS)
+    copies = []
+    for n, part in enumerate(parts):
         lanes = range(part.start // LANES, part.stop // LANES)
         bias = b2_ref[:, part]
 
-        def row(p, r, sums):
-            for m, (q, shift) in enumerate(((0, 0), (0, 1), (1, 1), (1, 2))):
-                cells = sums[m][r * PITCH : (r + 1) * PITCH]
-                at = pl.ds(MARGIN - 2 * shift + q, PITCH, stride=2)
+        def scatter(side, p, q, shift, sums):
+            at = pl.ds(MARGIN - 2 * shift + q, PITCH, stride=2)
+            for r in range(ROWS):
+                cells = sums[r * PITCH : (r + 1) * PITCH]
                 for lane, k in enumerate(lanes):
-                    wide[m % 2, k, 2 * r + p, at] = cells[:, lane * LANES : (lane + 1) * LANES]
+                    wide[side, k, 2 * r + p, at] = cells[:, lane * LANES : (lane + 1) * LANES]
+
+        by_row = []
+        for dx in range(3):
+            first, mid, last = (
+                jnp.dot(hid[a:b], w2_ref[dy, dx, :, part], preferred_element_type=F32)
+                for dy, (a, b) in enumerate(met)
+            )
+            if dx == 1:
+                mid = mid + bias
+            by_row.append((first[:span] + (mid + last[:span]), (first[PITCH:] + mid) + last[PITCH:]))
+            for p in range(2):
+                if dx == 0:
+                    scatter(0, p, 0, 0, by_row[0][p])
+                elif dx == 1:
+                    scatter(0, p, 1, 1, by_row[0][p] + by_row[1][p])
+                else:
+                    scatter(1, p, 0, 1, by_row[1][p] + by_row[2][p])
+                    scatter(1, p, 1, 2, by_row[2][p])
+        for row in range(2 * ROWS):
             for k in lanes:
-                cells = wide[0, k, 2 * r + p, within] + wide[1, k, 2 * r + p, within]
+                cells = wide[0, k, row, within] + wide[1, k, row, within]
                 lane = slice(k * LANES, (k + 1) * LANES)
-                done[2 * r + p, :, lane] = jnp.where(live[r // TS], cells, 0.0).astype(BF16)
-
-        within = slice(MARGIN, MARGIN + 2 * COLS)
-        for p in range(2):
-            left, mid, right = by_row[p]
-            mid = mid + bias
-            sums = (left, mid + right, mid + left, right)
-            for r in range(ROWS):
-                yield functools.partial(row, p, r, sums)
-
-    copies = []
-
-    def send(n, part):
+                done[row, :, lane] = jnp.where(live[row // (2 * TS)], cells, 0.0).astype(BF16)
         copy = pltpu.make_async_copy(done.at[:, :, part], o_ref.at[:, :, part], sems.at[n])
         copy.start()
         copies.append(copy)
-
-    steps = []
-    for n, part in enumerate(parts):
-        terms = {}
-        turns = 9
-        for turn in range(turns):
-            dx, dy = divmod(turn, 3)
-            a, b = met[dy]
-            terms[dy, dx] = jnp.dot(hid[a:b], w2_ref[dy, dx, :, part], preferred_element_type=F32)
-        by_row = [[], []]
-        for dx in range(3):
-            first, mid, last = (terms[dy, dx] for dy in range(3))
-            by_row[0].append(first[:span] + (mid + last[:span]))
-            by_row[1].append((first[PITCH:] + mid) + last[PITCH:])
-        for step in finish(n, part, by_row):
-            step()
-        send(n, part)
     for copy in copies:
         copy.wait()
 

time: 21.2 us -> 21.1 us (level)
  the two profiles are of different devices: /device:TPU:120 before, /device:TPU:248 now
where the time goes in v8:
time: 21.1 us; the launch traced here: 20.9 us
  blocking collectives  9.46 us (45%)
  starting transfers between devices  6.77 us (32%)
  Pallas kernels  4.4 us (21%)
    all_gather x1, blocking collectives, shards(): lax.all_gather(edge_core, mesh_axes, axis_index_groups=core_pairs)  4.87 us
    ppermute x1, starting transfers between devices, shards(): col_odd = lax.ppermute(edge_odd, 'bal', swaps(lax.axis_size('bal'), 1))  4.85 us
    all_gather x1, blocking collectives, shards(): lax.all_gather(edge_even, mesh_axes, axis_index_groups=even_pairs)  4.59 us
    pallas_call x1, Pallas kernels, run_block(): pl.pallas_call(functools.partial(block_kernel, full_rows, full_cols), out...  3.56 us
    ppermute x1, starting transfers between devices, shards(): row_z = lax.ppermute(edge_z, 'img', swaps(lax.axis_size('img'), 1))  1.92 us
    pallas_call x1, Pallas kernels, row_edges(): pl.pallas_call(rows_kernel, out_shape=(edge, edge), in_specs=[pl.BlockSpe...  0.79 us
  transfers between devices with their start and end apart: 2, of which 0 were waited for; matrix products, arithmetic and copies ran while one was open for 0% of the time, Pallas kernels for 0%

profile of v8, /device:TPU:248, one launch (start us, length us, event | category | flops | bytes accessed | tf_op | source)
XLA Modules:
  0.0 20.9 jit_solution(5278707074070368831)
XLA Ops:
  0.0 0.8 %row_edges.1 = (bf16[2,12,512]{2,1,0:T(8,128)(2,1)S(1)}, bf16[2,12,512]{2,1,0:T(8,128)(2,1)S(1)}) custom-call(bf16[12,12,512]{2,1,0:T(8,128)(2,1)} %x_ref.3), custom_call_target="tpu_custom_call" | custom-call | bytes 500000 | tf_op jit(solution)/shard_map/row_edges/pallas_call | solution.py:58
  0.8 1.9 %collective-permute-start = (bf16[2,12,512]{2,1,0:T(8,128)(2,1)S(1)}, bf16[2,12,512]{2,1,0:T(8,128)(2,1)S(1)}, u32[]{:S(2)}, u32[]{:S(2)}) collective-permute-start(bf16[2,12,512]{2,1,0:T(8,128)(2,1)S(1)} %get-tuple-element.9), channel_id=1, source_target_pairs={{16,32},{32,16},{48,64},{64,48},{80,96},{96,80},{112,128},{128,112... | collective-permute-start | bytes 73736 | tf_op jit(solution)/shard_map/ppermute | solution.py:301
  2.7 0.0 copy-start.2
  2.7 0.0 copy-start
  2.8 0.0 copy-start.1
  2.8 0.0 copy-start.3
  2.8 0.0 copy-start.4
  2.8 0.0 copy-start.5
  2.8 0.0 copy-start.6
  2.8 0.0 copy-start.7
  2.8 0.0 copy-start.8
  2.8 0.0 copy-start.9
  2.9 4.9 %all-gather = bf16[4,12,512]{2,1,0:T(8,128)(2,1)S(1)} all-gather(bf16[2,12,512]{2,1,0:T(8,128)(2,1)S(1)} %keep.1), channel_id=2, replica_groups={{0,16},{1,17},{2,18},{3,19},{4,20},{5,21},{6,22},{7,23},{8,24},{9,25},{..., dimensions={0}, use_global_device_ids=true | all-gather | bytes 73728 | tf_op jit(solution)/shard_map/all_gather | solution.py:303
  7.7 0.0 collective-permute-done.row_z
  7.7 0.0 copy-done.2
  7.7 0.1 column_edges.1
  7.8 4.8 %collective-permute-start.1 = (bf16[16,2,512]{2,1,0:T(2,128)(2,1)S(1)}, bf16[16,2,512]{2,1,0:T(2,128)(2,1)S(1)}, u32[]{:S(2)}, u32[]{:S(2)}) collective-permute-start(bf16[16,2,512]{2,1,0:T(2,128)(2,1)S(1)} %get-tuple-element.11), channel_id=1, source_target_pairs={{1,2},{2,1},{3,4},{4,3},{5,6},{6,5},{7,8},{8,7},{9,10},{10,9},{11,... | collective-permute-start | bytes 98312 | tf_op jit(solution)/shard_map/ppermute | solution.py:305
  12.6 4.6 %all-gather.1 = bf16[32,2,512]{2,1,0:T(2,128)(2,1)S(1)} all-gather(bf16[16,2,512]{2,1,0:T(2,128)(2,1)S(1)} %get-tuple-element.12), channel_id=3, replica_groups={{0,1},{2,3},{4,5},{6,7},{8,9},{10,11},{12,13},{14,15},{16,17},{18,19},{..., dimensions={0}, use_global_device_ids=true | all-gather | bytes 98304 | tf_op jit(solution)/shard_map/all_gather | solution.py:306
  17.2 0.0 collective-permute-done.1.col_odd
  17.2 0.0 copy-done
  17.2 0.0 copy-done.1
  17.2 0.0 copy-done.3
  17.3 0.0 copy-done.4
  17.3 0.0 copy-done.5
  17.3 0.0 copy-done.6
  17.3 0.0 copy-done.7
  17.3 0.0 copy-done.8
  17.3 0.0 copy-done.9
  17.3 3.6 %decode_block.1 = bf16[24,24,512]{2,1,0:T(8,128)(2,1)} custom-call(bf16[12,12,512]{2,1,0:T(8,128)(2,1)S(1)} %copy-done.2, bf16[2,12,512]{2,1,0:T(8,128)(2,1)S(1)} %collective-permute-done.row_z, bf16[2,2,12,512]{3,2,1,0:T(8,128)(2,1)S(1)} %bitcast.11, bf16[16,2,512]{2,1,0:T(2,128)(2,1)S(1)} %collective-permute-done.1.col_odd, ...), custom_call_target="tpu_custom_call" | custom-call | flops 2300000000 | bytes 14000000 | tf_op jit(solution)/shard_map/decode_block/pallas_call | solution.py:262
  (1 shorter events, 0.0 us)
Async XLA Ops:
  0.8 6.9 %collective-permute-start = (bf16[2,12,512]{2,1,0:T(8,128)(2,1)S(1)}, bf16[2,12,512]{2,1,0:T(8,128)(2,1)S(1)}, u32[]{:S(2)}, u32[]{:S(2)}) collective-permute-start(bf16[2,12,512]{2,1,0:T(8,128)(2,1)S(1)} %get-tuple-element.9), channel_id=1, source_target_pairs={{16,32},{32,16},{48,64},{64,48},{80,96},{96,80},{112,128},{128,112... | collective-permute-start | bytes 73736 | tf_op jit(solution)/shard_map/ppermute | solution.py:301
  2.7 5.0 %copy-start.2 = (bf16[12,12,512]{2,1,0:T(8,128)(2,1)S(1)}, bf16[12,12,512]{2,1,0:T(8,128)(2,1)}, u32[]{:S(2)}) copy-start(bf16[12,12,512]{2,1,0:T(8,128)(2,1)} %x_ref.3) | copy-start | bytes 442372
  2.7 14.5 %copy-start = (bf16[3,3,512,512]{3,2,1,0:T(8,128)(2,1)S(1)}, bf16[3,3,512,512]{3,2,1,0:T(8,128)(2,1)}, u32[]{:S(2)}) copy-start(bf16[3,3,512,512]{3,2,1,0:T(8,128)(2,1)} %refs_4_.1) | copy-start | bytes 14155780
  2.8 14.5 %copy-start.1 = (bf16[3,3,512,512]{3,2,1,0:T(8,128)(2,1)S(1)}, bf16[3,3,512,512]{3,2,1,0:T(8,128)(2,1)}, u32[]{:S(2)}) copy-start(bf16[3,3,512,512]{3,2,1,0:T(8,128)(2,1)} %w2_ref.1) | copy-start | bytes 14155780
  2.8 14.5 %copy-start.3 = (f32[512]{0:T(512)S(1)}, f32[512]{0:T(512)}, u32[]{:S(2)}) copy-start(f32[512]{0:T(512)} %param.13) | copy-start | bytes 6148
  2.8 14.5 %copy-start.4 = (f32[512]{0:T(512)S(1)}, f32[512]{0:T(512)}, u32[]{:S(2)}) copy-start(f32[512]{0:T(512)} %param.14) | copy-start | bytes 6148
  2.8 14.5 %copy-start.5 = (f32[512]{0:T(512)S(1)}, f32[512]{0:T(512)}, u32[]{:S(2)}) copy-start(f32[512]{0:T(512)} %param.16) | copy-start | bytes 6148
  2.8 14.5 %copy-start.6 = (f32[512]{0:T(512)S(1)}, f32[512]{0:T(512)}, u32[]{:S(2)}) copy-start(f32[512]{0:T(512)} %param.18) | copy-start | bytes 6148
  2.8 14.5 %copy-start.7 = (s32[4,4]{1,0:T(4,128)S(1)}, s32[4,4]{1,0:T(4,128)}, u32[]{:S(2)}) copy-start(s32[4,4]{1,0:T(4,128)} %dest_ref.1) | copy-start | bytes 196
  2.8 14.5 %copy-start.8 = (f32[32]{0:T(128)S(1)}, f32[32]{0:T(128)}, u32[]{:S(2)}) copy-start(f32[32]{0:T(128)} %param.11) | copy-start | bytes 388
  2.8 14.5 %copy-start.9 = (f32[32]{0:T(128)S(1)}, f32[32]{0:T(128)}, u32[]{:S(2)}) copy-start(f32[32]{0:T(128)} %param.12) | copy-start | bytes 388
  7.8 9.4 %collective-permute-start.1 = (bf16[16,2,512]{2,1,0:T(2,128)(2,1)S(1)}, bf16[16,2,512]{2,1,0:T(2,128)(2,1)S(1)}, u32[]{:S(2)}, u32[]{:S(2)}) collective-permute-start(bf16[16,2,512]{2,1,0:T(2,128)(2,1)S(1)} %get-tuple-element.11), channel_id=1, source_target_pairs={{1,2},{2,1},{3,4},{4,3},{5,6},{6,5},{7,8},{8,7},{9,10},{10,9},{11,... | collective-permute-start | bytes 98312 | tf_op jit(solution)/shard_map/ppermute | solution.py:305

commit v9 on v8

--- a/solution.py
+++ b/solution.py
@@ -14,6 +14,7 @@
 COLS = TC * TS
 LANES = 128
 SPLIT = 256
+BATCH = 12
 MARGIN = 8
 PITCH = 16
 F32 = jnp.float32
@@ -247,9 +248,11 @@
                 cells = wide[0, k, row, within] + wide[1, k, row, within]
                 lane = slice(k * LANES, (k + 1) * LANES)
                 done[row, :, lane] = jnp.where(live[row // (2 * TS)], cells, 0.0).astype(BF16)
-        copy = pltpu.make_async_copy(done.at[:, :, part], o_ref.at[:, :, part], sems.at[n])
-        copy.start()
-        copies.append(copy)
+            if (row + 1) % BATCH == 0:
+                at = (slice(row + 1 - BATCH, row + 1), slice(None), part)
+                copy = pltpu.make_async_copy(done.at[at], o_ref.at[at], sems.at[len(copies)])
+                copy.start()
+                copies.append(copy)
     for copy in copies:
         copy.wait()
 
@@ -270,7 +273,7 @@
             pltpu.VMEM((inner, chan), BF16),
             pltpu.VMEM((2, chan // LANES, 2 * ROWS, MARGIN + 2 * PITCH, LANES), F32),
             pltpu.VMEM((2 * ROWS, 2 * COLS, chan), BF16),
-            pltpu.SemaphoreType.DMA((chan // SPLIT,)),
+            pltpu.SemaphoreType.DMA((chan // SPLIT * 2 * ROWS // BATCH,)),
         ],
         compiler_params=pltpu.CompilerParams(vmem_limit_bytes=36 * 2**20),
         cost_estimate=pl.CostEstimate(

time: 21.1 us -> 21 us (level)
  no operation moved by 1% of the time
where the time goes in v9:
time: 21 us; the launch traced here: 20.8 us
  blocking collectives  9.46 us (45%)
  starting transfers between devices  6.77 us (32%)
  Pallas kernels  4.35 us (21%)
    all_gather x1, blocking collectives, shards(): lax.all_gather(edge_core, mesh_axes, axis_index_groups=core_pairs)  4.87 us
    ppermute x1, starting transfers between devices, shards(): col_odd = lax.ppermute(edge_odd, 'bal', swaps(lax.axis_size('bal'), 1))  4.85 us
    all_gather x1, blocking collectives, shards(): lax.all_gather(edge_even, mesh_axes, axis_index_groups=even_pairs)  4.59 us
    pallas_call x1, Pallas kernels, run_block(): pl.pallas_call(functools.partial(block_kernel, full_rows, full_cols), out...  3.51 us
    ppermute x1, starting transfers between devices, shards(): row_z = lax.ppermute(edge_z, 'img', swaps(lax.axis_size('img'), 1))  1.92 us
    pallas_call x1, Pallas kernels, row_edges(): pl.pallas_call(rows_kernel, out_shape=(edge, edge), in_specs=[pl.BlockSpe...  0.79 us
  transfers between devices with their start and end apart: 2, of which 0 were waited for; matrix products, arithmetic and copies ran while one was open for 0% of the time, Pallas kernels for 0%

profile of v9, /device:TPU:248, one launch (start us, length us, event | category | flops | bytes accessed | tf_op | source)
XLA Modules:
  0.0 20.8 jit_solution(143180316735341122)
XLA Ops:
  0.0 0.8 %row_edges.1 = (bf16[2,12,512]{2,1,0:T(8,128)(2,1)S(1)}, bf16[2,12,512]{2,1,0:T(8,128)(2,1)S(1)}) custom-call(bf16[12,12,512]{2,1,0:T(8,128)(2,1)} %x_ref.3), custom_call_target="tpu_custom_call" | custom-call | bytes 500000 | tf_op jit(solution)/shard_map/row_edges/pallas_call | solution.py:59
  0.8 1.9 %collective-permute-start = (bf16[2,12,512]{2,1,0:T(8,128)(2,1)S(1)}, bf16[2,12,512]{2,1,0:T(8,128)(2,1)S(1)}, u32[]{:S(2)}, u32[]{:S(2)}) collective-permute-start(bf16[2,12,512]{2,1,0:T(8,128)(2,1)S(1)} %get-tuple-element.9), channel_id=1, source_target_pairs={{16,32},{32,16},{48,64},{64,48},{80,96},{96,80},{112,128},{128,112... | collective-permute-start | bytes 73736 | tf_op jit(solution)/shard_map/ppermute | solution.py:304
  2.7 0.0 copy-start.2
  2.7 0.0 copy-start
  2.8 0.0 copy-start.1
  2.8 0.0 copy-start.3
  2.8 0.0 copy-start.4
  2.8 0.0 copy-start.5
  2.8 0.0 copy-start.6
  2.8 0.0 copy-start.7
  2.8 0.0 copy-start.8
  2.8 0.0 copy-start.9
  2.9 4.9 %all-gather = bf16[4,12,512]{2,1,0:T(8,128)(2,1)S(1)} all-gather(bf16[2,12,512]{2,1,0:T(8,128)(2,1)S(1)} %keep.1), channel_id=2, replica_groups={{0,16},{1,17},{2,18},{3,19},{4,20},{5,21},{6,22},{7,23},{8,24},{9,25},{..., dimensions={0}, use_global_device_ids=true | all-gather | bytes 73728 | tf_op jit(solution)/shard_map/all_gather | solution.py:306
  7.7 0.0 collective-permute-done.row_z
  7.7 0.0 copy-done.2
  7.7 0.1 column_edges.1
  7.8 4.8 %collective-permute-start.1 = (bf16[16,2,512]{2,1,0:T(2,128)(2,1)S(1)}, bf16[16,2,512]{2,1,0:T(2,128)(2,1)S(1)}, u32[]{:S(2)}, u32[]{:S(2)}) collective-permute-start(bf16[16,2,512]{2,1,0:T(2,128)(2,1)S(1)} %get-tuple-element.11), channel_id=1, source_target_pairs={{1,2},{2,1},{3,4},{4,3},{5,6},{6,5},{7,8},{8,7},{9,10},{10,9},{11,... | collective-permute-start | bytes 98312 | tf_op jit(solution)/shard_map/ppermute | solution.py:308
  12.6 4.6 %all-gather.1 = bf16[32,2,512]{2,1,0:T(2,128)(2,1)S(1)} all-gather(bf16[16,2,512]{2,1,0:T(2,128)(2,1)S(1)} %get-tuple-element.12), channel_id=3, replica_groups={{0,1},{2,3},{4,5},{6,7},{8,9},{10,11},{12,13},{14,15},{16,17},{18,19},{..., dimensions={0}, use_global_device_ids=true | all-gather | bytes 98304 | tf_op jit(solution)/shard_map/all_gather | solution.py:309
  17.2 0.0 collective-permute-done.1.col_odd
  17.2 0.0 copy-done
  17.2 0.0 copy-done.1
  17.2 0.0 copy-done.3
  17.3 0.0 copy-done.4
  17.3 0.0 copy-done.5
  17.3 0.0 copy-done.6
  17.3 0.0 copy-done.7
  17.3 0.0 copy-done.8
  17.3 0.0 copy-done.9
  17.3 3.5 %decode_block.1 = bf16[24,24,512]{2,1,0:T(8,128)(2,1)} custom-call(bf16[12,12,512]{2,1,0:T(8,128)(2,1)S(1)} %copy-done.2, bf16[2,12,512]{2,1,0:T(8,128)(2,1)S(1)} %collective-permute-done.row_z, bf16[2,2,12,512]{3,2,1,0:T(8,128)(2,1)S(1)} %bitcast.11, bf16[16,2,512]{2,1,0:T(2,128)(2,1)S(1)} %collective-permute-done.1.col_odd, ...), custom_call_target="tpu_custom_call" | custom-call | flops 2300000000 | bytes 14000000 | tf_op jit(solution)/shard_map/decode_block/pallas_call | solution.py:265
  (1 shorter events, 0.0 us)
Async XLA Ops:
  0.8 6.9 %collective-permute-start = (bf16[2,12,512]{2,1,0:T(8,128)(2,1)S(1)}, bf16[2,12,512]{2,1,0:T(8,128)(2,1)S(1)}, u32[]{:S(2)}, u32[]{:S(2)}) collective-permute-start(bf16[2,12,512]{2,1,0:T(8,128)(2,1)S(1)} %get-tuple-element.9), channel_id=1, source_target_pairs={{16,32},{32,16},{48,64},{64,48},{80,96},{96,80},{112,128},{128,112... | collective-permute-start | bytes 73736 | tf_op jit(solution)/shard_map/ppermute | solution.py:304
  2.7 5.0 %copy-start.2 = (bf16[12,12,512]{2,1,0:T(8,128)(2,1)S(1)}, bf16[12,12,512]{2,1,0:T(8,128)(2,1)}, u32[]{:S(2)}) copy-start(bf16[12,12,512]{2,1,0:T(8,128)(2,1)} %x_ref.3) | copy-start | bytes 442372
  2.7 14.5 %copy-start = (bf16[3,3,512,512]{3,2,1,0:T(8,128)(2,1)S(1)}, bf16[3,3,512,512]{3,2,1,0:T(8,128)(2,1)}, u32[]{:S(2)}) copy-start(bf16[3,3,512,512]{3,2,1,0:T(8,128)(2,1)} %refs_4_.1) | copy-start | bytes 14155780
  2.8 14.5 %copy-start.1 = (bf16[3,3,512,512]{3,2,1,0:T(8,128)(2,1)S(1)}, bf16[3,3,512,512]{3,2,1,0:T(8,128)(2,1)}, u32[]{:S(2)}) copy-start(bf16[3,3,512,512]{3,2,1,0:T(8,128)(2,1)} %w2_ref.1) | copy-start | bytes 14155780
  2.8 14.5 %copy-start.3 = (f32[512]{0:T(512)S(1)}, f32[512]{0:T(512)}, u32[]{:S(2)}) copy-start(f32[512]{0:T(512)} %param.13) | copy-start | bytes 6148
  2.8 14.5 %copy-start.4 = (f32[512]{0:T(512)S(1)}, f32[512]{0:T(512)}, u32[]{:S(2)}) copy-start(f32[512]{0:T(512)} %param.14) | copy-start | bytes 6148
  2.8 14.5 %copy-start.5 = (f32[512]{0:T(512)S(1)}, f32[512]{0:T(512)}, u32[]{:S(2)}) copy-start(f32[512]{0:T(512)} %param.16) | copy-start | bytes 6148
  2.8 14.5 %copy-start.6 = (f32[512]{0:T(512)S(1)}, f32[512]{0:T(512)}, u32[]{:S(2)}) copy-start(f32[512]{0:T(512)} %param.18) | copy-start | bytes 6148
  2.8 14.5 %copy-start.7 = (s32[4,4]{1,0:T(4,128)S(1)}, s32[4,4]{1,0:T(4,128)}, u32[]{:S(2)}) copy-start(s32[4,4]{1,0:T(4,128)} %dest_ref.1) | copy-start | bytes 196
  2.8 14.5 %copy-start.8 = (f32[32]{0:T(128)S(1)}, f32[32]{0:T(128)}, u32[]{:S(2)}) copy-start(f32[32]{0:T(128)} %param.11) | copy-start | bytes 388
  2.8 14.5 %copy-start.9 = (f32[32]{0:T(128)S(1)}, f32[32]{0:T(128)}, u32[]{:S(2)}) copy-start(f32[32]{0:T(128)} %param.12) | copy-start | bytes 388
  7.8 9.4 %collective-permute-start.1 = (bf16[16,2,512]{2,1,0:T(2,128)(2,1)S(1)}, bf16[16,2,512]{2,1,0:T(2,128)(2,1)S(1)}, u32[]{:S(2)}, u32[]{:S(2)}) collective-permute-start(bf16[16,2,512]{2,1,0:T(2,128)(2,1)S(1)} %get-tuple-element.11), channel_id=1, source_target_pairs={{1,2},{2,1},{3,4},{4,3},{5,6},{6,5},{7,8},{8,7},{9,10},{10,9},{11,... | collective-permute-start | bytes 98312 | tf_op jit(solution)/shard_map/ppermute | solution.py:308

commit v10 on v9

--- a/solution.py
+++ b/solution.py
@@ -148,12 +148,16 @@
 
     groups = mean_ref.shape[1]
     group_of = lax.broadcasted_iota(jnp.int32, (groups, chan), 1) // (chan // groups)
-    spread = (lax.broadcasted_iota(jnp.int32, (groups, chan), 0) == group_of).astype(F32)
-    exact = functools.partial(
-        jnp.dot, precision=lax.Precision.HIGHEST, preferred_element_type=F32
-    )
-    mean = exact(jnp.broadcast_to(mean_ref[...], (8, groups)), spread)[0:1]
-    rstd = exact(jnp.broadcast_to(rstd_ref[...], (8, groups)), spread)[0:1]
+    spread = lax.broadcasted_iota(jnp.int32, (groups, chan), 0) == group_of
+    square = (groups, groups)
+    diagonal = lax.broadcasted_iota(jnp.int32, square, 0) == lax.broadcasted_iota(jnp.int32, square, 1)
+
+    def per_channel(ref):
+        column = jnp.sum(jnp.where(diagonal, ref[...], 0.0), axis=1, keepdims=True)
+        return jnp.sum(jnp.where(spread, column, 0.0), axis=0, keepdims=True)
+
+    mean = per_channel(mean_ref)
+    rstd = per_channel(rstd_ref)
     gain = gain_ref[...]
     shift = shift_ref[...]
 

time: 21 us -> 21 us (level)
  no operation moved by 1% of the time
where the time goes in v10:
time: 21 us; the launch traced here: 20.8 us
  blocking collectives  9.46 us (45%)
  starting transfers between devices  6.77 us (32%)
  Pallas kernels  4.32 us (21%)
    all_gather x1, blocking collectives, shards(): lax.all_gather(edge_core, mesh_axes, axis_index_groups=core_pairs)  4.87 us
    ppermute x1, starting transfers between devices, shards(): col_odd = lax.ppermute(edge_odd, 'bal', swaps(lax.axis_size('bal'), 1))  4.85 us
    all_gather x1, blocking collectives, shards(): lax.all_gather(edge_even, mesh_axes, axis_index_groups=even_pairs)  4.59 us
    pallas_call x1, Pallas kernels, run_block(): pl.pallas_call(functools.partial(block_kernel, full_rows, full_cols), out...  3.47 us
    ppermute x1, starting transfers between devices, shards(): row_z = lax.ppermute(edge_z, 'img', swaps(lax.axis_size('img'), 1))  1.92 us
    pallas_call x1, Pallas kernels, row_edges(): pl.pallas_call(rows_kernel, out_shape=(edge, edge), in_specs=[pl.BlockSpe...  0.79 us
  transfers between devices with their start and end apart: 2, of which 0 were waited for; matrix products, arithmetic and copies ran while one was open for 0% of the time, Pallas kernels for 0%

profile of v10, /device:TPU:248, one launch (start us, length us, event | category | flops | bytes accessed | tf_op | source)
XLA Modules:
  0.0 20.8 jit_solution(611354128372004595)
XLA Ops:
  0.0 0.8 %row_edges.1 = (bf16[2,12,512]{2,1,0:T(8,128)(2,1)S(1)}, bf16[2,12,512]{2,1,0:T(8,128)(2,1)S(1)}) custom-call(bf16[12,12,512]{2,1,0:T(8,128)(2,1)} %x_ref.3), custom_call_target="tpu_custom_call" | custom-call | bytes 500000 | tf_op jit(solution)/shard_map/row_edges/pallas_call | solution.py:59
  0.8 1.9 %collective-permute-start = (bf16[2,12,512]{2,1,0:T(8,128)(2,1)S(1)}, bf16[2,12,512]{2,1,0:T(8,128)(2,1)S(1)}, u32[]{:S(2)}, u32[]{:S(2)}) collective-permute-start(bf16[2,12,512]{2,1,0:T(8,128)(2,1)S(1)} %get-tuple-element.9), channel_id=1, source_target_pairs={{16,32},{32,16},{48,64},{64,48},{80,96},{96,80},{112,128},{128,112... | collective-permute-start | bytes 73736 | tf_op jit(solution)/shard_map/ppermute | solution.py:308
  2.7 0.0 copy-start.2
  2.7 0.0 copy-start
  2.8 0.0 copy-start.1
  2.8 0.0 copy-start.3
  2.8 0.0 copy-start.4
  2.8 0.0 copy-start.5
  2.8 0.0 copy-start.6
  2.8 0.0 copy-start.7
  2.8 0.0 copy-start.8
  2.8 0.0 copy-start.9
  2.9 4.9 %all-gather = bf16[4,12,512]{2,1,0:T(8,128)(2,1)S(1)} all-gather(bf16[2,12,512]{2,1,0:T(8,128)(2,1)S(1)} %keep.1), channel_id=2, replica_groups={{0,16},{1,17},{2,18},{3,19},{4,20},{5,21},{6,22},{7,23},{8,24},{9,25},{..., dimensions={0}, use_global_device_ids=true | all-gather | bytes 73728 | tf_op jit(solution)/shard_map/all_gather | solution.py:310
  7.7 0.0 collective-permute-done.row_z
  7.7 0.0 copy-done.2
  7.7 0.1 column_edges.1
  7.8 4.8 %collective-permute-start.1 = (bf16[16,2,512]{2,1,0:T(2,128)(2,1)S(1)}, bf16[16,2,512]{2,1,0:T(2,128)(2,1)S(1)}, u32[]{:S(2)}, u32[]{:S(2)}) collective-permute-start(bf16[16,2,512]{2,1,0:T(2,128)(2,1)S(1)} %get-tuple-element.11), channel_id=1, source_target_pairs={{1,2},{2,1},{3,4},{4,3},{5,6},{6,5},{7,8},{8,7},{9,10},{10,9},{11,... | collective-permute-start | bytes 98312 | tf_op jit(solution)/shard_map/ppermute | solution.py:312
  12.6 4.6 %all-gather.1 = bf16[32,2,512]{2,1,0:T(2,128)(2,1)S(1)} all-gather(bf16[16,2,512]{2,1,0:T(2,128)(2,1)S(1)} %get-tuple-element.12), channel_id=3, replica_groups={{0,1},{2,3},{4,5},{6,7},{8,9},{10,11},{12,13},{14,15},{16,17},{18,19},{..., dimensions={0}, use_global_device_ids=true | all-gather | bytes 98304 | tf_op jit(solution)/shard_map/all_gather | solution.py:313
  17.2 0.0 collective-permute-done.1.col_odd
  17.2 0.0 copy-done
  17.2 0.0 copy-done.1
  17.2 0.0 copy-done.3
  17.3 0.0 copy-done.4
  17.3 0.0 copy-done.5
  17.3 0.0 copy-done.6
  17.3 0.0 copy-done.7
  17.3 0.0 copy-done.8
  17.3 0.0 copy-done.9
  17.3 3.5 %decode_block.1 = bf16[24,24,512]{2,1,0:T(8,128)(2,1)} custom-call(bf16[12,12,512]{2,1,0:T(8,128)(2,1)S(1)} %copy-done.2, bf16[2,12,512]{2,1,0:T(8,128)(2,1)S(1)} %collective-permute-done.row_z, bf16[2,2,12,512]{3,2,1,0:T(8,128)(2,1)S(1)} %bitcast.11, bf16[16,2,512]{2,1,0:T(2,128)(2,1)S(1)} %collective-permute-done.1.col_odd, ...), custom_call_target="tpu_custom_call" | custom-call | flops 2300000000 | bytes 14000000 | tf_op jit(solution)/shard_map/decode_block/pallas_call | solution.py:269
  (1 shorter events, 0.0 us)
Async XLA Ops:
  0.8 6.9 %collective-permute-start = (bf16[2,12,512]{2,1,0:T(8,128)(2,1)S(1)}, bf16[2,12,512]{2,1,0:T(8,128)(2,1)S(1)}, u32[]{:S(2)}, u32[]{:S(2)}) collective-permute-start(bf16[2,12,512]{2,1,0:T(8,128)(2,1)S(1)} %get-tuple-element.9), channel_id=1, source_target_pairs={{16,32},{32,16},{48,64},{64,48},{80,96},{96,80},{112,128},{128,112... | collective-permute-start | bytes 73736 | tf_op jit(solution)/shard_map/ppermute | solution.py:308
  2.7 5.0 %copy-start.2 = (bf16[12,12,512]{2,1,0:T(8,128)(2,1)S(1)}, bf16[12,12,512]{2,1,0:T(8,128)(2,1)}, u32[]{:S(2)}) copy-start(bf16[12,12,512]{2,1,0:T(8,128)(2,1)} %x_ref.3) | copy-start | bytes 442372
  2.7 14.5 %copy-start = (bf16[3,3,512,512]{3,2,1,0:T(8,128)(2,1)S(1)}, bf16[3,3,512,512]{3,2,1,0:T(8,128)(2,1)}, u32[]{:S(2)}) copy-start(bf16[3,3,512,512]{3,2,1,0:T(8,128)(2,1)} %refs_4_.1) | copy-start | bytes 14155780
  2.8 14.5 %copy-start.1 = (bf16[3,3,512,512]{3,2,1,0:T(8,128)(2,1)S(1)}, bf16[3,3,512,512]{3,2,1,0:T(8,128)(2,1)}, u32[]{:S(2)}) copy-start(bf16[3,3,512,512]{3,2,1,0:T(8,128)(2,1)} %w2_ref.1) | copy-start | bytes 14155780
  2.8 14.5 %copy-start.3 = (f32[512]{0:T(512)S(1)}, f32[512]{0:T(512)}, u32[]{:S(2)}) copy-start(f32[512]{0:T(512)} %param.13) | copy-start | bytes 6148
  2.8 14.5 %copy-start.4 = (f32[512]{0:T(512)S(1)}, f32[512]{0:T(512)}, u32[]{:S(2)}) copy-start(f32[512]{0:T(512)} %param.14) | copy-start | bytes 6148
  2.8 14.5 %copy-start.5 = (f32[512]{0:T(512)S(1)}, f32[512]{0:T(512)}, u32[]{:S(2)}) copy-start(f32[512]{0:T(512)} %param.16) | copy-start | bytes 6148
  2.8 14.5 %copy-start.6 = (f32[512]{0:T(512)S(1)}, f32[512]{0:T(512)}, u32[]{:S(2)}) copy-start(f32[512]{0:T(512)} %param.18) | copy-start | bytes 6148
  2.8 14.5 %copy-start.7 = (s32[4,4]{1,0:T(4,128)S(1)}, s32[4,4]{1,0:T(4,128)}, u32[]{:S(2)}) copy-start(s32[4,4]{1,0:T(4,128)} %dest_ref.1) | copy-start | bytes 196
  2.8 14.5 %copy-start.8 = (f32[32]{0:T(128)S(1)}, f32[32]{0:T(128)}, u32[]{:S(2)}) copy-start(f32[32]{0:T(128)} %param.11) | copy-start | bytes 388
  2.8 14.5 %copy-start.9 = (f32[32]{0:T(128)S(1)}, f32[32]{0:T(128)}, u32[]{:S(2)}) copy-start(f32[32]{0:T(128)} %param.12) | copy-start | bytes 388
  7.8 9.4 %collective-permute-start.1 = (bf16[16,2,512]{2,1,0:T(2,128)(2,1)S(1)}, bf16[16,2,512]{2,1,0:T(2,128)(2,1)S(1)}, u32[]{:S(2)}, u32[]{:S(2)}) collective-permute-start(bf16[16,2,512]{2,1,0:T(2,128)(2,1)S(1)} %get-tuple-element.11), channel_id=1, source_target_pairs={{1,2},{2,1},{3,4},{4,3},{5,6},{6,5},{7,8},{8,7},{9,10},{10,9},{11,... | collective-permute-start | bytes 98312 | tf_op jit(solution)/shard_map/ppermute | solution.py:312

commit v11 on v10

--- a/solution.py
+++ b/solution.py
@@ -172,21 +172,16 @@
     lines = [x_ref[r] for r in range(ROWS)]
     lines = [jnp.where(img_even, row_z[r], row_core[0, r]) for r in range(2)] + lines
     lines += [jnp.where(img_even, row_core[1, r], row_z[r]) for r in range(2)]
+    cell = lax.broadcasted_iota(jnp.int32, (PITCH, 1), 0)
+    col = bal * COLS - 2 + cell
+    col_ok = (col >= 0) & (col < full_cols)
     for r, line in enumerate(lines):
         left = jnp.where(bal_even, col_odd[r], col_even[0, r])
         right = jnp.where(bal_even, col_even[1, r], col_odd[r])
-        at = r * PITCH
-        act[at : at + 2] = left.astype(F32)
-        act[at + 2 : at + 2 + COLS] = line.astype(F32)
-        act[at + 2 + COLS : at + PITCH] = right.astype(F32)
-    cell = lax.broadcasted_iota(jnp.int32, (PITCH, 1), 0)
-    col = bal * COLS - 2 + cell
-    col_ok = (col >= 0) & (col < full_cols)
-    for r in range(side):
         row = img * ROWS - 2 + r
         ok = col_ok & ((row >= 0) & (row < full_rows))
-        at = slice(r * PITCH, (r + 1) * PITCH)
-        act[at] = jnp.where(ok, activate(act[at]), 0.0)
+        cells = jnp.concatenate([c.astype(F32) for c in (left, line, right)], axis=0)
+        act[r * PITCH : (r + 1) * PITCH] = jnp.where(ok, activate(cells), 0.0)
     total = side * PITCH
     act[total:] = jnp.zeros((act.shape[0] - total, chan), F32)
 

time: 21 us -> 21 us (level)
  no operation moved by 1% of the time
where the time goes in v11:
time: 21 us; the launch traced here: 20.8 us
  blocking collectives  9.46 us (45%)
  starting transfers between devices  6.77 us (32%)
  Pallas kernels  4.28 us (20%)
    all_gather x1, blocking collectives, shards(): lax.all_gather(edge_core, mesh_axes, axis_index_groups=core_pairs)  4.87 us
    ppermute x1, starting transfers between devices, shards(): col_odd = lax.ppermute(edge_odd, 'bal', swaps(lax.axis_size('bal'), 1))  4.85 us
    all_gather x1, blocking collectives, shards(): lax.all_gather(edge_even, mesh_axes, axis_index_groups=even_pairs)  4.59 us
    pallas_call x1, Pallas kernels, run_block(): pl.pallas_call(functools.partial(block_kernel, full_rows, full_cols), out...  3.44 us
    ppermute x1, starting transfers between devices, shards(): row_z = lax.ppermute(edge_z, 'img', swaps(lax.axis_size('img'), 1))  1.92 us
    pallas_call x1, Pallas kernels, row_edges(): pl.pallas_call(rows_kernel, out_shape=(edge, edge), in_specs=[pl.BlockSpe...  0.79 us
  transfers between devices with their start and end apart: 2, of which 0 were waited for; matrix products, arithmetic and copies ran while one was open for 0% of the time, Pallas kernels for 0%

profile of v11, /device:TPU:248, one launch (start us, length us, event | category | flops | bytes accessed | tf_op | source)
XLA Modules:
  0.0 20.8 jit_solution(2225443698241691741)
XLA Ops:
  0.0 0.8 %row_edges.1 = (bf16[2,12,512]{2,1,0:T(8,128)(2,1)S(1)}, bf16[2,12,512]{2,1,0:T(8,128)(2,1)S(1)}) custom-call(bf16[12,12,512]{2,1,0:T(8,128)(2,1)} %x_ref.3), custom_call_target="tpu_custom_call" | custom-call | bytes 500000 | tf_op jit(solution)/shard_map/row_edges/pallas_call | solution.py:59
  0.8 1.9 %collective-permute-start = (bf16[2,12,512]{2,1,0:T(8,128)(2,1)S(1)}, bf16[2,12,512]{2,1,0:T(8,128)(2,1)S(1)}, u32[]{:S(2)}, u32[]{:S(2)}) collective-permute-start(bf16[2,12,512]{2,1,0:T(8,128)(2,1)S(1)} %get-tuple-element.9), channel_id=1, source_target_pairs={{16,32},{32,16},{48,64},{64,48},{80,96},{96,80},{112,128},{128,112... | collective-permute-start | bytes 73736 | tf_op jit(solution)/shard_map/ppermute | solution.py:303
  2.7 0.0 copy-start.2
  2.7 0.0 copy-start
  2.8 0.0 copy-start.1
  2.8 0.0 copy-start.3
  2.8 0.0 copy-start.4
  2.8 0.0 copy-start.5
  2.8 0.0 copy-start.6
  2.8 0.0 copy-start.7
  2.8 0.0 copy-start.8
  2.8 0.0 copy-start.9
  2.9 4.9 %all-gather = bf16[4,12,512]{2,1,0:T(8,128)(2,1)S(1)} all-gather(bf16[2,12,512]{2,1,0:T(8,128)(2,1)S(1)} %keep.1), channel_id=2, replica_groups={{0,16},{1,17},{2,18},{3,19},{4,20},{5,21},{6,22},{7,23},{8,24},{9,25},{..., dimensions={0}, use_global_device_ids=true | all-gather | bytes 73728 | tf_op jit(solution)/shard_map/all_gather | solution.py:305
  7.7 0.0 collective-permute-done.row_z
  7.7 0.0 copy-done.2
  7.7 0.1 column_edges.1
  7.8 4.8 %collective-permute-start.1 = (bf16[16,2,512]{2,1,0:T(2,128)(2,1)S(1)}, bf16[16,2,512]{2,1,0:T(2,128)(2,1)S(1)}, u32[]{:S(2)}, u32[]{:S(2)}) collective-permute-start(bf16[16,2,512]{2,1,0:T(2,128)(2,1)S(1)} %get-tuple-element.11), channel_id=1, source_target_pairs={{1,2},{2,1},{3,4},{4,3},{5,6},{6,5},{7,8},{8,7},{9,10},{10,9},{11,... | collective-permute-start | bytes 98312 | tf_op jit(solution)/shard_map/ppermute | solution.py:307
  12.6 4.6 %all-gather.1 = bf16[32,2,512]{2,1,0:T(2,128)(2,1)S(1)} all-gather(bf16[16,2,512]{2,1,0:T(2,128)(2,1)S(1)} %get-tuple-element.12), channel_id=3, replica_groups={{0,1},{2,3},{4,5},{6,7},{8,9},{10,11},{12,13},{14,15},{16,17},{18,19},{..., dimensions={0}, use_global_device_ids=true | all-gather | bytes 98304 | tf_op jit(solution)/shard_map/all_gather | solution.py:308
  17.2 0.0 collective-permute-done.1.col_odd
  17.2 0.0 copy-done
  17.2 0.0 copy-done.1
  17.2 0.0 copy-done.3
  17.3 0.0 copy-done.4
  17.3 0.0 copy-done.5
  17.3 0.0 copy-done.6
  17.3 0.0 copy-done.7
  17.3 0.0 copy-done.8
  17.3 0.0 copy-done.9
  17.3 3.4 %decode_block.1 = bf16[24,24,512]{2,1,0:T(8,128)(2,1)} custom-call(bf16[12,12,512]{2,1,0:T(8,128)(2,1)S(1)} %copy-done.2, bf16[2,12,512]{2,1,0:T(8,128)(2,1)S(1)} %collective-permute-done.row_z, bf16[2,2,12,512]{3,2,1,0:T(8,128)(2,1)S(1)} %bitcast.11, bf16[16,2,512]{2,1,0:T(2,128)(2,1)S(1)} %collective-permute-done.1.col_odd, ...), custom_call_target="tpu_custom_call" | custom-call | flops 2300000000 | bytes 14000000 | tf_op jit(solution)/shard_map/decode_block/pallas_call | solution.py:264
  (1 shorter events, 0.0 us)
Async XLA Ops:
  0.8 6.9 %collective-permute-start = (bf16[2,12,512]{2,1,0:T(8,128)(2,1)S(1)}, bf16[2,12,512]{2,1,0:T(8,128)(2,1)S(1)}, u32[]{:S(2)}, u32[]{:S(2)}) collective-permute-start(bf16[2,12,512]{2,1,0:T(8,128)(2,1)S(1)} %get-tuple-element.9), channel_id=1, source_target_pairs={{16,32},{32,16},{48,64},{64,48},{80,96},{96,80},{112,128},{128,112... | collective-permute-start | bytes 73736 | tf_op jit(solution)/shard_map/ppermute | solution.py:303
  2.7 5.0 %copy-start.2 = (bf16[12,12,512]{2,1,0:T(8,128)(2,1)S(1)}, bf16[12,12,512]{2,1,0:T(8,128)(2,1)}, u32[]{:S(2)}) copy-start(bf16[12,12,512]{2,1,0:T(8,128)(2,1)} %x_ref.3) | copy-start | bytes 442372
  2.7 14.5 %copy-start = (bf16[3,3,512,512]{3,2,1,0:T(8,128)(2,1)S(1)}, bf16[3,3,512,512]{3,2,1,0:T(8,128)(2,1)}, u32[]{:S(2)}) copy-start(bf16[3,3,512,512]{3,2,1,0:T(8,128)(2,1)} %refs_4_.1) | copy-start | bytes 14155780
  2.8 14.5 %copy-start.1 = (bf16[3,3,512,512]{3,2,1,0:T(8,128)(2,1)S(1)}, bf16[3,3,512,512]{3,2,1,0:T(8,128)(2,1)}, u32[]{:S(2)}) copy-start(bf16[3,3,512,512]{3,2,1,0:T(8,128)(2,1)} %w2_ref.1) | copy-start | bytes 14155780
  2.8 14.5 %copy-start.3 = (f32[512]{0:T(512)S(1)}, f32[512]{0:T(512)}, u32[]{:S(2)}) copy-start(f32[512]{0:T(512)} %param.13) | copy-start | bytes 6148
  2.8 14.5 %copy-start.4 = (f32[512]{0:T(512)S(1)}, f32[512]{0:T(512)}, u32[]{:S(2)}) copy-start(f32[512]{0:T(512)} %param.14) | copy-start | bytes 6148
  2.8 14.5 %copy-start.5 = (f32[512]{0:T(512)S(1)}, f32[512]{0:T(512)}, u32[]{:S(2)}) copy-start(f32[512]{0:T(512)} %param.16) | copy-start | bytes 6148
  2.8 14.5 %copy-start.6 = (f32[512]{0:T(512)S(1)}, f32[512]{0:T(512)}, u32[]{:S(2)}) copy-start(f32[512]{0:T(512)} %param.18) | copy-start | bytes 6148
  2.8 14.5 %copy-start.7 = (s32[4,4]{1,0:T(4,128)S(1)}, s32[4,4]{1,0:T(4,128)}, u32[]{:S(2)}) copy-start(s32[4,4]{1,0:T(4,128)} %dest_ref.1) | copy-start | bytes 196
  2.8 14.5 %copy-start.8 = (f32[32]{0:T(128)S(1)}, f32[32]{0:T(128)}, u32[]{:S(2)}) copy-start(f32[32]{0:T(128)} %param.11) | copy-start | bytes 388
  2.8 14.5 %copy-start.9 = (f32[32]{0:T(128)S(1)}, f32[32]{0:T(128)}, u32[]{:S(2)}) copy-start(f32[32]{0:T(128)} %param.12) | copy-start | bytes 388
  7.8 9.4 %collective-permute-start.1 = (bf16[16,2,512]{2,1,0:T(2,128)(2,1)S(1)}, bf16[16,2,512]{2,1,0:T(2,128)(2,1)S(1)}, u32[]{:S(2)}, u32[]{:S(2)}) collective-permute-start(bf16[16,2,512]{2,1,0:T(2,128)(2,1)S(1)} %get-tuple-element.11), channel_id=1, source_target_pairs={{1,2},{2,1},{3,4},{4,3},{5,6},{6,5},{7,8},{8,7},{9,10},{10,9},{11,... | collective-permute-start | bytes 98312 | tf_op jit(solution)/shard_map/ppermute | solution.py:307
